TPU v7x, 32 devices: a whole 2x2x4 slice. The times are simulated.
32 devices in a mesh: dp: 16 (over z, x, core), expert: 2 (over y).
Axes of the slice: x: 2, y: 2, z: 4, core: 2. Of those that a mesh axis runs over, the one named last changes fastest.
Arguments:
- tokens: bfloat16 [4096, 2048], P(('dp', 'expert')), may hold values from -6 to 6
- expert_ids: int32 [4096, 8], P(('dp', 'expert')), may hold values from 0 to 16, as said below
- gate_weights: float32 [4096, 8], P(('dp', 'expert')), may hold values from 0.2 to 1
- hot_weights: bfloat16 [1, 3, 768, 2048], P(None, None, 'expert'), may hold values from -0.125 to 0.125
- cold_weights: bfloat16 [16, 3, 768, 2048], P('dp'), may hold values from -0.125 to 0.125
Outputs:
- combined: bfloat16 [4096, 2048], P(('dp', 'expert'))
Inputs may be any that keep to these rules, and one draw needn't show every extreme that they name: `expert_ids`: each row names 8 different experts; among the rows of one device expert 0 is named by exactly 80 rows and no other expert by more than 80 rows.
All inputs are finite; a program needn't handle non-finite values.
Results may differ from a plain program's by a relative error of at most 0.0057.
Values may be sent and summed in bfloat16 or wider, within the bound.
No kernel may reach another device: no remote copies, remote signals or barrier semaphores. Data moves between devices by JAX's collectives and lax.ppermute only.
A program may use at most 128 MiB of HBM per device.

v0:
```python
import jax
import jax.numpy as jnp
from jax import lax
from jax.sharding import PartitionSpec as P

TOP = 8
HOT = 1


def shifted(shard, axis, by):
    size = lax.axis_size(axis)
    return lax.ppermute(shard, axis, [(i, (i + by) % size) for i in range(size)])


def expert_partial(inputs, weights):
    gate_part = lax.dot_general(
        inputs, weights[0], (((1,), (1,)), ((), ())), preferred_element_type=jnp.float32
    )
    up_part = lax.dot_general(
        inputs, weights[1], (((1,), (1,)), ((), ())), preferred_element_type=jnp.float32
    )
    hidden = (jax.nn.silu(gate_part) * up_part).astype(jnp.bfloat16)
    return jnp.dot(hidden, weights[2], preferred_element_type=jnp.float32)


def on_device(tokens, expert_ids, gate_weights, hot_weights, cold_weights):
    tok_rows, features = tokens.shape
    dp_count = lax.axis_size("dp")
    cycle_count = lax.axis_size("expert")
    cold_count = cold_weights.shape[0]
    experts = HOT + cold_count * dp_count
    capacity = 8 * (tok_rows * TOP * 5 // (experts * 32) + 1)
    flat_ids = expert_ids.reshape(-1)
    onehot = (flat_ids[:, None] == jnp.arange(experts, dtype=jnp.int32)[None, :]).astype(jnp.int32)
    before = jnp.cumsum(onehot, axis=0) - onehot
    ranks = jnp.sum(before * onehot, axis=1)
    slots = flat_ids * capacity + ranks
    owner_token = jnp.arange(flat_ids.shape[0], dtype=jnp.int32) // TOP
    sources = jnp.full((experts * capacity,), tok_rows, jnp.int32).at[slots].set(owner_token)
    padded = jnp.concatenate([tokens, jnp.zeros((1, features), tokens.dtype)], axis=0)
    dispatched = padded[sources]
    hot_inputs = dispatched[: HOT * capacity].reshape(HOT, capacity, features)
    cold_inputs = dispatched[HOT * capacity :].reshape(dp_count, cold_count, capacity, features)
    segment = lax.all_to_all(cold_inputs, "dp", split_axis=0, concat_axis=0, tiled=True)[:, 0]
    served = expert_partial(segment.reshape(-1, features), cold_weights[0])
    results_list = [served.astype(jnp.bfloat16).reshape(segment.shape)]
    answer = jnp.stack(results_list, axis=1)
    cold_results = lax.all_to_all(answer, "dp", split_axis=0, concat_axis=0, tiled=True)

    def apply_block(weight_block):
        return jnp.stack([expert_partial(hot_inputs[0], weight_block[0])])

    weight_block = hot_weights
    summed = apply_block(weight_block)
    for rounds in range(cycle_count - 1):
        weight_block = shifted(weight_block, "expert", 1)
        summed = summed + apply_block(weight_block)
    hot_results = summed.astype(jnp.bfloat16)
    results = jnp.concatenate(
        [hot_results.reshape(-1, features), cold_results.reshape(-1, features)], axis=0
    )
    picked = results[slots.reshape(tok_rows, TOP)]
    combined = jnp.sum(gate_weights[:, :, None] * picked.astype(jnp.float32), axis=1)
    return combined.astype(jnp.bfloat16)


def solution(mesh):
    placed = (
        P(("dp", "expert"), None),
        P(("dp", "expert"), None),
        P(("dp", "expert"), None),
        P(None, None, "expert", None),
        P("dp", None, None, None),
    )
    return jax.shard_map(
        on_device, mesh=mesh, in_specs=placed, out_specs=P(("dp", "expert"), None), check_vma=False
    )
```

profile of v0, /device:TPU:0, one launch (start us, length us, event | category | flops | bytes accessed | tf_op | source)
XLA Modules:
  0.0 301.1 jit_solution(4621756641660758721)
XLA Ops:
  0.0 0.8 copy.14
  0.8 0.1 eq.29
  0.9 0.1 eq.25
  1.0 4.8 %reduce-window.6 = s32[17,8,128]{2,1,0:T(8,128)S(1)} reduce-window(s32[17,8,128]{2,1,0:T(8,128)S(1)} %fusion.41, s32[]{:T(128)} %constant.36.clone.1), window={size=1x1x128 pad=0_0x0_0x127_0}, to_apply=%region_0.0 | reduce-window | flops 2210816 | bytes 139268 | tf_op jit(solution)/shard_map/reduce-window
  5.8 0.1 slice.65
  5.9 0.1 copy.17
  6.0 0.1 copy.18
  6.1 0.1 broadcast_add_fusion
  6.3 0.1 reduce_sum.24
  6.4 0.1 mul.51
  6.5 4.3 %scatter_custom_fusion = s32[1360]{0:T(1024)S(1)} fusion(s32[1024]{0:T(1024)S(1)} %bitcast.71, s32[1024]{0:T(1024)S(1)} %add_select_fusion, s32[]{:T(128)} %constant.34.clone.1), kind=kCustom, calls=%fused_computation.64 | custom fusion | bytes 5444 | tf_op jit(solution)/shard_map/scatter | solution.py:39
  10.9 1.1 concatenate.6
  12.0 6.8 %gather_fusion = bf16[1360,2048]{1,0:T(8,128)(2,1)} fusion(bf16[129,2048]{1,0:T(8,128)(2,1)S(1)} %concatenate.6, s32[2048]{0:T(1024)S(1)} %pad_clamp_fusion), kind=kCustom, calls=%fused_computation | custom fusion | bytes 11146560 | tf_op jit(solution)/shard_map/gather | solution.py:41
  18.8 0.0 slice-start
  18.8 2.5 slice-done
  21.3 0.0 slice-start.1
  21.3 122.1 %all_to_all.10 = bf16[16,1,80,2048]{3,2,1,0:T(8,128)(2,1)S(1)} all-to-all(bf16[16,1,80,2048]{3,2,1,0:T(8,128)(2,1)S(1)} %bitcast.63), channel_id=1, replica_groups=mesh['dp'=16,'expert'=2] {'dp'}, dimensions={0} | all-to-all | bytes 10485760 | tf_op jit(solution)/shard_map/all_to_all | solution.py:44
  143.4 0.0 slice-start.2
  143.4 0.0 slice-start.3
  143.4 6.3 %fusion.4 = f32[1280,768]{1,0:T(8,128)S(1)} fusion(bf16[1280,2048]{1,0:T(8,128)(2,1)S(1)} %bitcast.65, bf16[1,3,768,2048]{3,2,1,0:T(8,128)(2,1)} %param.9), kind=kOutput, calls=%fused_computation.11 | convolution fusion | flops 4026531840 | bytes 12320768 | tf_op jit(solution)/shard_map/dot_general | solution.py:16
  149.7 0.0 slice-done.1
  149.8 0.0 slice-done.2
  149.8 0.0 slice-done.3
  149.8 4.7 %fusion.1 = bf16[1280,768]{1,0:T(8,128)(2,1)S(1)} fusion(bf16[1280,2048]{1,0:T(8,128)(2,1)S(1)} %bitcast.66, f32[1280,768]{1,0:T(8,128)S(1)} %fusion.4, bf16[1,3,768,2048]{3,2,1,0:T(8,128)(2,1)S(1)} %bitcast.73), kind=kOutput, calls=%fused_computation.8 | convolution fusion | flops 4032430080 | bytes 14286848 | tf_op jit(solution)/shard_map/dot_general | solution.py:19
  154.5 6.0 %convolution_convert_fusion = bf16[1280,2048]{1,0:T(8,128)(2,1)} fusion(bf16[1280,768]{1,0:T(8,128)(2,1)S(1)} %fusion.1, bf16[1,3,768,2048]{3,2,1,0:T(8,128)(2,1)S(1)} %bitcast.73), kind=kOutput, calls=%fused_computation.5 | convolution fusion | flops 4029153280 | bytes 10354688 | tf_op jit(solution)/shard_map/dot_general | solution.py:23
  160.5 0.0 copy-start
  160.5 5.6 %all-to-all-start.1 = ((bf16[16,1,80,2048]{3,2,1,0:T(8,128)(2,1)}), bf16[16,1,80,2048]{3,2,1,0:T(8,128)(2,1)}, u32[]{:S(2)}, u32[]{:S(2)}) async-start(bf16[16,1,80,2048]{3,2,1,0:T(8,128)(2,1)} %bitcast.64), calls=%async_computation.1 | async-start | bytes 10485760 | tf_op jit(solution)/shard_map/all_to_all | solution.py:48
  166.1 1.6 collective-permute-start
  167.7 0.1 reshape.90
  167.7 0.0 copy-done
  167.8 0.1 copy.13
  167.9 2.1 fusion.16
  170.0 3.1 %fusion.12 = f32[80,2048]{1,0:T(8,128)S(1)} fusion(bf16[1,3,384,2048]{3,2,1,0:T(8,128)(2,1)} %param.8, bf16[1360,2048]{1,0:T(8,128)(2,1)} %gather_fusion, f32[80,384]{1,0:T(8,128)S(1)} %fusion.16), kind=kOutput, calls=%fused_computation.23 | convolution fusion | flops 251842560 | bytes 4251648 | tf_op jit(solution)/shard_map/dot_general | solution.py:23
  173.1 97.4 %collective-permute-done = bf16[1,3,384,2048]{3,2,1,0:T(8,128)(2,1)} collective-permute-done((bf16[1,3,384,2048]{3,2,1,0:T(8,128)(2,1)}, bf16[1,3,384,2048]{3,2,1,0:T(8,128)(2,1)}, u32[]{:S(2)}, u32[]{:S(2)}) %collective-permute-start) | collective-permute-done | bytes 4718624 | tf_op jit(solution)/shard_map/ppermute | solution.py:12
  270.5 2.1 fusion.10
  272.6 3.2 %fusion.9 = bf16[80,2048]{1,0:T(8,128)(2,1)S(1)} fusion(f32[80,2048]{1,0:T(8,128)S(1)} %fusion.12, bf16[1,3,384,2048]{3,2,1,0:T(8,128)(2,1)} %collective-permute-done, f32[80,384]{1,0:T(8,128)S(1)} %fusion.10, bf16[1360,2048]{1,0:T(8,128)(2,1)} %gather_fusion), kind=kOutput, calls=%fused_computation.17 | convolution fusion | flops 252170240 | bytes 4579328 | tf_op jit(solution)/shard_map/dot_general | solution.py:23
  275.8 0.0 all-to-all-done.1
  275.8 5.8 %pad_maximum_fusion = bf16[1360,2048]{1,0:T(8,128)(2,1)} fusion(bf16[1280,2048]{1,0:T(8,128)(2,1)} %bitcast.18, bf16[80,2048]{1,0:T(8,128)(2,1)S(1)} %fusion.9), kind=kLoop, calls=%fused_computation.6 | loop fusion | flops 11141120 | bytes 11141120 | tf_op jit(solution)/shard_map/concatenate | solution.py:59
  281.7 12.1 %gather_fusion.1 = bf16[1024,2048]{1,0:T(8,128)(2,1)} fusion(bf16[1360,2048]{1,0:T(8,128)(2,1)} %pad_maximum_fusion, s32[1024]{0:T(1024)S(1)} %broadcast_clamp_fusion), kind=kCustom, calls=%fused_computation.1 | custom fusion | bytes 8392704 | tf_op jit(solution)/shard_map/gather | solution.py:62
  293.8 7.3 %fusion = bf16[128,2048]{1,0:T(8,128)(2,1)} fusion(bf16[1024,2048]{1,0:T(8,128)(2,1)} %gather_fusion.1, f32[128,8]{1,0:T(8,128)S(1)} %copy.13), kind=kLoop, calls=%fused_computation.4 | loop fusion | flops 6029312 | bytes 4722688 | tf_op jit(solution)/shard_map/reduce_sum | solution.py:63
  (13 shorter events, 0.1 us)
Async XLA Ops:
  18.8 2.5 slice-start
  21.3 128.5 %slice-start.1 = ((s8[9437184]{0:T(1024)(128)(4,1)}), s8[4194304]{0:T(1024)(128)(4,1)S(1)}, s32[]{:S(2)}) async-start(s8[9437184]{0:T(1024)(128)(4,1)} %bitcast.72), calls=%async_computation.3 | async-start | bytes 8388608
  143.4 6.3 %slice-start.2 = ((s8[9437184]{0:T(1024)(128)(4,1)}), s8[4194304]{0:T(1024)(128)(4,1)S(1)}, s32[]{:S(2)}) async-start(s8[9437184]{0:T(1024)(128)(4,1)} %bitcast.72), calls=%async_computation.4 | async-start | bytes 8388608
  143.4 6.3 %slice-start.3 = ((s8[9437184]{0:T(1024)(128)(4,1)}), s8[1048576]{0:T(1024)(128)(4,1)S(1)}, s32[]{:S(2)}) async-start(s8[9437184]{0:T(1024)(128)(4,1)} %bitcast.72), calls=%async_computation.5 | async-start | bytes 2097152
  160.5 7.3 %copy-start = (f32[128,8]{0,1:T(8,128)S(1)}, f32[128,8]{0,1:T(8,128)}, u32[]{:S(2)}) copy-start(f32[128,8]{0,1:T(8,128)} %param.7) | copy-start | bytes 12292
  160.5 115.3 %all-to-all-start.1 = ((bf16[16,1,80,2048]{3,2,1,0:T(8,128)(2,1)}), bf16[16,1,80,2048]{3,2,1,0:T(8,128)(2,1)}, u32[]{:S(2)}, u32[]{:S(2)}) async-start(bf16[16,1,80,2048]{3,2,1,0:T(8,128)(2,1)} %bitcast.64), calls=%async_computation.1 | async-start | bytes 10485760 | tf_op jit(solution)/shard_map/all_to_all | solution.py:48
  166.1 104.4 %collective-permute-start = (bf16[1,3,384,2048]{3,2,1,0:T(8,128)(2,1)}, bf16[1,3,384,2048]{3,2,1,0:T(8,128)(2,1)}, u32[]{:S(2)}, u32[]{:S(2)}) collective-permute-start(bf16[1,3,384,2048]{3,2,1,0:T(8,128)(2,1)} %param.8), channel_id=1, source_target_pairs={{0,1},{1,0},{2,3},{3,2},{4,5},{5,4},{6,7},{7,6},{8,9},{9,8},{10,11... | collective-permute-start | bytes 14155784 | tf_op jit(solution)/shard_map/ppermute | solution.py:12
where the time goes:
time: 306 us; the launch traced here: 301 us
  blocking collectives  122 us (40%)
  waiting for transfers between devices  97.4 us (32%)
  local copies, waits for them, and re-layouts  28.5 us (9%)
  matrix products  27.6 us (9%)
  other arithmetic  18.2 us (6%)
  starting transfers between devices  7.15 us (2%)
    all_to_all x1, blocking collectives, on_device(): lax.all_to_all(cold_inputs, 'dp', split_axis=0, concat_axis=0, tiled=True)  122 us
    ppermute x1, waiting for transfers between devices, shifted(): lax.ppermute(shard, axis, [(i, (i + by) % size) for i in range(size)])  97.4 us
    dot_general x3, matrix products, expert_partial(): return jnp.dot(hidden, weights[2], preferred_element_type=jnp.float32)  12.3 us
    gather x1, local copies, waits for them, and re-layouts, on_device(): picked = results[slots.reshape(tok_rows, TOP)]  12.1 us
    dot_general x2, matrix products, expert_partial(): lax.dot_general(inputs, weights[0], (((1,), (1,)), ((), ())), preferred_e...  8.43 us
    reduce_sum x1, other arithmetic, on_device(): jnp.sum(gate_weights[:, :, None] * picked.astype(jnp.float32), axis=1)  7.33 us
    dot_general x2, matrix products, expert_partial(): lax.dot_general(inputs, weights[1], (((1,), (1,)), ((), ())), preferred_e...  6.84 us
    gather x1, local copies, waits for them, and re-layouts, on_device(): dispatched = padded[sources]  6.81 us
  transfers between devices with their start and end apart: 2, of which 1 were waited for; matrix products, arithmetic and copies ran while one was open for 4% of the time, Pallas kernels for 0%

commit v1 on v0

v1 whole, which is shorter than its diff:
```python
import functools

import jax
import jax.numpy as jnp
from jax import lax
from jax.experimental import pallas as pl
from jax.experimental.pallas import tpu as pltpu
from jax.sharding import PartitionSpec as P

LANES = 128
NT = (((1,), (1,)), ((), ()))


def shifted(block, axis, by):
    size = lax.axis_size(axis)
    return lax.ppermute(block, axis, [(i, (i + by) % size) for i in range(size)])


def ring_pairs(count):
    chips = count // 2
    half = chips // 2

    def first_core(place):
        place %= chips
        return 4 * place if place < half else 4 * (chips - 1 - place) + 2

    onward = [
        (first_core(place) + core, first_core(place + 1) + core)
        for place in range(chips)
        for core in range(2)
    ]
    return onward, [(target, source) for source, target in onward]


def expert_kernel(parts, kept_rows, features, scaled, owner_ref, *refs):
    blocks, (gate_ref, up_ref, down_ref, keep_ref, send_ref, inputs, scale, total) = (
        refs[:parts],
        refs[parts:],
    )
    step = pl.program_id(0)

    @pl.when(step == 0)
    def _():
        row = 0
        for block in blocks:
            rows = block.shape[0]
            inputs[row : row + rows, :] = block[:, :features]
            if scaled:
                extra = block[:, features:].astype(jnp.float32)
                lane = lax.broadcasted_iota(jnp.int32, extra.shape, 1)
                owner, count = owner_ref[0], owner_ref[1]
                mine = (lane == owner) | (lane == owner + count) | (lane == owner + 2 * count)
                scale[row : row + rows, :] = jnp.sum(
                    jnp.where(mine, extra, 0.0), axis=1, keepdims=True
                )
            row += rows

    values = inputs[...]
    gate = lax.dot_general(values, gate_ref[0, 0], NT, preferred_element_type=jnp.float32)
    up = lax.dot_general(values, up_ref[0, 0], NT, preferred_element_type=jnp.float32)
    hidden = (gate / (1.0 + jnp.exp(-gate)) * up).astype(jnp.bfloat16)
    partial = jnp.dot(hidden, down_ref[0, 0], preferred_element_type=jnp.float32)

    @pl.when(step == 0)
    def _():
        total[...] = partial

    @pl.when(step > 0)
    def _():
        total[...] += partial

    @pl.when(step == pl.num_programs(0) - 1)
    def _():
        result = total[...]
        if scaled:
            result = result * scale[...]
        keep_ref[...] = result[:kept_rows]
        send_ref[...] = result[kept_rows:].astype(jnp.bfloat16)


def expert_apply(blocks, weights, kept_rows, features, owner, tile):
    scaled = owner is not None
    if owner is None:
        owner = jnp.zeros((2,), jnp.int32)
    rows = sum(block.shape[0] for block in blocks)
    hidden = weights.shape[2]
    tile = min(tile, hidden)
    whole = [pl.BlockSpec(block.shape, lambda i, owner: (0, 0)) for block in blocks]

    def matrix(which):
        return pl.BlockSpec((1, 1, tile, features), lambda i, owner: (0, which, i, 0))

    return pl.pallas_call(
        functools.partial(expert_kernel, len(blocks), kept_rows, features, scaled),
        grid_spec=pltpu.PrefetchScalarGridSpec(
            num_scalar_prefetch=1,
            grid=(hidden // tile,),
            in_specs=whole + [matrix(0), matrix(1), matrix(2)],
            out_specs=[
                pl.BlockSpec((kept_rows, features), lambda i, owner: (0, 0)),
                pl.BlockSpec((rows - kept_rows, features), lambda i, owner: (0, 0)),
            ],
            scratch_shapes=[
                pltpu.VMEM((rows, features), jnp.bfloat16),
                pltpu.VMEM((rows, 1), jnp.float32),
                pltpu.VMEM((rows, features), jnp.float32),
            ],
        ),
        out_shape=[
            jax.ShapeDtypeStruct((kept_rows, features), jnp.float32),
            jax.ShapeDtypeStruct((rows - kept_rows, features), jnp.bfloat16),
        ],
        compiler_params=pltpu.CompilerParams(
            dimension_semantics=("arbitrary",), vmem_limit_bytes=40 * 1024 * 1024
        ),
        cost_estimate=pl.CostEstimate(
            flops=6 * rows * hidden * features,
            bytes_accessed=2 * 3 * hidden * features + 8 * rows * features,
            transcendentals=rows * hidden,
        ),
    )(owner, *blocks, weights, weights, weights)


def on_device(tokens, expert_ids, gate_weights, hot_weights, cold_weights):
    rows, features = tokens.shape
    count = lax.axis_size("dp")
    groups = lax.axis_size("expert")
    experts = 1 + count
    onward, backward = ring_pairs(count)
    across = [(i, i ^ 1) for i in range(count)]
    reach = count // 4
    owner = jnp.stack([lax.axis_index("dp"), count]).astype(jnp.int32)

    labels = jnp.arange(experts, dtype=jnp.int32)[None, :]
    table = jnp.zeros((rows, experts), jnp.float32)
    for k in range(expert_ids.shape[1]):
        table = table + jnp.where(
            expert_ids[:, k : k + 1] == labels, gate_weights[:, k : k + 1], 0.0
        )
    cold_table = table[:, 1:]
    high = lax.reduce_precision(cold_table, 8, 7)
    rest = cold_table - high
    middle = lax.reduce_precision(rest, 8, 7)
    low = rest - middle
    extra = -(3 * count) % LANES
    payload = jnp.concatenate(
        [
            tokens,
            jnp.pad(
                jnp.concatenate([high, middle, low], axis=1).astype(jnp.bfloat16),
                ((0, 0), (0, extra)),
            ),
        ],
        axis=1,
    )

    def go(block, pairs):
        return lax.ppermute(block, "dp", pairs)

    ahead, behind = {}, {}
    fore = back = payload
    for k in range(1, reach):
        fore, back = go(fore, onward), go(back, backward)
        behind[k], ahead[k] = fore, back
    fore, back = go(fore[: rows // 2], onward), go(back[rows // 2 :], backward)

    hot_blocks = [tokens] + [shifted(tokens, "expert", by) for by in range(1, groups)]
    hot_keep, hot_send = expert_apply(hot_blocks, hot_weights, rows, features, None, 384)

    def serve(blocks):
        others = [go(block, across) for block in blocks]
        kept = sum(block.shape[0] for block in blocks)
        keep, send = expert_apply(blocks + others, cold_weights, kept, features, owner, 256)
        return keep, go(send, across)

    keep, got = serve([payload])
    own = keep + got.astype(jnp.float32)
    sums = {}
    for k in range(1, reach):
        keep, got = serve([ahead[k], behind[k]])
        both = keep + got.astype(jnp.float32)
        sums[k], sums[-k] = both[:rows], both[rows:]
    keep, got = serve([fore, back])
    both = keep + got.astype(jnp.float32)

    half = rows // 2
    fore = go(both[:half].astype(jnp.bfloat16), onward)
    back = go(both[half:].astype(jnp.bfloat16), backward)
    for k in range(reach - 1, 0, -1):
        fore_sum, back_sum = sums[k], sums[-k]
        if k == reach - 1:
            fore = jnp.concatenate([fore_sum[:half] + fore, fore_sum[half:]], axis=0)
            back = jnp.concatenate([back_sum[:half], back_sum[half:] + back], axis=0)
        else:
            fore, back = fore_sum + fore, back_sum + back
        fore, back = go(fore.astype(jnp.bfloat16), onward), go(back.astype(jnp.bfloat16), backward)

    hot = hot_keep
    for by in range(1, groups):
        hot = hot + shifted(hot_send[(by - 1) * rows : by * rows], "expert", -by)
    combined = own + fore.astype(jnp.float32) + back.astype(jnp.float32) + table[:, :1] * hot
    return combined.astype(jnp.bfloat16)


def solution(mesh):
    placed = (
        P(("dp", "expert"), None),
        P(("dp", "expert"), None),
        P(("dp", "expert"), None),
        P(None, None, "expert", None),
        P("dp", None, None, None),
    )
    return jax.shard_map(
        on_device, mesh=mesh, in_specs=placed, out_specs=P(("dp", "expert"), None), check_vma=False
    )
```

time: 306 us -> 159 us (0.52); the launches traced: 301 us -> 159 us
  blocking collectives: 122 us -> 0 us
  Pallas kernels: 0 us -> 45.5 us
  matrix products: 27.6 us -> 0 us
  waiting for transfers between devices: 97.4 us -> 74.7 us
  local copies, waits for them, and re-layouts: 28.5 us -> 8.28 us
  starting transfers between devices: 7.15 us -> 24.3 us
  other arithmetic: 18.2 us -> 5.67 us
    all_to_all x1 -> x0, blocking collectives: 122 us -> none  [on_device(): lax.all_to_all(cold_inputs, 'dp', split_axis=0, concat_axis=0, tiled=True)]
    pallas_call x0 -> x6, Pallas kernels: none -> 45.5 us  [expert_apply(): pl.pallas_call(functools.partial(expert_kernel, len(blocks), kept_rows, f...]
    dot_general x7 -> x0, matrix products: 27.6 us -> none  [the longest x3 12.3 us: expert_partial(): return jnp.dot(hidden, weights[2], preferred_element_type=jnp.float32)]
    ppermute x1 -> x32, starting transfers between devices: 1.59 us -> 24.3 us  [the longest x30 21.4 us: go(): return lax.ppermute(block, 'dp', pairs)]
    ppermute x1 -> x32, waiting for transfers between devices: 97.4 us -> 74.7 us  [the longest x30 74.7 us: go(): return lax.ppermute(block, 'dp', pairs)]
    gather x2 -> x0, local copies, waits for them, and re-layouts: 18.9 us -> none  [the longest x1 12.1 us: on_device(): picked = results[slots.reshape(tok_rows, TOP)]]
    reduce_sum x2 -> x0, other arithmetic: 7.36 us -> none  [the longest x1 7.33 us: on_device(): jnp.sum(gate_weights[:, :, None] * picked.astype(jnp.float32), axis=1)]
    all_to_all x1 -> x0, starting transfers between devices: 5.56 us -> none  [on_device(): lax.all_to_all(answer, 'dp', split_axis=0, concat_axis=0, tiled=True)]
  transfers between devices with their start and end apart: 2 -> 32, of which waited for: 1 -> 12; matrix products, arithmetic and copies ran while one was open for 4% -> 1% of each run, Pallas kernels for 0% -> 29%
where the time goes in v1:
time: 159 us
  waiting for transfers between devices  74.7 us (47%)
  Pallas kernels  45.5 us (29%)
  starting transfers between devices  24.3 us (15%)
  local copies, waits for them, and re-layouts  8.28 us (5%)
  other arithmetic  5.67 us (4%)
    ppermute x30, waiting for transfers between devices, go(): return lax.ppermute(block, 'dp', pairs)  74.7 us
    pallas_call x6, Pallas kernels, expert_apply(): pl.pallas_call(functools.partial(expert_kernel, len(blocks), kept_rows, f...  45.5 us
    ppermute x30, starting transfers between devices, go(): return lax.ppermute(block, 'dp', pairs)  21.4 us
    unnamed x24, local copies, waits for them, and re-layouts  6.06 us
  transfers between devices with their start and end apart: 32, of which 12 were waited for; matrix products, arithmetic and copies ran while one was open for 1% of the time, Pallas kernels for 29%

profile of v1, /device:TPU:0, one launch (start us, length us, event | category | flops | bytes accessed | tf_op | source)
XLA Modules:
  0.0 158.7 jit_solution(11362924942184914443)
XLA Ops:
  0.0 1.0 slice_bitcast_fusion.16
  1.0 1.0 slice_bitcast_fusion.15
  2.0 0.1 copy.6
  2.1 0.0 slice-start
  2.1 1.2 fusion.5.refs_0_
  3.3 3.1 %collective-permute-start.3 = (bf16[128,2176]{1,0:T(8,128)(2,1)S(1)}, bf16[128,2176]{1,0:T(8,128)(2,1)}, u32[]{:S(2)}, u32[]{:S(2)}) collective-permute-start(bf16[128,2176]{1,0:T(8,128)(2,1)S(1)} %fusion.5.refs_0_), channel_id=1, source_target_pairs={{0,8},{2,10},{8,16},{10,18},{16,24},{18,26},{24,28},{26,30},{28,20... | collective-permute-start | bytes 1671176 | tf_op jit(solution)/shard_map/ppermute | solution.py:158
  6.4 12.6 %collective-permute-done.3.refs_1_ = bf16[128,2176]{1,0:T(8,128)(2,1)} collective-permute-done((bf16[128,2176]{1,0:T(8,128)(2,1)S(1)}, bf16[128,2176]{1,0:T(8,128)(2,1)}, u32[]{:S(2)}, u32[]{:S(2)}) %collective-permute-start.3) | collective-permute-done | bytes 557088 | tf_op jit(solution)/shard_map/ppermute | solution.py:158
  19.0 1.8 %collective-permute-start.8 = (bf16[128,2176]{1,0:T(8,128)(2,1)}, bf16[128,2176]{1,0:T(8,128)(2,1)S(1)}, u32[]{:S(2)}, u32[]{:S(2)}) collective-permute-start(bf16[128,2176]{1,0:T(8,128)(2,1)} %collective-permute-done.3.refs_1_), channel_id=1, source_target_pairs={{0,8},{2,10},{8,16},{10,18},{16,24},{18,26},{24,28},{26,30},{28,20... | collective-permute-start | bytes 1671176 | tf_op jit(solution)/shard_map/ppermute | solution.py:158
  20.9 0.2 collective-permute-start.7
  21.1 12.0 %collective-permute-done.8.refs_1_ = bf16[128,2176]{1,0:T(8,128)(2,1)S(1)} collective-permute-done((bf16[128,2176]{1,0:T(8,128)(2,1)}, bf16[128,2176]{1,0:T(8,128)(2,1)S(1)}, u32[]{:S(2)}, u32[]{:S(2)}) %collective-permute-start.8) | collective-permute-done | bytes 557088 | tf_op jit(solution)/shard_map/ppermute | solution.py:158
  33.1 1.5 collective-permute-start.13
  34.6 0.0 collective-permute-done.7.refs_0_
  34.6 0.5 collective-permute-start.12
  35.1 1.4 collective-permute-start.30
  36.6 0.0 collective-permute-start
  36.6 0.5 collective-permute-start.4
  37.1 9.0 %collective-permute-done.13.refs_1_ = bf16[128,2176]{1,0:T(8,128)(2,1)S(1)} collective-permute-done((bf16[128,2176]{1,0:T(8,128)(2,1)S(1)}, bf16[128,2176]{1,0:T(8,128)(2,1)S(1)}, u32[]{:S(2)}, u32[]{:S(2)}) %collective-permute-start.13) | collective-permute-done | bytes 557088 | tf_op jit(solution)/shard_map/ppermute | solution.py:158
  46.1 0.1 pad_add_fusion.owner_ref
  46.2 1.0 collective-permute-done.12.refs_0_
  47.2 1.6 collective-permute-start.17
  48.8 0.5 collective-permute-start.18
  49.3 2.3 %copy-done.1 = bf16[1,3,384,2048]{3,2,1,0:T(8,128)(2,1)S(1)} copy-done((bf16[1,3,384,2048]{3,2,1,0:T(8,128)(2,1)S(1)}, bf16[1,3,384,2048]{3,2,1,0:T(8,128)(2,1)}, u32[]{:S(2)}) %copy-start.1) | copy-done | bytes 4718616
  51.7 4.5 %shard_map.60 = (f32[128,2048]{1,0:T(8,128)S(1)}, bf16[128,2048]{1,0:T(8,128)(2,1)}) custom-call(s32[2]{0:T(128)S(1)} %broadcast_1_owner_ref.2.owner_ref, bf16[128,2048]{1,0:T(8,128)(2,1)S(1)} %copy-done.2, bf16[128,2048]{1,0:T(8,128)(2,1)} %collective-permute-done.30.refs_1_, bf16[1,3,384,2048]{3,2,1,0:T(8,128)(2,1)S(1)} %copy-done.1, ...), custom_call_target="tpu_custom_call" | custom-call | flops 1207959552 | bytes 8912896 | tf_op jit(solution)/shard_map/pallas_call | solution.py:93
  56.2 1.5 collective-permute-start.31
  57.7 6.0 %shard_map.55 = (f32[128,2048]{1,0:T(8,128)S(1)}, bf16[128,2048]{1,0:T(8,128)(2,1)S(1)}) custom-call(s32[2]{0:T(128)S(1)} %pad_add_fusion.owner_ref, bf16[128,2176]{1,0:T(8,128)(2,1)S(1)} %fusion.5.refs_0_, bf16[128,2176]{1,0:T(8,128)(2,1)} %collective-permute-done.refs_1_, bf16[1,3,768,2048]{3,2,1,0:T(8,128)(2,1)S(1)} %bitcast.36, ...), custom_call_target="tpu_custom_call" | custom-call | flops 2415919104 | bytes 13631488 | tf_op jit(solution)/shard_map/pallas_call | solution.py:93
  63.8 0.1 collective-permute-start.14
  63.9 0.5 collective-permute-start.15
  64.4 0.1 collective-permute-start.19
  64.4 0.4 collective-permute-start.20
  64.9 10.5 %shard_map.56 = (f32[256,2048]{1,0:T(8,128)S(1)}, bf16[256,2048]{1,0:T(8,128)(2,1)S(1)}) custom-call(s32[2]{0:T(128)S(1)} %pad_add_fusion.owner_ref, bf16[128,2176]{1,0:T(8,128)(2,1)} %collective-permute-done.2.refs_0_, bf16[128,2176]{1,0:T(8,128)(2,1)} %collective-permute-done.3.refs_1_, bf16[128,2176]{1,0:T(8,128)(2,1)} %collective-permute-done.4.refs_2_, ...), custom_call_target="tpu_custom_call" | custom-call | flops 4831838208 | bytes 17825792 | tf_op jit(solution)/shard_map/pallas_call | solution.py:93
  75.4 0.1 collective-permute-start.10
  75.6 0.4 collective-permute-start.9
  76.0 3.7 %copy-done = bf16[1,3,768,2048]{3,2,1,0:T(8,128)(2,1)S(1)} copy-done((bf16[1,3,768,2048]{3,2,1,0:T(8,128)(2,1)S(1)}, bf16[1,3,768,2048]{3,2,1,0:T(8,128)(2,1)}, u32[]{:S(2)}) %copy-start) | copy-done | bytes 9437208
  79.7 4.8 %shard_map.59 = (f32[128,2048]{1,0:T(8,128)S(1)}, bf16[128,2048]{1,0:T(8,128)(2,1)S(1)}) custom-call(s32[2]{0:T(128)S(1)} %pad_add_fusion.owner_ref, bf16[64,2176]{1,0:T(8,128)(2,1)S(1)} %collective-permute-done.17.refs_0_, bf16[64,2176]{1,0:T(8,128)(2,1)S(1)} %collective-permute-done.18.refs_1_, bf16[64,2176]{1,0:T(8,128)(2,1)S(1)} %collective-permute-done.19.refs_2_, ...), custom_call_target="tpu_custom_call" | custom-call | flops 2415919104 | bytes 13631488 | tf_op jit(solution)/shard_map/pallas_call | solution.py:93
  84.5 0.2 collective-permute-start.1
  84.7 0.4 collective-permute-start.21
  85.1 9.6 %shard_map.58 = (f32[256,2048]{1,0:T(8,128)S(1)}, bf16[256,2048]{1,0:T(8,128)(2,1)S(1)}) custom-call(s32[2]{0:T(128)S(1)} %pad_add_fusion.owner_ref, bf16[128,2176]{1,0:T(8,128)(2,1)S(1)} %collective-permute-done.12.refs_0_, bf16[128,2176]{1,0:T(8,128)(2,1)S(1)} %collective-permute-done.13.refs_1_, bf16[128,2176]{1,0:T(8,128)(2,1)S(1)} %collective-permute-done.14.refs_2_, ...), custom_call_target="tpu_custom_call" | custom-call | flops 4831838208 | bytes 17825792 | tf_op jit(solution)/shard_map/pallas_call | solution.py:93
  94.7 0.2 collective-permute-start.16
  94.8 10.0 %shard_map.57 = (f32[256,2048]{1,0:T(8,128)S(1)}, bf16[256,2048]{1,0:T(8,128)(2,1)S(1)}) custom-call(s32[2]{0:T(128)S(1)} %pad_add_fusion.owner_ref, bf16[128,2176]{1,0:T(8,128)(2,1)} %collective-permute-done.7.refs_0_, bf16[128,2176]{1,0:T(8,128)(2,1)S(1)} %copy-done.8, bf16[128,2176]{1,0:T(8,128)(2,1)S(1)} %collective-permute-done.9.refs_2_, ...), custom_call_target="tpu_custom_call" | custom-call | flops 4831838208 | bytes 17825792 | tf_op jit(solution)/shard_map/pallas_call | solution.py:93
  104.9 0.5 collective-permute-start.11
  105.4 0.1 add_convert_fusion.1
  105.5 1.6 %collective-permute-start.22 = (bf16[64,2048]{1,0:T(8,128)(2,1)S(1)}, bf16[64,2048]{1,0:T(8,128)(2,1)S(1)}, u32[]{:S(2)}, u32[]{:S(2)}) collective-permute-start(bf16[64,2048]{1,0:T(8,128)(2,1)S(1)} %get-tuple-element.39), channel_id=1, source_target_pairs={{0,8},{2,10},{8,16},{10,18},{16,24},{18,26},{24,28},{26,30},{28,20... | collective-permute-start | bytes 786440 | tf_op jit(solution)/shard_map/ppermute | solution.py:158
  107.2 0.4 collective-permute-start.26
  107.6 0.4 fusion.9
  108.1 0.1 fusion.10
  108.1 5.8 %collective-permute-done.22 = bf16[64,2048]{1,0:T(8,128)(2,1)S(1)} collective-permute-done((bf16[64,2048]{1,0:T(8,128)(2,1)S(1)}, bf16[64,2048]{1,0:T(8,128)(2,1)S(1)}, u32[]{:S(2)}, u32[]{:S(2)}) %collective-permute-start.22) | collective-permute-done | bytes 262176 | tf_op jit(solution)/shard_map/ppermute | solution.py:158
  113.9 1.3 collective-permute-done.26
  115.2 0.1 fusion.7
  115.3 0.5 collective-permute-start.27
  115.9 1.6 %collective-permute-start.23 = (bf16[128,2048]{1,0:T(8,128)(2,1)S(1)}, bf16[128,2048]{1,0:T(8,128)(2,1)S(1)}, u32[]{:S(2)}, u32[]{:S(2)}) collective-permute-start(bf16[128,2048]{1,0:T(8,128)(2,1)S(1)} %pad_maximum_fusion), channel_id=1, source_target_pairs={{0,8},{2,10},{8,16},{10,18},{16,24},{18,26},{24,28},{26,30},{28,20... | collective-permute-start | bytes 1572872 | tf_op jit(solution)/shard_map/ppermute | solution.py:158
  117.5 0.4 convert_add_fusion.1
  117.9 10.5 %collective-permute-done.27 = bf16[128,2048]{1,0:T(8,128)(2,1)S(1)} collective-permute-done((bf16[128,2048]{1,0:T(8,128)(2,1)S(1)}, bf16[128,2048]{1,0:T(8,128)(2,1)S(1)}, u32[]{:S(2)}, u32[]{:S(2)}) %collective-permute-start.27) | collective-permute-done | bytes 524320 | tf_op jit(solution)/shard_map/ppermute | solution.py:158
  128.4 0.4 collective-permute-done.23
  128.8 0.3 fusion.3
  129.1 1.5 collective-permute-start.24
  130.6 0.5 collective-permute-start.28
  131.2 0.4 convert_add_fusion.2
  131.6 10.3 %collective-permute-done.24 = bf16[128,2048]{1,0:T(8,128)(2,1)S(1)} collective-permute-done((bf16[128,2048]{1,0:T(8,128)(2,1)S(1)}, bf16[128,2048]{1,0:T(8,128)(2,1)S(1)}, u32[]{:S(2)}, u32[]{:S(2)}) %collective-permute-start.24) | collective-permute-done | bytes 524320 | tf_op jit(solution)/shard_map/ppermute | solution.py:158
  141.9 0.3 collective-permute-done.28
  142.2 0.3 fusion.4
  142.5 2.5 %collective-permute-start.25 = (bf16[128,2048]{1,0:T(8,128)(2,1)S(1)}, bf16[128,2048]{1,0:T(8,128)(2,1)S(1)}, u32[]{:S(2)}, u32[]{:S(2)}) collective-permute-start(bf16[128,2048]{1,0:T(8,128)(2,1)S(1)} %get-tuple-element.31), channel_id=1, source_target_pairs={{0,8},{2,10},{8,16},{10,18},{16,24},{18,26},{24,28},{26,30},{28,20... | collective-permute-start | bytes 1572872 | tf_op jit(solution)/shard_map/ppermute | solution.py:158
  145.0 9.2 %collective-permute-done.25 = bf16[128,2048]{1,0:T(8,128)(2,1)S(1)} collective-permute-done((bf16[128,2048]{1,0:T(8,128)(2,1)S(1)}, bf16[128,2048]{1,0:T(8,128)(2,1)S(1)}, u32[]{:S(2)}, u32[]{:S(2)}) %collective-permute-start.25) | collective-permute-done | bytes 524320 | tf_op jit(solution)/shard_map/ppermute | solution.py:158
  154.2 2.1 %collective-permute-done.29 = bf16[128,2048]{1,0:T(8,128)(2,1)S(1)} collective-permute-done((bf16[128,2048]{1,0:T(8,128)(2,1)S(1)}, bf16[128,2048]{1,0:T(8,128)(2,1)S(1)}, u32[]{:S(2)}, u32[]{:S(2)}) %collective-permute-start.29) | collective-permute-done | bytes 524320 | tf_op jit(solution)/shard_map/ppermute | solution.py:158
  156.4 2.4 %add_convert_fusion = bf16[128,2048]{1,0:T(8,128)(2,1)} fusion(f32[128,2048]{1,0:T(8,128)S(1)} %copy-done.4, bf16[128,2048]{1,0:T(8,128)(2,1)} %collective-permute-done.31, bf16[128,2048]{1,0:T(8,128)(2,1)S(1)} %collective-permute-done.29, bf16[128,2048]{1,0:T(8,128)(2,1)S(1)} %collective-permute-done.25, f32[128,2048]{1,0:T(8,128)S(1)} %copy-done.6, ...), kind=kLoop, calls=%fused_computation.13 | loop fusion | flops 2883584 | bytes 4719104 | tf_op jit(solution)/shard_map/convert_element_type | solution.py:202
  (55 shorter events, 0.3 us)
Async XLA Ops:
  0.0 49.3 %copy-start.2 = (bf16[128,2048]{1,0:T(8,128)(2,1)S(1)}, bf16[128,2048]{1,0:T(8,128)(2,1)}, u32[]{:S(2)}) copy-start(bf16[128,2048]{1,0:T(8,128)(2,1)} %refs_0_.1) | copy-start | bytes 1572868
  2.1 55.6 %slice-start = ((s8[9437184]{0:T(1024)(128)(4,1)}), s8[1048576]{0:T(1024)(128)(4,1)S(1)}, s32[]{:S(2)}) async-start(s8[9437184]{0:T(1024)(128)(4,1)} %bitcast.35), calls=%async_computation | async-start | bytes 2097152
  3.3 15.7 %collective-permute-start.3 = (bf16[128,2176]{1,0:T(8,128)(2,1)S(1)}, bf16[128,2176]{1,0:T(8,128)(2,1)}, u32[]{:S(2)}, u32[]{:S(2)}) collective-permute-start(bf16[128,2176]{1,0:T(8,128)(2,1)S(1)} %fusion.5.refs_0_), channel_id=1, source_target_pairs={{0,8},{2,10},{8,16},{10,18},{16,24},{18,26},{24,28},{26,30},{28,20... | collective-permute-start | bytes 1671176 | tf_op jit(solution)/shard_map/ppermute | solution.py:158
  6.4 14.5 %collective-permute-start.2 = (bf16[128,2176]{1,0:T(8,128)(2,1)S(1)}, bf16[128,2176]{1,0:T(8,128)(2,1)}, u32[]{:S(2)}, u32[]{:S(2)}) collective-permute-start(bf16[128,2176]{1,0:T(8,128)(2,1)S(1)} %fusion.5.refs_0_), channel_id=1, source_target_pairs={{8,0},{10,2},{16,8},{18,10},{24,16},{26,18},{28,24},{30,26},{20,28... | collective-permute-start | bytes 1671176 | tf_op jit(solution)/shard_map/ppermute | solution.py:158
  19.0 14.0 %collective-permute-start.8 = (bf16[128,2176]{1,0:T(8,128)(2,1)}, bf16[128,2176]{1,0:T(8,128)(2,1)S(1)}, u32[]{:S(2)}, u32[]{:S(2)}) collective-permute-start(bf16[128,2176]{1,0:T(8,128)(2,1)} %collective-permute-done.3.refs_1_), channel_id=1, source_target_pairs={{0,8},{2,10},{8,16},{10,18},{16,24},{18,26},{24,28},{26,30},{28,20... | collective-permute-start | bytes 1671176 | tf_op jit(solution)/shard_map/ppermute | solution.py:158
  20.9 13.7 %collective-permute-start.7 = (bf16[128,2176]{1,0:T(8,128)(2,1)}, bf16[128,2176]{1,0:T(8,128)(2,1)}, u32[]{:S(2)}, u32[]{:S(2)}) collective-permute-start(bf16[128,2176]{1,0:T(8,128)(2,1)} %collective-permute-done.2.refs_0_), channel_id=1, source_target_pairs={{8,0},{10,2},{16,8},{18,10},{24,16},{26,18},{28,24},{30,26},{20,28... | collective-permute-start | bytes 1671176 | tf_op jit(solution)/shard_map/ppermute | solution.py:158
  33.1 13.0 %copy-start.7 = (bf16[128,2176]{1,0:T(8,128)(2,1)}, bf16[128,2176]{1,0:T(8,128)(2,1)S(1)}, u32[]{:S(2)}) copy-start(bf16[128,2176]{1,0:T(8,128)(2,1)S(1)} %collective-permute-done.8.refs_1_) | copy-start | bytes 1671172
  33.1 13.0 %collective-permute-start.13 = (bf16[128,2176]{1,0:T(8,128)(2,1)S(1)}, bf16[128,2176]{1,0:T(8,128)(2,1)S(1)}, u32[]{:S(2)}, u32[]{:S(2)}) collective-permute-start(bf16[128,2176]{1,0:T(8,128)(2,1)S(1)} %collective-permute-done.8.refs_1_), channel_id=1, source_target_pairs={{0,8},{2,10},{8,16},{10,18},{16,24},{18,26},{24,28},{26,30},{28,20... | collective-permute-start | bytes 1671176 | tf_op jit(solution)/shard_map/ppermute | solution.py:158
  34.6 12.6 %collective-permute-start.12 = (bf16[128,2176]{1,0:T(8,128)(2,1)}, bf16[128,2176]{1,0:T(8,128)(2,1)S(1)}, u32[]{:S(2)}, u32[]{:S(2)}) collective-permute-start(bf16[128,2176]{1,0:T(8,128)(2,1)} %collective-permute-done.7.refs_0_), channel_id=1, source_target_pairs={{8,0},{10,2},{16,8},{18,10},{24,16},{26,18},{28,24},{30,26},{20,28... | collective-permute-start | bytes 1671176 | tf_op jit(solution)/shard_map/ppermute | solution.py:158
  35.1 13.7 %collective-permute-start.30 = (bf16[128,2048]{1,0:T(8,128)(2,1)}, bf16[128,2048]{1,0:T(8,128)(2,1)}, u32[]{:S(2)}, u32[]{:S(2)}) collective-permute-start(bf16[128,2048]{1,0:T(8,128)(2,1)} %refs_0_.1), channel_id=1, source_target_pairs={{0,1},{1,0},{2,3},{3,2},{4,5},{5,4},{6,7},{7,6},{8,9},{9,8},{10,11... | collective-permute-start | bytes 1572872 | tf_op jit(solution)/shard_map/ppermute | solution.py:16
  36.6 19.6 %collective-permute-start = (bf16[128,2176]{1,0:T(8,128)(2,1)S(1)}, bf16[128,2176]{1,0:T(8,128)(2,1)}, u32[]{:S(2)}, u32[]{:S(2)}) collective-permute-start(bf16[128,2176]{1,0:T(8,128)(2,1)S(1)} %fusion.5.refs_0_), channel_id=1, source_target_pairs={{0,2},{2,0},{4,6},{6,4},{8,10},{10,8},{12,14},{14,12},{16,18},{18,... | collective-permute-start | bytes 1671176 | tf_op jit(solution)/shard_map/ppermute | solution.py:158
  36.6 27.2 %collective-permute-start.4 = (bf16[128,2176]{1,0:T(8,128)(2,1)}, bf16[128,2176]{1,0:T(8,128)(2,1)}, u32[]{:S(2)}, u32[]{:S(2)}) collective-permute-start(bf16[128,2176]{1,0:T(8,128)(2,1)} %collective-permute-done.2.refs_0_), channel_id=1, source_target_pairs={{0,2},{2,0},{4,6},{6,4},{8,10},{10,8},{12,14},{14,12},{16,18},{18,... | collective-permute-start | bytes 1671176 | tf_op jit(solution)/shard_map/ppermute | solution.py:158
  46.1 17.8 %collective-permute-start.5 = (bf16[128,2176]{1,0:T(8,128)(2,1)}, bf16[128,2176]{1,0:T(8,128)(2,1)}, u32[]{:S(2)}, u32[]{:S(2)}) collective-permute-start(bf16[128,2176]{1,0:T(8,128)(2,1)} %collective-permute-done.3.refs_1_), channel_id=1, source_target_pairs={{0,2},{2,0},{4,6},{6,4},{8,10},{10,8},{12,14},{14,12},{16,18},{18,... | collective-permute-start | bytes 1671176 | tf_op jit(solution)/shard_map/ppermute | solution.py:158
  47.2 17.2 %collective-permute-start.17 = (bf16[64,2176]{1,0:T(8,128)(2,1)S(1)}, bf16[64,2176]{1,0:T(8,128)(2,1)S(1)}, u32[]{:S(2)}, u32[]{:S(2)}) collective-permute-start(bf16[64,2176]{1,0:T(8,128)(2,1)S(1)} %slice.134), channel_id=1, source_target_pairs={{0,8},{2,10},{8,16},{10,18},{16,24},{18,26},{24,28},{26,30},{28,20... | collective-permute-start | bytes 835592 | tf_op jit(solution)/shard_map/ppermute | solution.py:158
  48.8 15.6 %collective-permute-start.18 = (bf16[64,2176]{1,0:T(8,128)(2,1)S(1)}, bf16[64,2176]{1,0:T(8,128)(2,1)S(1)}, u32[]{:S(2)}, u32[]{:S(2)}) collective-permute-start(bf16[64,2176]{1,0:T(8,128)(2,1)S(1)} %slice.135), channel_id=1, source_target_pairs={{8,0},{10,2},{16,8},{18,10},{24,16},{26,18},{28,24},{30,26},{20,28... | collective-permute-start | bytes 835592 | tf_op jit(solution)/shard_map/ppermute | solution.py:158
  49.3 2.3 %copy-start.1 = (bf16[1,3,384,2048]{3,2,1,0:T(8,128)(2,1)S(1)}, bf16[1,3,384,2048]{3,2,1,0:T(8,128)(2,1)}, u32[]{:S(2)}) copy-start(bf16[1,3,384,2048]{3,2,1,0:T(8,128)(2,1)} %refs_4_.11) | copy-start | bytes 14155780
  51.6 6.1 %slice-start.1 = ((s8[9437184]{0:T(1024)(128)(4,1)}), s8[4194304]{0:T(1024)(128)(4,1)S(1)}, s32[]{:S(2)}) async-start(s8[9437184]{0:T(1024)(128)(4,1)} %bitcast.35), calls=%async_computation.1 | async-start | bytes 8388608
  51.6 6.1 %slice-start.2 = ((s8[9437184]{0:T(1024)(128)(4,1)}), s8[4194304]{0:T(1024)(128)(4,1)S(1)}, s32[]{:S(2)}) async-start(s8[9437184]{0:T(1024)(128)(4,1)} %bitcast.35), calls=%async_computation.2 | async-start | bytes 8388608
  56.2 7.5 %copy-start.3 = (f32[128,2048]{1,0:T(8,128)}, f32[128,2048]{1,0:T(8,128)S(1)}, u32[]{:S(2)}) copy-start(f32[128,2048]{1,0:T(8,128)S(1)} %get-tuple-element.27) | copy-start | bytes 3145732
  56.2 88.8 %collective-permute-start.31 = (bf16[128,2048]{1,0:T(8,128)(2,1)}, bf16[128,2048]{1,0:T(8,128)(2,1)}, u32[]{:S(2)}, u32[]{:S(2)}) collective-permute-start(bf16[128,2048]{1,0:T(8,128)(2,1)} %get-tuple-element.28), channel_id=1, source_target_pairs={{0,1},{1,0},{2,3},{3,2},{4,5},{5,4},{6,7},{7,6},{8,9},{9,8},{10,11... | collective-permute-start | bytes 1572872 | tf_op jit(solution)/shard_map/ppermute | solution.py:16
  63.7 11.7 %copy-start.5 = (f32[128,2048]{1,0:T(8,128)}, f32[128,2048]{1,0:T(8,128)S(1)}, u32[]{:S(2)}) copy-start(f32[128,2048]{1,0:T(8,128)S(1)} %get-tuple-element.17) | copy-start | bytes 3145732
  63.7 11.7 %copy-start.8 = (bf16[128,2176]{1,0:T(8,128)(2,1)S(1)}, bf16[128,2176]{1,0:T(8,128)(2,1)}, u32[]{:S(2)}) copy-start(bf16[128,2176]{1,0:T(8,128)(2,1)} %copy-done.7) | copy-start | bytes 1671172
  63.8 20.7 %collective-permute-start.14 = (bf16[128,2176]{1,0:T(8,128)(2,1)S(1)}, bf16[128,2176]{1,0:T(8,128)(2,1)S(1)}, u32[]{:S(2)}, u32[]{:S(2)}) collective-permute-start(bf16[128,2176]{1,0:T(8,128)(2,1)S(1)} %collective-permute-done.12.refs_0_), channel_id=1, source_target_pairs={{0,2},{2,0},{4,6},{6,4},{8,10},{10,8},{12,14},{14,12},{16,18},{18,... | collective-permute-start | bytes 1671176 | tf_op jit(solution)/shard_map/ppermute | solution.py:158
  63.9 20.8 %collective-permute-start.15 = (bf16[128,2176]{1,0:T(8,128)(2,1)S(1)}, bf16[128,2176]{1,0:T(8,128)(2,1)S(1)}, u32[]{:S(2)}, u32[]{:S(2)}) collective-permute-start(bf16[128,2176]{1,0:T(8,128)(2,1)S(1)} %collective-permute-done.13.refs_1_), channel_id=1, source_target_pairs={{0,2},{2,0},{4,6},{6,4},{8,10},{10,8},{12,14},{14,12},{16,18},{18,... | collective-permute-start | bytes 1671176 | tf_op jit(solution)/shard_map/ppermute | solution.py:158
  64.4 11.1 %collective-permute-start.19 = (bf16[64,2176]{1,0:T(8,128)(2,1)S(1)}, bf16[64,2176]{1,0:T(8,128)(2,1)S(1)}, u32[]{:S(2)}, u32[]{:S(2)}) collective-permute-start(bf16[64,2176]{1,0:T(8,128)(2,1)S(1)} %collective-permute-done.17.refs_0_), channel_id=1, source_target_pairs={{0,2},{2,0},{4,6},{6,4},{8,10},{10,8},{12,14},{14,12},{16,18},{18,... | collective-permute-start | bytes 835592 | tf_op jit(solution)/shard_map/ppermute | solution.py:158
  64.4 11.2 %collective-permute-start.20 = (bf16[64,2176]{1,0:T(8,128)(2,1)S(1)}, bf16[64,2176]{1,0:T(8,128)(2,1)S(1)}, u32[]{:S(2)}, u32[]{:S(2)}) collective-permute-start(bf16[64,2176]{1,0:T(8,128)(2,1)S(1)} %collective-permute-done.18.refs_1_), channel_id=1, source_target_pairs={{0,2},{2,0},{4,6},{6,4},{8,10},{10,8},{12,14},{14,12},{16,18},{18,... | collective-permute-start | bytes 835592 | tf_op jit(solution)/shard_map/ppermute | solution.py:158
  75.4 19.2 %collective-permute-start.10 = (bf16[128,2176]{1,0:T(8,128)(2,1)S(1)}, bf16[128,2176]{1,0:T(8,128)(2,1)S(1)}, u32[]{:S(2)}, u32[]{:S(2)}) collective-permute-start(bf16[128,2176]{1,0:T(8,128)(2,1)S(1)} %copy-done.8), channel_id=1, source_target_pairs={{0,2},{2,0},{4,6},{6,4},{8,10},{10,8},{12,14},{14,12},{16,18},{18,... | collective-permute-start | bytes 1671176 | tf_op jit(solution)/shard_map/ppermute | solution.py:158
  75.6 19.2 %collective-permute-start.9 = (bf16[128,2176]{1,0:T(8,128)(2,1)}, bf16[128,2176]{1,0:T(8,128)(2,1)S(1)}, u32[]{:S(2)}, u32[]{:S(2)}) collective-permute-start(bf16[128,2176]{1,0:T(8,128)(2,1)} %collective-permute-done.7.refs_0_), channel_id=1, source_target_pairs={{0,2},{2,0},{4,6},{6,4},{8,10},{10,8},{12,14},{14,12},{16,18},{18,... | collective-permute-start | bytes 1671176 | tf_op jit(solution)/shard_map/ppermute | solution.py:158
  76.0 3.7 %copy-start = (bf16[1,3,768,2048]{3,2,1,0:T(8,128)(2,1)S(1)}, bf16[1,3,768,2048]{3,2,1,0:T(8,128)(2,1)}, u32[]{:S(2)}) copy-start(bf16[1,3,768,2048]{3,2,1,0:T(8,128)(2,1)} %refs_6_.7) | copy-start | bytes 28311556
  84.5 60.5 %collective-permute-start.1 = (bf16[128,2048]{1,0:T(8,128)(2,1)S(1)}, bf16[128,2048]{1,0:T(8,128)(2,1)S(1)}, u32[]{:S(2)}, u32[]{:S(2)}) collective-permute-start(bf16[128,2048]{1,0:T(8,128)(2,1)S(1)} %get-tuple-element.18), channel_id=1, source_target_pairs={{0,2},{2,0},{4,6},{6,4},{8,10},{10,8},{12,14},{14,12},{16,18},{18,... | collective-permute-start | bytes 1572872 | tf_op jit(solution)/shard_map/ppermute | solution.py:158
  84.7 20.7 %collective-permute-start.21 = (bf16[128,2048]{1,0:T(8,128)(2,1)S(1)}, bf16[128,2048]{1,0:T(8,128)(2,1)S(1)}, u32[]{:S(2)}, u32[]{:S(2)}) collective-permute-start(bf16[128,2048]{1,0:T(8,128)(2,1)S(1)} %get-tuple-element.26), channel_id=1, source_target_pairs={{0,2},{2,0},{4,6},{6,4},{8,10},{10,8},{12,14},{14,12},{16,18},{18,... | collective-permute-start | bytes 1572872 | tf_op jit(solution)/shard_map/ppermute | solution.py:158
  94.7 12.5 %collective-permute-start.16 = (bf16[256,2048]{1,0:T(8,128)(2,1)S(1)}, bf16[256,2048]{1,0:T(8,128)(2,1)S(1)}, u32[]{:S(2)}, u32[]{:S(2)}) collective-permute-start(bf16[256,2048]{1,0:T(8,128)(2,1)S(1)} %get-tuple-element.24), channel_id=1, source_target_pairs={{0,2},{2,0},{4,6},{6,4},{8,10},{10,8},{12,14},{14,12},{16,18},{18,... | collective-permute-start | bytes 3145736 | tf_op jit(solution)/shard_map/ppermute | solution.py:158
  104.9 11.0 %collective-permute-start.11 = (bf16[256,2048]{1,0:T(8,128)(2,1)S(1)}, bf16[256,2048]{1,0:T(8,128)(2,1)S(1)}, u32[]{:S(2)}, u32[]{:S(2)}) collective-permute-start(bf16[256,2048]{1,0:T(8,128)(2,1)S(1)} %get-tuple-element.22), channel_id=1, source_target_pairs={{0,2},{2,0},{4,6},{6,4},{8,10},{10,8},{12,14},{14,12},{16,18},{18,... | collective-permute-start | bytes 3145736 | tf_op jit(solution)/shard_map/ppermute | solution.py:158
  105.5 8.4 %collective-permute-start.22 = (bf16[64,2048]{1,0:T(8,128)(2,1)S(1)}, bf16[64,2048]{1,0:T(8,128)(2,1)S(1)}, u32[]{:S(2)}, u32[]{:S(2)}) collective-permute-start(bf16[64,2048]{1,0:T(8,128)(2,1)S(1)} %get-tuple-element.39), channel_id=1, source_target_pairs={{0,8},{2,10},{8,16},{10,18},{16,24},{18,26},{24,28},{26,30},{28,20... | collective-permute-start | bytes 786440 | tf_op jit(solution)/shard_map/ppermute | solution.py:158
  107.2 8.0 %collective-permute-start.26 = (bf16[64,2048]{1,0:T(8,128)(2,1)S(1)}, bf16[64,2048]{1,0:T(8,128)(2,1)S(1)}, u32[]{:S(2)}, u32[]{:S(2)}) collective-permute-start(bf16[64,2048]{1,0:T(8,128)(2,1)S(1)} %get-tuple-element.40), channel_id=1, source_target_pairs={{8,0},{10,2},{16,8},{18,10},{24,16},{26,18},{28,24},{30,26},{20,28... | collective-permute-start | bytes 786440 | tf_op jit(solution)/shard_map/ppermute | solution.py:158
  113.9 17.3 %collective-permute-start.6 = (bf16[256,2048]{1,0:T(8,128)(2,1)S(1)}, bf16[256,2048]{1,0:T(8,128)(2,1)S(1)}, u32[]{:S(2)}, u32[]{:S(2)}) collective-permute-start(bf16[256,2048]{1,0:T(8,128)(2,1)S(1)} %get-tuple-element.20), channel_id=1, source_target_pairs={{0,2},{2,0},{4,6},{6,4},{8,10},{10,8},{12,14},{14,12},{16,18},{18,... | collective-permute-start | bytes 3145736 | tf_op jit(solution)/shard_map/ppermute | solution.py:158
  115.3 13.1 %collective-permute-start.27 = (bf16[128,2048]{1,0:T(8,128)(2,1)S(1)}, bf16[128,2048]{1,0:T(8,128)(2,1)S(1)}, u32[]{:S(2)}, u32[]{:S(2)}) collective-permute-start(bf16[128,2048]{1,0:T(8,128)(2,1)S(1)} %pad_maximum_fusion.1), channel_id=1, source_target_pairs={{8,0},{10,2},{16,8},{18,10},{24,16},{26,18},{28,24},{30,26},{20,28... | collective-permute-start | bytes 1572872 | tf_op jit(solution)/shard_map/ppermute | solution.py:158
  115.9 12.9 %collective-permute-start.23 = (bf16[128,2048]{1,0:T(8,128)(2,1)S(1)}, bf16[128,2048]{1,0:T(8,128)(2,1)S(1)}, u32[]{:S(2)}, u32[]{:S(2)}) collective-permute-start(bf16[128,2048]{1,0:T(8,128)(2,1)S(1)} %pad_maximum_fusion), channel_id=1, source_target_pairs={{0,8},{2,10},{8,16},{10,18},{16,24},{18,26},{24,28},{26,30},{28,20... | collective-permute-start | bytes 1572872 | tf_op jit(solution)/shard_map/ppermute | solution.py:158
  129.1 12.8 %collective-permute-start.24 = (bf16[128,2048]{1,0:T(8,128)(2,1)S(1)}, bf16[128,2048]{1,0:T(8,128)(2,1)S(1)}, u32[]{:S(2)}, u32[]{:S(2)}) collective-permute-start(bf16[128,2048]{1,0:T(8,128)(2,1)S(1)} %get-tuple-element.33), channel_id=1, source_target_pairs={{0,8},{2,10},{8,16},{10,18},{16,24},{18,26},{24,28},{26,30},{28,20... | collective-permute-start | bytes 1572872 | tf_op jit(solution)/shard_map/ppermute | solution.py:158
  130.6 11.6 %collective-permute-start.28 = (bf16[128,2048]{1,0:T(8,128)(2,1)S(1)}, bf16[128,2048]{1,0:T(8,128)(2,1)S(1)}, u32[]{:S(2)}, u32[]{:S(2)}) collective-permute-start(bf16[128,2048]{1,0:T(8,128)(2,1)S(1)} %get-tuple-element.34), channel_id=1, source_target_pairs={{8,0},{10,2},{16,8},{18,10},{24,16},{26,18},{28,24},{30,26},{20,28... | collective-permute-start | bytes 1572872 | tf_op jit(solution)/shard_map/ppermute | solution.py:158
  131.5 24.8 %copy-start.4 = (f32[128,2048]{1,0:T(8,128)S(1)}, f32[128,2048]{1,0:T(8,128)}, u32[]{:S(2)}) copy-start(f32[128,2048]{1,0:T(8,128)} %copy-done.3) | copy-start | bytes 3145732
  131.6 24.8 %copy-start.6 = (f32[128,2048]{1,0:T(8,128)S(1)}, f32[128,2048]{1,0:T(8,128)}, u32[]{:S(2)}) copy-start(f32[128,2048]{1,0:T(8,128)} %copy-done.5) | copy-start | bytes 3145732
  142.5 11.7 %collective-permute-start.25 = (bf16[128,2048]{1,0:T(8,128)(2,1)S(1)}, bf16[128,2048]{1,0:T(8,128)(2,1)S(1)}, u32[]{:S(2)}, u32[]{:S(2)}) collective-permute-start(bf16[128,2048]{1,0:T(8,128)(2,1)S(1)} %get-tuple-element.31), channel_id=1, source_target_pairs={{0,8},{2,10},{8,16},{10,18},{16,24},{18,26},{24,28},{26,30},{28,20... | collective-permute-start | bytes 1572872 | tf_op jit(solution)/shard_map/ppermute | solution.py:158
  145.0 11.4 %collective-permute-start.29 = (bf16[128,2048]{1,0:T(8,128)(2,1)S(1)}, bf16[128,2048]{1,0:T(8,128)(2,1)S(1)}, u32[]{:S(2)}, u32[]{:S(2)}) collective-permute-start(bf16[128,2048]{1,0:T(8,128)(2,1)S(1)} %get-tuple-element.32), channel_id=1, source_target_pairs={{8,0},{10,2},{16,8},{18,10},{24,16},{26,18},{28,24},{30,26},{20,28... | collective-permute-start | bytes 1572872 | tf_op jit(solution)/shard_map/ppermute | solution.py:158

commit v2 on v1

v2 whole, which is shorter than its diff:
```python
import functools

import jax
import jax.numpy as jnp
from jax import lax
from jax.experimental import pallas as pl
from jax.experimental.pallas import tpu as pltpu
from jax.sharding import PartitionSpec as P

LANES = 128
NT = (((1,), (1,)), ((), ()))


def shifted(block, axis, by):
    size = lax.axis_size(axis)
    return lax.ppermute(block, axis, [(i, (i + by) % size) for i in range(size)])


def ring_pairs(count):
    chips = count // 2
    half = chips // 2

    def first_core(place):
        place %= chips
        return 4 * place if place < half else 4 * (chips - 1 - place) + 2

    onward = [
        (first_core(place) + core, first_core(place + 1) + core)
        for place in range(chips)
        for core in range(2)
    ]
    return onward, [(target, source) for source, target in onward]


def expert_kernel(parts, kept_rows, features, scaled, tile, width, owner_ref, *refs):
    blocks, (weight_ref, keep_ref, send_ref, inputs, scale, hidden) = refs[:parts], refs[parts:]
    row = 0
    for block in blocks:
        rows = block.shape[0]
        inputs[row : row + rows, :] = block[:, :features]
        if scaled:
            extra = block[:, features:].astype(jnp.float32)
            lane = lax.broadcasted_iota(jnp.int32, extra.shape, 1)
            owner, count = owner_ref[0], owner_ref[1]
            mine = (lane == owner) | (lane == owner + count) | (lane == owner + 2 * count)
            scale[row : row + rows, :] = jnp.sum(
                jnp.where(mine, extra, 0.0), axis=1, keepdims=True
            )
        row += rows

    units = hidden.shape[1]
    for first in range(0, units, tile):
        some = slice(first, first + tile)
        values = inputs[...]
        gate = lax.dot_general(
            values, weight_ref[0, 0, some, :], NT, preferred_element_type=jnp.float32
        )
        up = lax.dot_general(
            values, weight_ref[0, 1, some, :], NT, preferred_element_type=jnp.float32
        )
        hidden[:, some] = (gate / (1.0 + jnp.exp(-gate)) * up).astype(jnp.bfloat16)
    for first in range(0, features, width):
        some = slice(first, first + width)
        result = jnp.dot(
            hidden[...], weight_ref[0, 2, :, some], preferred_element_type=jnp.float32
        )
        if scaled:
            result = result * scale[...]
        keep_ref[:, some] = result[:kept_rows]
        send_ref[:, some] = result[kept_rows:].astype(jnp.bfloat16)


def expert_apply(blocks, weights, kept_rows, features, owner, tile, width):
    scaled = owner is not None
    if owner is None:
        owner = jnp.zeros((2,), jnp.int32)
    rows = sum(block.shape[0] for block in blocks)
    units = weights.shape[2]
    tile = tile if units % tile == 0 else units
    whole = pl.BlockSpec(memory_space=pltpu.VMEM)
    return pl.pallas_call(
        functools.partial(
            expert_kernel, len(blocks), kept_rows, features, scaled, tile, width
        ),
        in_specs=[pl.BlockSpec(memory_space=pltpu.SMEM)] + [whole] * (len(blocks) + 1),
        out_specs=[whole, whole],
        out_shape=[
            jax.ShapeDtypeStruct((kept_rows, features), jnp.float32),
            jax.ShapeDtypeStruct((rows - kept_rows, features), jnp.bfloat16),
        ],
        scratch_shapes=[
            pltpu.VMEM((rows, features), jnp.bfloat16),
            pltpu.VMEM((rows, 1), jnp.float32),
            pltpu.VMEM((rows, units), jnp.bfloat16),
        ],
        compiler_params=pltpu.CompilerParams(vmem_limit_bytes=32 * 1024 * 1024),
        cost_estimate=pl.CostEstimate(
            flops=6 * rows * units * features,
            bytes_accessed=2 * 3 * units * features + 8 * rows * features,
            transcendentals=rows * units,
        ),
    )(owner, *blocks, weights)


def on_device(tokens, expert_ids, gate_weights, hot_weights, cold_weights):
    rows, features = tokens.shape
    count = lax.axis_size("dp")
    groups = lax.axis_size("expert")
    experts = 1 + count
    onward, backward = ring_pairs(count)
    across = [(i, i ^ 1) for i in range(count)]
    reach = count // 4
    owner = jnp.stack([lax.axis_index("dp"), count]).astype(jnp.int32)

    labels = jnp.arange(experts, dtype=jnp.int32)[None, :]
    table = jnp.zeros((rows, experts), jnp.float32)
    for k in range(expert_ids.shape[1]):
        table = table + jnp.where(
            expert_ids[:, k : k + 1] == labels, gate_weights[:, k : k + 1], 0.0
        )
    cold_table = table[:, 1:]
    high = lax.reduce_precision(cold_table, 8, 7)
    rest = cold_table - high
    middle = lax.reduce_precision(rest, 8, 7)
    low = rest - middle
    extra = -(3 * count) % LANES
    payload = jnp.concatenate(
        [
            tokens,
            jnp.pad(
                jnp.concatenate([high, middle, low], axis=1).astype(jnp.bfloat16),
                ((0, 0), (0, extra)),
            ),
        ],
        axis=1,
    )

    def go(block, pairs):
        return lax.ppermute(block, "dp", pairs)

    def exchange(blocks):
        return [go(block, across) for block in blocks]

    def serve(blocks, others):
        kept = sum(block.shape[0] for block in blocks)
        keep, send = expert_apply(blocks + others, cold_weights, kept, features, owner, 256, 512)
        return keep, send

    def hold(*values):
        return lax.optimization_barrier(values)

    half = rows // 2
    hot_blocks = [tokens] + [shifted(tokens, "expert", by) for by in range(1, groups)]
    fore, back = go(payload, onward), go(payload, backward)
    blocks = [payload]
    others = exchange(blocks)
    served = {}
    for k in range(1, reach + 1):
        result = serve(blocks, others)
        fore, back, *result = hold(fore, back, *result)
        served[k - 1] = result
        blocks = [back, fore]
        others = exchange(blocks)
        if k + 1 < reach:
            fore, back = go(fore, onward), go(back, backward)
        elif k + 1 == reach:
            fore, back = go(fore[:half], onward), go(back[half:], backward)
        else:
            blocks = [fore, back]
            others = exchange(blocks)
            served[reach] = serve(blocks, others)

    hot_keep, hot_send = expert_apply(hot_blocks, hot_weights, rows, features, None, 384, 512)

    def joined(k):
        keep, send = served[k]
        return keep + go(send, across).astype(jnp.float32)

    own = joined(0)
    sums = {}
    for k in range(1, reach):
        both = joined(k)
        sums[k], sums[-k] = both[:rows], both[rows:]
    both = joined(reach)

    fore = go(both[:half].astype(jnp.bfloat16), onward)
    back = go(both[half:].astype(jnp.bfloat16), backward)
    for k in range(reach - 1, 0, -1):
        fore_sum, back_sum = sums[k], sums[-k]
        if k == reach - 1:
            fore = jnp.concatenate([fore_sum[:half] + fore, fore_sum[half:]], axis=0)
            back = jnp.concatenate([back_sum[:half], back_sum[half:] + back], axis=0)
        else:
            fore, back = fore_sum + fore, back_sum + back
        fore, back = go(fore.astype(jnp.bfloat16), onward), go(back.astype(jnp.bfloat16), backward)

    hot = hot_keep
    for by in range(1, groups):
        hot = hot + shifted(hot_send[(by - 1) * rows : by * rows], "expert", -by)
    combined = own + fore.astype(jnp.float32) + back.astype(jnp.float32) + table[:, :1] * hot
    return combined.astype(jnp.bfloat16)


def solution(mesh):
    placed = (
        P(("dp", "expert"), None),
        P(("dp", "expert"), None),
        P(("dp", "expert"), None),
        P(None, None, "expert", None),
        P("dp", None, None, None),
    )
    return jax.shard_map(
        on_device, mesh=mesh, in_specs=placed, out_specs=P(("dp", "expert"), None), check_vma=False
    )
```

time: 159 us -> 135 us (0.85)
  Pallas kernels: 45.5 us -> 26.1 us
  local copies, waits for them, and re-layouts: 8.28 us -> 5.92 us
    pallas_call x6, Pallas kernels: 45.5 us -> 26.1 us  [expert_apply(): pl.pallas_call(functools.partial(expert_kernel, len(blocks), kept_rows, f...]
    ppermute x30, waiting for transfers between devices: 74.7 us -> 65.7 us  [go(): return lax.ppermute(block, 'dp', pairs)]
    ppermute x2, waiting for transfers between devices: 0.01 us -> 8.51 us  [shifted(): lax.ppermute(block, axis, [(i, (i + by) % size) for i in range(size)])]
    unnamed x24 -> x10, local copies, waits for them, and re-layouts: 6.06 us -> 3.7 us
  transfers between devices with their start and end apart: 32 -> 32, of which waited for: 12 -> 20; matrix products, arithmetic and copies ran while one was open for 1% -> 2% of each run, Pallas kernels for 29% -> 19%
where the time goes in v2:
time: 135 us
  waiting for transfers between devices  74.2 us (55%)
  Pallas kernels  26.1 us (19%)
  starting transfers between devices  23.9 us (18%)
  local copies, waits for them, and re-layouts  5.92 us (4%)
  other arithmetic  4.51 us (3%)
    ppermute x30, waiting for transfers between devices, go(): return lax.ppermute(block, 'dp', pairs)  65.7 us
    pallas_call x6, Pallas kernels, expert_apply(): pl.pallas_call(functools.partial(expert_kernel, len(blocks), kept_rows, f...  26.1 us
    ppermute x30, starting transfers between devices, go(): return lax.ppermute(block, 'dp', pairs)  20.8 us
    ppermute x2, waiting for transfers between devices, shifted(): lax.ppermute(block, axis, [(i, (i + by) % size) for i in range(size)])  8.51 us
    unnamed x10, local copies, waits for them, and re-layouts  3.7 us
    ppermute x2, starting transfers between devices, shifted(): lax.ppermute(block, axis, [(i, (i + by) % size) for i in range(size)])  3.11 us
  transfers between devices with their start and end apart: 32, of which 20 were waited for; matrix products, arithmetic and copies ran while one was open for 2% of the time, Pallas kernels for 19%

profile of v2, /device:TPU:0, one launch (start us, length us, event | category | flops | bytes accessed | tf_op | source)
XLA Modules:
  0.0 134.8 jit_solution(1214784585640024721)
XLA Ops:
  0.0 1.0 slice_bitcast_fusion.15
  1.0 1.0 slice_bitcast_fusion.16
  2.0 0.1 copy.6
  2.1 1.1 fusion.5.refs_0_
  3.2 0.5 collective-permute-start.2
  3.7 2.6 %collective-permute-start = (bf16[128,2176]{1,0:T(8,128)(2,1)S(1)}, bf16[128,2176]{1,0:T(8,128)(2,1)S(1)}, u32[]{:S(2)}, u32[]{:S(2)}) collective-permute-start(bf16[128,2176]{1,0:T(8,128)(2,1)S(1)} %fusion.5.refs_0_), channel_id=1, source_target_pairs={{0,8},{2,10},{8,16},{10,18},{16,24},{18,26},{24,28},{26,30},{28,20... | collective-permute-start | bytes 1671176 | tf_op jit(solution)/shard_map/ppermute | solution.py:139
  6.5 3.7 %copy-done = bf16[1,3,768,2048]{3,2,1,0:T(8,128)(2,1)S(1)} copy-done((bf16[1,3,768,2048]{3,2,1,0:T(8,128)(2,1)S(1)}, bf16[1,3,768,2048]{3,2,1,0:T(8,128)(2,1)}, u32[]{:S(2)}) %copy-start) | copy-done | bytes 9437208
  10.1 3.3 %shard_map.55 = (f32[128,2048]{1,0:T(8,128)S(1)}, bf16[128,2048]{1,0:T(8,128)(2,1)S(1)}) custom-call(s32[2]{0:T(128)S(1)} %pad_add_fusion.owner_ref, bf16[128,2176]{1,0:T(8,128)(2,1)S(1)} %fusion.5.refs_0_, bf16[128,2176]{1,0:T(8,128)(2,1)S(1)} %collective-permute-done.2.refs_1_, bf16[1,3,768,2048]{3,2,1,0:T(8,128)(2,1)S(1)} %copy-done), custom_call_target="tpu_custom_call" | custom-call | flops 2415919104 | bytes 13631488 | tf_op jit(solution)/shard_map/pallas_call | solution.py:81
  13.4 6.1 %collective-permute-done.refs_1_ = bf16[128,2176]{1,0:T(8,128)(2,1)S(1)} collective-permute-done((bf16[128,2176]{1,0:T(8,128)(2,1)S(1)}, bf16[128,2176]{1,0:T(8,128)(2,1)S(1)}, u32[]{:S(2)}, u32[]{:S(2)}) %collective-permute-start) | collective-permute-done | bytes 557088 | tf_op jit(solution)/shard_map/ppermute | solution.py:139
  19.5 1.5 %collective-permute-done.1.refs_0_ = bf16[128,2176]{1,0:T(8,128)(2,1)S(1)} collective-permute-done((bf16[128,2176]{1,0:T(8,128)(2,1)S(1)}, bf16[128,2176]{1,0:T(8,128)(2,1)S(1)}, u32[]{:S(2)}, u32[]{:S(2)}) %collective-permute-start.1) | collective-permute-done | bytes 557088 | tf_op jit(solution)/shard_map/ppermute | solution.py:139
  21.1 0.5 collective-permute-start.7
  21.6 1.6 %collective-permute-start.4 = (bf16[128,2176]{1,0:T(8,128)(2,1)S(1)}, bf16[128,2176]{1,0:T(8,128)(2,1)S(1)}, u32[]{:S(2)}, u32[]{:S(2)}) collective-permute-start(bf16[128,2176]{1,0:T(8,128)(2,1)S(1)} %collective-permute-done.refs_1_), channel_id=1, source_target_pairs={{0,8},{2,10},{8,16},{10,18},{16,24},{18,26},{24,28},{26,30},{28,20... | collective-permute-start | bytes 1671176 | tf_op jit(solution)/shard_map/ppermute | solution.py:139
  23.2 0.4 collective-permute-start.5
  23.6 0.2 collective-permute-done.7.refs_3_
  23.8 5.7 %shard_map.56 = (f32[256,2048]{1,0:T(8,128)S(1)}, bf16[256,2048]{1,0:T(8,128)(2,1)S(1)}) custom-call(s32[2]{0:T(128)S(1)} %pad_add_fusion.owner_ref, bf16[128,2176]{1,0:T(8,128)(2,1)S(1)} %collective-permute-done.1.refs_0_, bf16[128,2176]{1,0:T(8,128)(2,1)S(1)} %collective-permute-done.refs_1_, bf16[128,2176]{1,0:T(8,128)(2,1)S(1)} %collective-permute-done.6.refs_2_, ...), custom_call_target="tpu_custom_call" | custom-call | flops 4831838208 | bytes 17825792 | tf_op jit(solution)/shard_map/pallas_call | solution.py:81
  29.6 6.6 %collective-permute-done.4.refs_1_ = bf16[128,2176]{1,0:T(8,128)(2,1)S(1)} collective-permute-done((bf16[128,2176]{1,0:T(8,128)(2,1)S(1)}, bf16[128,2176]{1,0:T(8,128)(2,1)S(1)}, u32[]{:S(2)}, u32[]{:S(2)}) %collective-permute-start.4) | collective-permute-done | bytes 557088 | tf_op jit(solution)/shard_map/ppermute | solution.py:139
  36.1 1.3 collective-permute-done.5.refs_0_
  37.4 0.5 collective-permute-start.12
  37.9 1.6 %collective-permute-start.9 = (bf16[128,2176]{1,0:T(8,128)(2,1)S(1)}, bf16[128,2176]{1,0:T(8,128)(2,1)S(1)}, u32[]{:S(2)}, u32[]{:S(2)}) collective-permute-start(bf16[128,2176]{1,0:T(8,128)(2,1)S(1)} %collective-permute-done.4.refs_1_), channel_id=1, source_target_pairs={{0,8},{2,10},{8,16},{10,18},{16,24},{18,26},{24,28},{26,30},{28,20... | collective-permute-start | bytes 1671176 | tf_op jit(solution)/shard_map/ppermute | solution.py:139
  39.5 0.4 collective-permute-start.10
  40.0 0.2 collective-permute-done.12.refs_3_
  40.2 5.7 %shard_map.57 = (f32[256,2048]{1,0:T(8,128)S(1)}, bf16[256,2048]{1,0:T(8,128)(2,1)S(1)}) custom-call(s32[2]{0:T(128)S(1)} %pad_add_fusion.owner_ref, bf16[128,2176]{1,0:T(8,128)(2,1)S(1)} %collective-permute-done.5.refs_0_, bf16[128,2176]{1,0:T(8,128)(2,1)S(1)} %collective-permute-done.4.refs_1_, bf16[128,2176]{1,0:T(8,128)(2,1)S(1)} %collective-permute-done.11.refs_2_, ...), custom_call_target="tpu_custom_call" | custom-call | flops 4831838208 | bytes 17825792 | tf_op jit(solution)/shard_map/pallas_call | solution.py:81
  45.9 6.6 %collective-permute-done.9.refs_1_ = bf16[128,2176]{1,0:T(8,128)(2,1)S(1)} collective-permute-done((bf16[128,2176]{1,0:T(8,128)(2,1)S(1)}, bf16[128,2176]{1,0:T(8,128)(2,1)S(1)}, u32[]{:S(2)}, u32[]{:S(2)}) %collective-permute-start.9) | collective-permute-done | bytes 557088 | tf_op jit(solution)/shard_map/ppermute | solution.py:139
  52.5 1.3 collective-permute-done.10.refs_0_
  53.8 0.5 collective-permute-start.17
  54.3 1.5 %collective-permute-start.14 = (bf16[64,2176]{1,0:T(8,128)(2,1)S(1)}, bf16[64,2176]{1,0:T(8,128)(2,1)S(1)}, u32[]{:S(2)}, u32[]{:S(2)}) collective-permute-start(bf16[64,2176]{1,0:T(8,128)(2,1)S(1)} %slice.119), channel_id=1, source_target_pairs={{0,8},{2,10},{8,16},{10,18},{16,24},{18,26},{24,28},{26,30},{28,20... | collective-permute-start | bytes 835592 | tf_op jit(solution)/shard_map/ppermute | solution.py:139
  55.9 0.5 collective-permute-start.15
  56.4 0.1 collective-permute-done.17.refs_3_
  56.5 5.7 %shard_map.58 = (f32[256,2048]{1,0:T(8,128)S(1)}, bf16[256,2048]{1,0:T(8,128)(2,1)S(1)}) custom-call(s32[2]{0:T(128)S(1)} %pad_add_fusion.owner_ref, bf16[128,2176]{1,0:T(8,128)(2,1)S(1)} %collective-permute-done.10.refs_0_, bf16[128,2176]{1,0:T(8,128)(2,1)S(1)} %collective-permute-done.9.refs_1_, bf16[128,2176]{1,0:T(8,128)(2,1)S(1)} %collective-permute-done.16.refs_2_, ...), custom_call_target="tpu_custom_call" | custom-call | flops 4831838208 | bytes 17825792 | tf_op jit(solution)/shard_map/pallas_call | solution.py:81
  62.2 0.7 collective-permute-done.14.refs_0_
  63.0 1.2 collective-permute-done.15.refs_1_
  64.2 0.5 collective-permute-start.20
  64.7 1.5 %collective-permute-start.30 = (bf16[128,2048]{1,0:T(8,128)(2,1)S(1)}, bf16[128,2048]{1,0:T(8,128)(2,1)S(1)}, u32[]{:S(2)}, u32[]{:S(2)}) collective-permute-start(bf16[128,2048]{1,0:T(8,128)(2,1)S(1)} %copy-done.2), channel_id=1, source_target_pairs={{0,1},{1,0},{2,3},{3,2},{4,5},{5,4},{6,7},{7,6},{8,9},{9,8},{10,11... | collective-permute-start | bytes 1572872 | tf_op jit(solution)/shard_map/ppermute | solution.py:16
  66.2 3.3 %shard_map.59 = (f32[128,2048]{1,0:T(8,128)S(1)}, bf16[128,2048]{1,0:T(8,128)(2,1)S(1)}) custom-call(s32[2]{0:T(128)S(1)} %pad_add_fusion.owner_ref, bf16[64,2176]{1,0:T(8,128)(2,1)S(1)} %collective-permute-done.14.refs_0_, bf16[64,2176]{1,0:T(8,128)(2,1)S(1)} %collective-permute-done.15.refs_1_, bf16[64,2176]{1,0:T(8,128)(2,1)S(1)} %collective-permute-done.19.refs_2_, ...), custom_call_target="tpu_custom_call" | custom-call | flops 2415919104 | bytes 13631488 | tf_op jit(solution)/shard_map/pallas_call | solution.py:81
  69.5 0.1 collective-permute-start.21
  69.6 0.5 collective-permute-start.18
  70.1 8.5 %collective-permute-done.30.refs_1_ = bf16[128,2048]{1,0:T(8,128)(2,1)S(1)} collective-permute-done((bf16[128,2048]{1,0:T(8,128)(2,1)S(1)}, bf16[128,2048]{1,0:T(8,128)(2,1)S(1)}, u32[]{:S(2)}, u32[]{:S(2)}) %collective-permute-start.30) | collective-permute-done | bytes 524320 | tf_op jit(solution)/shard_map/ppermute | solution.py:16
  78.6 2.4 %shard_map.60 = (f32[128,2048]{1,0:T(8,128)S(1)}, bf16[128,2048]{1,0:T(8,128)(2,1)S(1)}) custom-call(s32[2]{0:T(128)S(1)} %broadcast_1_owner_ref.2.owner_ref, bf16[128,2048]{1,0:T(8,128)(2,1)S(1)} %copy-done.2, bf16[128,2048]{1,0:T(8,128)(2,1)S(1)} %collective-permute-done.30.refs_1_, bf16[1,3,384,2048]{3,2,1,0:T(8,128)(2,1)S(1)} %bitcast.36), custom_call_target="tpu_custom_call" | custom-call | flops 1207959552 | bytes 8912896 | tf_op jit(solution)/shard_map/pallas_call | solution.py:81
  81.0 1.6 %collective-permute-start.31 = (bf16[128,2048]{1,0:T(8,128)(2,1)S(1)}, bf16[128,2048]{1,0:T(8,128)(2,1)S(1)}, u32[]{:S(2)}, u32[]{:S(2)}) collective-permute-start(bf16[128,2048]{1,0:T(8,128)(2,1)S(1)} %get-tuple-element.60), channel_id=1, source_target_pairs={{0,1},{1,0},{2,3},{3,2},{4,5},{5,4},{6,7},{7,6},{8,9},{9,8},{10,11... | collective-permute-start | bytes 1572872 | tf_op jit(solution)/shard_map/ppermute | solution.py:16
  82.6 0.5 collective-permute-start.13
  83.1 0.1 add_convert_fusion.1
  83.3 0.6 collective-permute-start.22
  83.9 1.5 %collective-permute-start.26 = (bf16[64,2048]{1,0:T(8,128)(2,1)S(1)}, bf16[64,2048]{1,0:T(8,128)(2,1)S(1)}, u32[]{:S(2)}, u32[]{:S(2)}) collective-permute-start(bf16[64,2048]{1,0:T(8,128)(2,1)S(1)} %get-tuple-element.72), channel_id=1, source_target_pairs={{8,0},{10,2},{16,8},{18,10},{24,16},{26,18},{28,24},{30,26},{20,28... | collective-permute-start | bytes 786440 | tf_op jit(solution)/shard_map/ppermute | solution.py:139
  85.4 0.4 fusion.9
  85.9 5.7 %collective-permute-done.22 = bf16[64,2048]{1,0:T(8,128)(2,1)S(1)} collective-permute-done((bf16[64,2048]{1,0:T(8,128)(2,1)S(1)}, bf16[64,2048]{1,0:T(8,128)(2,1)S(1)}, u32[]{:S(2)}, u32[]{:S(2)}) %collective-permute-start.22) | collective-permute-done | bytes 262176 | tf_op jit(solution)/shard_map/ppermute | solution.py:139
  91.6 0.2 collective-permute-done.26
  91.8 0.1 fusion.7
  92.0 0.5 collective-permute-start.23
  92.5 1.6 %collective-permute-start.27 = (bf16[128,2048]{1,0:T(8,128)(2,1)S(1)}, bf16[128,2048]{1,0:T(8,128)(2,1)S(1)}, u32[]{:S(2)}, u32[]{:S(2)}) collective-permute-start(bf16[128,2048]{1,0:T(8,128)(2,1)S(1)} %pad_maximum_fusion.1), channel_id=1, source_target_pairs={{8,0},{10,2},{16,8},{18,10},{24,16},{26,18},{28,24},{30,26},{20,28... | collective-permute-start | bytes 1572872 | tf_op jit(solution)/shard_map/ppermute | solution.py:139
  94.2 0.4 convert_add_fusion.1
  94.5 11.6 %collective-permute-done.23 = bf16[128,2048]{1,0:T(8,128)(2,1)S(1)} collective-permute-done((bf16[128,2048]{1,0:T(8,128)(2,1)S(1)}, bf16[128,2048]{1,0:T(8,128)(2,1)S(1)}, u32[]{:S(2)}, u32[]{:S(2)}) %collective-permute-start.23) | collective-permute-done | bytes 524320 | tf_op jit(solution)/shard_map/ppermute | solution.py:139
  106.1 0.4 collective-permute-done.27
  106.5 0.3 fusion.3
  106.8 0.5 collective-permute-start.24
  107.3 1.6 %collective-permute-start.28 = (bf16[128,2048]{1,0:T(8,128)(2,1)S(1)}, bf16[128,2048]{1,0:T(8,128)(2,1)S(1)}, u32[]{:S(2)}, u32[]{:S(2)}) collective-permute-start(bf16[128,2048]{1,0:T(8,128)(2,1)S(1)} %get-tuple-element.66), channel_id=1, source_target_pairs={{8,0},{10,2},{16,8},{18,10},{24,16},{26,18},{28,24},{30,26},{20,28... | collective-permute-start | bytes 1572872 | tf_op jit(solution)/shard_map/ppermute | solution.py:139
  108.9 0.4 convert_add_fusion.2
  109.2 10.6 %collective-permute-done.24 = bf16[128,2048]{1,0:T(8,128)(2,1)S(1)} collective-permute-done((bf16[128,2048]{1,0:T(8,128)(2,1)S(1)}, bf16[128,2048]{1,0:T(8,128)(2,1)S(1)}, u32[]{:S(2)}, u32[]{:S(2)}) %collective-permute-start.24) | collective-permute-done | bytes 524320 | tf_op jit(solution)/shard_map/ppermute | solution.py:139
  119.9 0.2 collective-permute-done.28
  120.1 0.3 fusion.4
  120.4 1.6 %collective-permute-start.29 = (bf16[128,2048]{1,0:T(8,128)(2,1)S(1)}, bf16[128,2048]{1,0:T(8,128)(2,1)S(1)}, u32[]{:S(2)}, u32[]{:S(2)}) collective-permute-start(bf16[128,2048]{1,0:T(8,128)(2,1)S(1)} %get-tuple-element.64), channel_id=1, source_target_pairs={{8,0},{10,2},{16,8},{18,10},{24,16},{26,18},{28,24},{30,26},{20,28... | collective-permute-start | bytes 1572872 | tf_op jit(solution)/shard_map/ppermute | solution.py:139
  122.0 0.5 collective-permute-start.25
  122.5 9.9 %collective-permute-done.29 = bf16[128,2048]{1,0:T(8,128)(2,1)S(1)} collective-permute-done((bf16[128,2048]{1,0:T(8,128)(2,1)S(1)}, bf16[128,2048]{1,0:T(8,128)(2,1)S(1)}, u32[]{:S(2)}, u32[]{:S(2)}) %collective-permute-start.29) | collective-permute-done | bytes 524320 | tf_op jit(solution)/shard_map/ppermute | solution.py:139
  132.3 1.2 collective-permute-done.25
  133.5 1.3 add_convert_fusion
  (41 shorter events, 0.4 us)
Async XLA Ops:
  3.2 3.2 %collective-permute-start.2 = (bf16[128,2176]{1,0:T(8,128)(2,1)S(1)}, bf16[128,2176]{1,0:T(8,128)(2,1)S(1)}, u32[]{:S(2)}, u32[]{:S(2)}) collective-permute-start(bf16[128,2176]{1,0:T(8,128)(2,1)S(1)} %fusion.5.refs_0_), channel_id=1, source_target_pairs={{0,2},{2,0},{4,6},{6,4},{8,10},{10,8},{12,14},{14,12},{16,18},{18,... | collective-permute-start | bytes 1671176 | tf_op jit(solution)/shard_map/ppermute | solution.py:139
  3.7 15.8 %collective-permute-start = (bf16[128,2176]{1,0:T(8,128)(2,1)S(1)}, bf16[128,2176]{1,0:T(8,128)(2,1)S(1)}, u32[]{:S(2)}, u32[]{:S(2)}) collective-permute-start(bf16[128,2176]{1,0:T(8,128)(2,1)S(1)} %fusion.5.refs_0_), channel_id=1, source_target_pairs={{0,8},{2,10},{8,16},{10,18},{16,24},{18,26},{24,28},{26,30},{28,20... | collective-permute-start | bytes 1671176 | tf_op jit(solution)/shard_map/ppermute | solution.py:139
  6.4 14.7 %collective-permute-start.1 = (bf16[128,2176]{1,0:T(8,128)(2,1)S(1)}, bf16[128,2176]{1,0:T(8,128)(2,1)S(1)}, u32[]{:S(2)}, u32[]{:S(2)}) collective-permute-start(bf16[128,2176]{1,0:T(8,128)(2,1)S(1)} %fusion.5.refs_0_), channel_id=1, source_target_pairs={{8,0},{10,2},{16,8},{18,10},{24,16},{26,18},{28,24},{30,26},{20,28... | collective-permute-start | bytes 1671176 | tf_op jit(solution)/shard_map/ppermute | solution.py:139
  6.5 3.7 %copy-start = (bf16[1,3,768,2048]{3,2,1,0:T(8,128)(2,1)S(1)}, bf16[1,3,768,2048]{3,2,1,0:T(8,128)(2,1)}, u32[]{:S(2)}) copy-start(bf16[1,3,768,2048]{3,2,1,0:T(8,128)(2,1)} %refs_4_.7) | copy-start | bytes 28311556
  10.1 13.7 %copy-start.1 = (bf16[1,3,768,2048]{3,2,1,0:T(8,128)(2,1)S(1)}, bf16[1,3,768,2048]{3,2,1,0:T(8,128)(2,1)}, u32[]{:S(2)}) copy-start(bf16[1,3,768,2048]{3,2,1,0:T(8,128)(2,1)} %refs_4_.7) | copy-start | bytes 28311556
  21.1 2.5 %collective-permute-start.6 = (bf16[128,2176]{1,0:T(8,128)(2,1)S(1)}, bf16[128,2176]{1,0:T(8,128)(2,1)S(1)}, u32[]{:S(2)}, u32[]{:S(2)}) collective-permute-start(bf16[128,2176]{1,0:T(8,128)(2,1)S(1)} %collective-permute-done.1.refs_0_), channel_id=1, source_target_pairs={{0,2},{2,0},{4,6},{6,4},{8,10},{10,8},{12,14},{14,12},{16,18},{18,... | collective-permute-start | bytes 1671176 | tf_op jit(solution)/shard_map/ppermute | solution.py:139
  21.1 2.8 %collective-permute-start.7 = (bf16[128,2176]{1,0:T(8,128)(2,1)S(1)}, bf16[128,2176]{1,0:T(8,128)(2,1)S(1)}, u32[]{:S(2)}, u32[]{:S(2)}) collective-permute-start(bf16[128,2176]{1,0:T(8,128)(2,1)S(1)} %collective-permute-done.refs_1_), channel_id=1, source_target_pairs={{0,2},{2,0},{4,6},{6,4},{8,10},{10,8},{12,14},{14,12},{16,18},{18,... | collective-permute-start | bytes 1671176 | tf_op jit(solution)/shard_map/ppermute | solution.py:139
  21.6 14.5 %collective-permute-start.4 = (bf16[128,2176]{1,0:T(8,128)(2,1)S(1)}, bf16[128,2176]{1,0:T(8,128)(2,1)S(1)}, u32[]{:S(2)}, u32[]{:S(2)}) collective-permute-start(bf16[128,2176]{1,0:T(8,128)(2,1)S(1)} %collective-permute-done.refs_1_), channel_id=1, source_target_pairs={{0,8},{2,10},{8,16},{10,18},{16,24},{18,26},{24,28},{26,30},{28,20... | collective-permute-start | bytes 1671176 | tf_op jit(solution)/shard_map/ppermute | solution.py:139
  23.2 14.3 %collective-permute-start.5 = (bf16[128,2176]{1,0:T(8,128)(2,1)S(1)}, bf16[128,2176]{1,0:T(8,128)(2,1)S(1)}, u32[]{:S(2)}, u32[]{:S(2)}) collective-permute-start(bf16[128,2176]{1,0:T(8,128)(2,1)S(1)} %collective-permute-done.1.refs_0_), channel_id=1, source_target_pairs={{8,0},{10,2},{16,8},{18,10},{24,16},{26,18},{28,24},{30,26},{20,28... | collective-permute-start | bytes 1671176 | tf_op jit(solution)/shard_map/ppermute | solution.py:139
  37.4 2.5 %collective-permute-start.11 = (bf16[128,2176]{1,0:T(8,128)(2,1)S(1)}, bf16[128,2176]{1,0:T(8,128)(2,1)S(1)}, u32[]{:S(2)}, u32[]{:S(2)}) collective-permute-start(bf16[128,2176]{1,0:T(8,128)(2,1)S(1)} %collective-permute-done.5.refs_0_), channel_id=1, source_target_pairs={{0,2},{2,0},{4,6},{6,4},{8,10},{10,8},{12,14},{14,12},{16,18},{18,... | collective-permute-start | bytes 1671176 | tf_op jit(solution)/shard_map/ppermute | solution.py:139
  37.4 2.8 %collective-permute-start.12 = (bf16[128,2176]{1,0:T(8,128)(2,1)S(1)}, bf16[128,2176]{1,0:T(8,128)(2,1)S(1)}, u32[]{:S(2)}, u32[]{:S(2)}) collective-permute-start(bf16[128,2176]{1,0:T(8,128)(2,1)S(1)} %collective-permute-done.4.refs_1_), channel_id=1, source_target_pairs={{0,2},{2,0},{4,6},{6,4},{8,10},{10,8},{12,14},{14,12},{16,18},{18,... | collective-permute-start | bytes 1671176 | tf_op jit(solution)/shard_map/ppermute | solution.py:139
  37.9 14.5 %collective-permute-start.9 = (bf16[128,2176]{1,0:T(8,128)(2,1)S(1)}, bf16[128,2176]{1,0:T(8,128)(2,1)S(1)}, u32[]{:S(2)}, u32[]{:S(2)}) collective-permute-start(bf16[128,2176]{1,0:T(8,128)(2,1)S(1)} %collective-permute-done.4.refs_1_), channel_id=1, source_target_pairs={{0,8},{2,10},{8,16},{10,18},{16,24},{18,26},{24,28},{26,30},{28,20... | collective-permute-start | bytes 1671176 | tf_op jit(solution)/shard_map/ppermute | solution.py:139
  39.5 14.3 %collective-permute-start.10 = (bf16[128,2176]{1,0:T(8,128)(2,1)S(1)}, bf16[128,2176]{1,0:T(8,128)(2,1)S(1)}, u32[]{:S(2)}, u32[]{:S(2)}) collective-permute-start(bf16[128,2176]{1,0:T(8,128)(2,1)S(1)} %collective-permute-done.5.refs_0_), channel_id=1, source_target_pairs={{8,0},{10,2},{16,8},{18,10},{24,16},{26,18},{28,24},{30,26},{20,28... | collective-permute-start | bytes 1671176 | tf_op jit(solution)/shard_map/ppermute | solution.py:139
  53.8 2.7 %collective-permute-start.16 = (bf16[128,2176]{1,0:T(8,128)(2,1)S(1)}, bf16[128,2176]{1,0:T(8,128)(2,1)S(1)}, u32[]{:S(2)}, u32[]{:S(2)}) collective-permute-start(bf16[128,2176]{1,0:T(8,128)(2,1)S(1)} %collective-permute-done.10.refs_0_), channel_id=1, source_target_pairs={{0,2},{2,0},{4,6},{6,4},{8,10},{10,8},{12,14},{14,12},{16,18},{18,... | collective-permute-start | bytes 1671176 | tf_op jit(solution)/shard_map/ppermute | solution.py:139
  53.8 2.8 %collective-permute-start.17 = (bf16[128,2176]{1,0:T(8,128)(2,1)S(1)}, bf16[128,2176]{1,0:T(8,128)(2,1)S(1)}, u32[]{:S(2)}, u32[]{:S(2)}) collective-permute-start(bf16[128,2176]{1,0:T(8,128)(2,1)S(1)} %collective-permute-done.9.refs_1_), channel_id=1, source_target_pairs={{0,2},{2,0},{4,6},{6,4},{8,10},{10,8},{12,14},{14,12},{16,18},{18,... | collective-permute-start | bytes 1671176 | tf_op jit(solution)/shard_map/ppermute | solution.py:139
  54.3 10.4 %copy-start.2 = (bf16[128,2048]{1,0:T(8,128)(2,1)S(1)}, bf16[128,2048]{1,0:T(8,128)(2,1)}, u32[]{:S(2)}) copy-start(bf16[128,2048]{1,0:T(8,128)(2,1)} %refs_0_.1) | copy-start | bytes 1572868
  54.3 8.6 %collective-permute-start.14 = (bf16[64,2176]{1,0:T(8,128)(2,1)S(1)}, bf16[64,2176]{1,0:T(8,128)(2,1)S(1)}, u32[]{:S(2)}, u32[]{:S(2)}) collective-permute-start(bf16[64,2176]{1,0:T(8,128)(2,1)S(1)} %slice.119), channel_id=1, source_target_pairs={{0,8},{2,10},{8,16},{10,18},{16,24},{18,26},{24,28},{26,30},{28,20... | collective-permute-start | bytes 835592 | tf_op jit(solution)/shard_map/ppermute | solution.py:139
  55.9 8.3 %collective-permute-start.15 = (bf16[64,2176]{1,0:T(8,128)(2,1)S(1)}, bf16[64,2176]{1,0:T(8,128)(2,1)S(1)}, u32[]{:S(2)}, u32[]{:S(2)}) collective-permute-start(bf16[64,2176]{1,0:T(8,128)(2,1)S(1)} %slice.120), channel_id=1, source_target_pairs={{8,0},{10,2},{16,8},{18,10},{24,16},{26,18},{28,24},{30,26},{20,28... | collective-permute-start | bytes 835592 | tf_op jit(solution)/shard_map/ppermute | solution.py:139
  64.2 14.4 %slice-start = ((s8[4718592]{0:T(1024)(128)(4,1)}), s8[4194304]{0:T(1024)(128)(4,1)S(1)}, s32[]{:S(2)}) async-start(s8[4718592]{0:T(1024)(128)(4,1)} %bitcast.35), calls=%async_computation | async-start | bytes 8388608
  64.2 14.4 %slice-start.1 = ((s8[4718592]{0:T(1024)(128)(4,1)}), s8[524288]{0:T(1024)(128)(4,1)S(1)}, s32[]{:S(2)}) async-start(s8[4718592]{0:T(1024)(128)(4,1)} %bitcast.35), calls=%async_computation.1 | async-start | bytes 1048576
  64.2 2.0 %collective-permute-start.19 = (bf16[64,2176]{1,0:T(8,128)(2,1)S(1)}, bf16[64,2176]{1,0:T(8,128)(2,1)S(1)}, u32[]{:S(2)}, u32[]{:S(2)}) collective-permute-start(bf16[64,2176]{1,0:T(8,128)(2,1)S(1)} %collective-permute-done.14.refs_0_), channel_id=1, source_target_pairs={{0,2},{2,0},{4,6},{6,4},{8,10},{10,8},{12,14},{14,12},{16,18},{18,... | collective-permute-start | bytes 835592 | tf_op jit(solution)/shard_map/ppermute | solution.py:139
  64.2 2.0 %collective-permute-start.20 = (bf16[64,2176]{1,0:T(8,128)(2,1)S(1)}, bf16[64,2176]{1,0:T(8,128)(2,1)S(1)}, u32[]{:S(2)}, u32[]{:S(2)}) collective-permute-start(bf16[64,2176]{1,0:T(8,128)(2,1)S(1)} %collective-permute-done.15.refs_1_), channel_id=1, source_target_pairs={{0,2},{2,0},{4,6},{6,4},{8,10},{10,8},{12,14},{14,12},{16,18},{18,... | collective-permute-start | bytes 835592 | tf_op jit(solution)/shard_map/ppermute | solution.py:139
  64.7 13.9 %collective-permute-start.30 = (bf16[128,2048]{1,0:T(8,128)(2,1)S(1)}, bf16[128,2048]{1,0:T(8,128)(2,1)S(1)}, u32[]{:S(2)}, u32[]{:S(2)}) collective-permute-start(bf16[128,2048]{1,0:T(8,128)(2,1)S(1)} %copy-done.2), channel_id=1, source_target_pairs={{0,1},{1,0},{2,3},{3,2},{4,5},{5,4},{6,7},{7,6},{8,9},{9,8},{10,11... | collective-permute-start | bytes 1572872 | tf_op jit(solution)/shard_map/ppermute | solution.py:16
  69.5 13.6 %collective-permute-start.21 = (bf16[128,2048]{1,0:T(8,128)(2,1)S(1)}, bf16[128,2048]{1,0:T(8,128)(2,1)S(1)}, u32[]{:S(2)}, u32[]{:S(2)}) collective-permute-start(bf16[128,2048]{1,0:T(8,128)(2,1)S(1)} %get-tuple-element.58), channel_id=1, source_target_pairs={{0,2},{2,0},{4,6},{6,4},{8,10},{10,8},{12,14},{14,12},{16,18},{18,... | collective-permute-start | bytes 1572872 | tf_op jit(solution)/shard_map/ppermute | solution.py:139
  69.6 14.3 %collective-permute-start.18 = (bf16[256,2048]{1,0:T(8,128)(2,1)S(1)}, bf16[256,2048]{1,0:T(8,128)(2,1)S(1)}, u32[]{:S(2)}, u32[]{:S(2)}) collective-permute-start(bf16[256,2048]{1,0:T(8,128)(2,1)S(1)} %get-tuple-element.54), channel_id=1, source_target_pairs={{0,2},{2,0},{4,6},{6,4},{8,10},{10,8},{12,14},{14,12},{16,18},{18,... | collective-permute-start | bytes 3145736 | tf_op jit(solution)/shard_map/ppermute | solution.py:139
  81.0 41.4 %collective-permute-start.31 = (bf16[128,2048]{1,0:T(8,128)(2,1)S(1)}, bf16[128,2048]{1,0:T(8,128)(2,1)S(1)}, u32[]{:S(2)}, u32[]{:S(2)}) collective-permute-start(bf16[128,2048]{1,0:T(8,128)(2,1)S(1)} %get-tuple-element.60), channel_id=1, source_target_pairs={{0,1},{1,0},{2,3},{3,2},{4,5},{5,4},{6,7},{7,6},{8,9},{9,8},{10,11... | collective-permute-start | bytes 1572872 | tf_op jit(solution)/shard_map/ppermute | solution.py:16
  82.6 39.8 %collective-permute-start.3 = (bf16[128,2048]{1,0:T(8,128)(2,1)S(1)}, bf16[128,2048]{1,0:T(8,128)(2,1)S(1)}, u32[]{:S(2)}, u32[]{:S(2)}) collective-permute-start(bf16[128,2048]{1,0:T(8,128)(2,1)S(1)} %get-tuple-element.36), channel_id=1, source_target_pairs={{0,2},{2,0},{4,6},{6,4},{8,10},{10,8},{12,14},{14,12},{16,18},{18,... | collective-permute-start | bytes 1572872 | tf_op jit(solution)/shard_map/ppermute | solution.py:139
  82.6 9.9 %collective-permute-start.13 = (bf16[256,2048]{1,0:T(8,128)(2,1)S(1)}, bf16[256,2048]{1,0:T(8,128)(2,1)S(1)}, u32[]{:S(2)}, u32[]{:S(2)}) collective-permute-start(bf16[256,2048]{1,0:T(8,128)(2,1)S(1)} %get-tuple-element.48), channel_id=1, source_target_pairs={{0,2},{2,0},{4,6},{6,4},{8,10},{10,8},{12,14},{14,12},{16,18},{18,... | collective-permute-start | bytes 3145736 | tf_op jit(solution)/shard_map/ppermute | solution.py:139
  83.3 8.3 %collective-permute-start.22 = (bf16[64,2048]{1,0:T(8,128)(2,1)S(1)}, bf16[64,2048]{1,0:T(8,128)(2,1)S(1)}, u32[]{:S(2)}, u32[]{:S(2)}) collective-permute-start(bf16[64,2048]{1,0:T(8,128)(2,1)S(1)} %get-tuple-element.71), channel_id=1, source_target_pairs={{0,8},{2,10},{8,16},{10,18},{16,24},{18,26},{24,28},{26,30},{28,20... | collective-permute-start | bytes 786440 | tf_op jit(solution)/shard_map/ppermute | solution.py:139
  83.9 7.9 %collective-permute-start.26 = (bf16[64,2048]{1,0:T(8,128)(2,1)S(1)}, bf16[64,2048]{1,0:T(8,128)(2,1)S(1)}, u32[]{:S(2)}, u32[]{:S(2)}) collective-permute-start(bf16[64,2048]{1,0:T(8,128)(2,1)S(1)} %get-tuple-element.72), channel_id=1, source_target_pairs={{8,0},{10,2},{16,8},{18,10},{24,16},{26,18},{28,24},{30,26},{20,28... | collective-permute-start | bytes 786440 | tf_op jit(solution)/shard_map/ppermute | solution.py:139
  91.6 17.3 %collective-permute-start.8 = (bf16[256,2048]{1,0:T(8,128)(2,1)S(1)}, bf16[256,2048]{1,0:T(8,128)(2,1)S(1)}, u32[]{:S(2)}, u32[]{:S(2)}) collective-permute-start(bf16[256,2048]{1,0:T(8,128)(2,1)S(1)} %get-tuple-element.42), channel_id=1, source_target_pairs={{0,2},{2,0},{4,6},{6,4},{8,10},{10,8},{12,14},{14,12},{16,18},{18,... | collective-permute-start | bytes 3145736 | tf_op jit(solution)/shard_map/ppermute | solution.py:139
  92.0 14.1 %collective-permute-start.23 = (bf16[128,2048]{1,0:T(8,128)(2,1)S(1)}, bf16[128,2048]{1,0:T(8,128)(2,1)S(1)}, u32[]{:S(2)}, u32[]{:S(2)}) collective-permute-start(bf16[128,2048]{1,0:T(8,128)(2,1)S(1)} %pad_maximum_fusion), channel_id=1, source_target_pairs={{0,8},{2,10},{8,16},{10,18},{16,24},{18,26},{24,28},{26,30},{28,20... | collective-permute-start | bytes 1572872 | tf_op jit(solution)/shard_map/ppermute | solution.py:139
  92.5 13.9 %collective-permute-start.27 = (bf16[128,2048]{1,0:T(8,128)(2,1)S(1)}, bf16[128,2048]{1,0:T(8,128)(2,1)S(1)}, u32[]{:S(2)}, u32[]{:S(2)}) collective-permute-start(bf16[128,2048]{1,0:T(8,128)(2,1)S(1)} %pad_maximum_fusion.1), channel_id=1, source_target_pairs={{8,0},{10,2},{16,8},{18,10},{24,16},{26,18},{28,24},{30,26},{20,28... | collective-permute-start | bytes 1572872 | tf_op jit(solution)/shard_map/ppermute | solution.py:139
  106.8 13.1 %collective-permute-start.24 = (bf16[128,2048]{1,0:T(8,128)(2,1)S(1)}, bf16[128,2048]{1,0:T(8,128)(2,1)S(1)}, u32[]{:S(2)}, u32[]{:S(2)}) collective-permute-start(bf16[128,2048]{1,0:T(8,128)(2,1)S(1)} %get-tuple-element.65), channel_id=1, source_target_pairs={{0,8},{2,10},{8,16},{10,18},{16,24},{18,26},{24,28},{26,30},{28,20... | collective-permute-start | bytes 1572872 | tf_op jit(solution)/shard_map/ppermute | solution.py:139
  107.3 12.8 %collective-permute-start.28 = (bf16[128,2048]{1,0:T(8,128)(2,1)S(1)}, bf16[128,2048]{1,0:T(8,128)(2,1)S(1)}, u32[]{:S(2)}, u32[]{:S(2)}) collective-permute-start(bf16[128,2048]{1,0:T(8,128)(2,1)S(1)} %get-tuple-element.66), channel_id=1, source_target_pairs={{8,0},{10,2},{16,8},{18,10},{24,16},{26,18},{28,24},{30,26},{20,28... | collective-permute-start | bytes 1572872 | tf_op jit(solution)/shard_map/ppermute | solution.py:139
  120.4 12.0 %collective-permute-start.29 = (bf16[128,2048]{1,0:T(8,128)(2,1)S(1)}, bf16[128,2048]{1,0:T(8,128)(2,1)S(1)}, u32[]{:S(2)}, u32[]{:S(2)}) collective-permute-start(bf16[128,2048]{1,0:T(8,128)(2,1)S(1)} %get-tuple-element.64), channel_id=1, source_target_pairs={{8,0},{10,2},{16,8},{18,10},{24,16},{26,18},{28,24},{30,26},{20,28... | collective-permute-start | bytes 1572872 | tf_op jit(solution)/shard_map/ppermute | solution.py:139
  122.0 11.6 %collective-permute-start.25 = (bf16[128,2048]{1,0:T(8,128)(2,1)S(1)}, bf16[128,2048]{1,0:T(8,128)(2,1)S(1)}, u32[]{:S(2)}, u32[]{:S(2)}) collective-permute-start(bf16[128,2048]{1,0:T(8,128)(2,1)S(1)} %get-tuple-element.63), channel_id=1, source_target_pairs={{0,8},{2,10},{8,16},{10,18},{16,24},{18,26},{24,28},{26,30},{28,20... | collective-permute-start | bytes 1572872 | tf_op jit(solution)/shard_map/ppermute | solution.py:139

commit v3 on v2

v3 whole, which is shorter than its diff:
```python
import functools

import jax
import jax.numpy as jnp
from jax import lax
from jax.experimental import pallas as pl
from jax.experimental.pallas import tpu as pltpu
from jax.sharding import PartitionSpec as P

LANES = 128
VMEM_BYTES = 12 * 1024 * 1024
NT = (((1,), (1,)), ((), ()))


def shifted(block, axis, by):
    size = lax.axis_size(axis)
    return lax.ppermute(block, axis, [(i, (i + by) % size) for i in range(size)])


def ring_pairs(count):
    chips = count // 2
    half = chips // 2

    def first_core(place):
        place %= chips
        return 4 * place if place < half else 4 * (chips - 1 - place) + 2

    onward = [
        (first_core(place) + core, first_core(place + 1) + core)
        for place in range(chips)
        for core in range(2)
    ]
    return onward, [(target, source) for source, target in onward]


def expert_kernel(parts, experts, features, kept_rows, tile, width, owners_ref, *refs):
    blocks, weights, (keep_ref, *send_ref), (inputs, scales, hidden) = (
        refs[:parts],
        refs[parts : parts + experts],
        refs[parts + experts : -3],
        refs[-3:],
    )
    row = 0
    for block in blocks:
        rows = block.shape[0]
        inputs[row : row + rows, :] = block[:, :features]
        if block.shape[1] > features:
            extra = block[:, features:].astype(jnp.float32)
            lane = lax.broadcasted_iota(jnp.int32, extra.shape, 1)
            count = owners_ref[experts]
            for expert in range(experts):
                owner = owners_ref[expert]
                mine = (lane == owner) | (lane == owner + count) | (lane == owner + 2 * count)
                scales[expert, row : row + rows, :] = jnp.sum(
                    jnp.where(mine, extra, 0.0), axis=1, keepdims=True
                )
        else:
            scales[0, row : row + rows, :] = jnp.ones((rows, 1), jnp.float32)
        row += rows

    units = hidden.shape[2]
    for expert in range(experts):
        for first in range(0, units, tile):
            some = slice(first, first + tile)
            values = inputs[...]
            gate = lax.dot_general(
                values, weights[expert][0, 0, some, :], NT, preferred_element_type=jnp.float32
            )
            up = lax.dot_general(
                values, weights[expert][0, 1, some, :], NT, preferred_element_type=jnp.float32
            )
            hidden[expert, :, some] = (gate / (1.0 + jnp.exp(-gate)) * up).astype(jnp.bfloat16)
    for first in range(0, features, width):
        some = slice(first, first + width)
        result = 0.0
        for expert in range(experts):
            output = jnp.dot(
                hidden[expert], weights[expert][0, 2, :, some], preferred_element_type=jnp.float32
            )
            result = result + output * scales[expert]
        keep_ref[:, some] = result[:kept_rows]
        if send_ref:
            send_ref[0][:, some] = result[kept_rows:].astype(jnp.bfloat16)


def expert_apply(blocks, weights, owners, features, kept_rows, tile=256, width=512):
    rows = sum(block.shape[0] for block in blocks)
    experts = len(weights)
    units = weights[0].shape[2]
    tile = tile if units % tile == 0 else units
    whole = pl.BlockSpec(memory_space=pltpu.VMEM)
    out_shape = [jax.ShapeDtypeStruct((kept_rows, features), jnp.float32)]
    if rows > kept_rows:
        out_shape.append(jax.ShapeDtypeStruct((rows - kept_rows, features), jnp.bfloat16))
    return pl.pallas_call(
        functools.partial(
            expert_kernel, len(blocks), experts, features, kept_rows, tile, width
        ),
        in_specs=[pl.BlockSpec(memory_space=pltpu.SMEM)] + [whole] * (len(blocks) + experts),
        out_specs=[whole] * len(out_shape),
        out_shape=out_shape,
        scratch_shapes=[
            pltpu.VMEM((rows, features), jnp.bfloat16),
            pltpu.VMEM((experts, rows, 1), jnp.float32),
            pltpu.VMEM((experts, rows, units), jnp.bfloat16),
        ],
        compiler_params=pltpu.CompilerParams(vmem_limit_bytes=VMEM_BYTES),
        cost_estimate=pl.CostEstimate(
            flops=6 * rows * units * features * experts,
            bytes_accessed=2 * 3 * units * features * experts + 8 * rows * features,
            transcendentals=rows * units * experts,
        ),
    )(owners, *blocks, *weights)


def stage_kernel(source_ref, target_ref, semaphore):
    copy = pltpu.make_async_copy(source_ref, target_ref, semaphore)
    copy.start()
    copy.wait()


def stage(weights):
    return pl.pallas_call(
        stage_kernel,
        in_specs=[pl.BlockSpec(memory_space=pl.ANY)],
        out_specs=pl.BlockSpec(memory_space=pltpu.VMEM),
        out_shape=jax.ShapeDtypeStruct(weights.shape, weights.dtype),
        scratch_shapes=[pltpu.SemaphoreType.DMA(())],
        compiler_params=pltpu.CompilerParams(vmem_limit_bytes=VMEM_BYTES),
    )(weights)


def on_device(tokens, expert_ids, gate_weights, hot_weights, cold_weights):
    rows, features = tokens.shape
    count = lax.axis_size("dp")
    groups = lax.axis_size("expert")
    experts = 1 + count
    onward, backward = ring_pairs(count)
    across = [(i, i ^ 1) for i in range(count)]
    reach = count // 4
    place = lax.axis_index("dp")
    owners = jnp.stack([place, place ^ 1, count]).astype(jnp.int32)

    labels = jnp.arange(experts, dtype=jnp.int32)[None, :]
    table = jnp.zeros((rows, experts), jnp.float32)
    for k in range(expert_ids.shape[1]):
        table = table + jnp.where(
            expert_ids[:, k : k + 1] == labels, gate_weights[:, k : k + 1], 0.0
        )
    cold_table = table[:, 1:]
    high = lax.reduce_precision(cold_table, 8, 7)
    rest = cold_table - high
    middle = lax.reduce_precision(rest, 8, 7)
    low = rest - middle
    extra = -(3 * count) % LANES
    payload = jnp.concatenate(
        [
            tokens,
            jnp.pad(
                jnp.concatenate([high, middle, low], axis=1).astype(jnp.bfloat16),
                ((0, 0), (0, extra)),
            ),
        ],
        axis=1,
    )

    def go(block, pairs):
        return lax.ppermute(block, "dp", pairs)

    def hold(*values):
        return lax.optimization_barrier(values)

    half = rows // 2
    top, bottom = payload[:half], payload[half:]
    ways = (backward, onward)

    def move(blocks):
        return [go(block, way) for block, way in zip(blocks, ways)]

    short = move([top, bottom])
    long = move([bottom, top])
    mine, other = hold(stage(cold_weights), go(cold_weights, across))
    pair = [mine, stage(other)]

    def serve(blocks):
        kept = sum(block.shape[0] for block in blocks)
        return expert_apply(blocks, pair, owners, features, kept)[0]

    sums = {}
    for k in range(1, reach - 1):
        here, there = short, long
        short, long = move(short), move(long)
        both = serve(here + there)
        *short, both = hold(*short, both)
        sums["short", k], sums["long", k] = both[:rows], both[rows:]
    last = reach - 1
    both = serve(short)
    *long, both = hold(*long, both)
    sums["short", last] = both
    here, long = long, move(long)
    both = serve(here)
    *long, both = hold(*long, both)
    sums["long", last] = both
    sums["long", reach] = serve(long)

    def move_on(values):
        return [go(value.astype(jnp.bfloat16), way) for value, way in zip(values, (onward, backward))]

    def grow(moving, mine):
        return move_on([mine[:half] + moving[0], mine[half:] + moving[1]])

    short = move_on([sums["short", last][:half], sums["short", last][half:]])
    long = move_on([sums["long", reach][:half], sums["long", reach][half:]])
    for k in range(last, 0, -1):
        if k > 1:
            short = grow(short, sums["short", k - 1])
        long = grow(long, sums["long", k])

    worked, own_block, own_tokens = hold(sums["long", reach], payload, tokens)
    hot_blocks = [own_tokens] + [shifted(own_tokens, "expert", by) for by in range(1, groups)]
    hot, hot_send = expert_apply(
        hot_blocks, [hot_weights], owners[1:], features, rows, tile=384
    )
    for by in range(1, groups):
        hot = hot + shifted(hot_send[(by - 1) * rows : by * rows], "expert", -by)
    (base,) = hold(serve([own_block]) + table[:, :1] * hot)
    combined = [
        base[:half] + short[0].astype(jnp.float32) + long[1].astype(jnp.float32),
        base[half:] + short[1].astype(jnp.float32) + long[0].astype(jnp.float32),
    ]
    return jnp.concatenate(combined, axis=0).astype(jnp.bfloat16)


def solution(mesh):
    placed = (
        P(("dp", "expert"), None),
        P(("dp", "expert"), None),
        P(("dp", "expert"), None),
        P(None, None, "expert", None),
        P("dp", None, None, None),
    )
    return jax.shard_map(
        on_device, mesh=mesh, in_specs=placed, out_specs=P(("dp", "expert"), None), check_vma=False
    )
```

time: 135 us -> 116 us (0.86)
  waiting for transfers between devices: 74.2 us -> 25.6 us
  Pallas kernels: 26.1 us -> 41.5 us
  starting transfers between devices: 23.9 us -> 33.1 us
  local copies, waits for them, and re-layouts: 5.92 us -> 12.1 us
    ppermute x30 -> x29, waiting for transfers between devices: 65.7 us -> 25.6 us  [go(): return lax.ppermute(block, 'dp', pairs)]
    pallas_call x6 -> x9, Pallas kernels: 26.1 us -> 41.5 us  [the longest x7 37 us: expert_apply(): pl.pallas_call(functools.partial(expert_kernel, len(blocks), experts, fea...]
    ppermute x30 -> x29, starting transfers between devices: 20.8 us -> 30 us  [go(): return lax.ppermute(block, 'dp', pairs)]
    ppermute x2, waiting for transfers between devices: 8.51 us -> 0.01 us  [shifted(): lax.ppermute(block, axis, [(i, (i + by) % size) for i in range(size)])]
    unnamed x10 -> x12, local copies, waits for them, and re-layouts: 3.7 us -> 9.87 us
  transfers between devices with their start and end apart: 32 -> 31, of which waited for: 20 -> 12; matrix products, arithmetic and copies ran while one was open for 2% -> 4% of each run, Pallas kernels for 19% -> 31%
where the time goes in v3:
time: 116 us
  Pallas kernels  41.5 us (36%)
  starting transfers between devices  33.1 us (29%)
  waiting for transfers between devices  25.6 us (22%)
  local copies, waits for them, and re-layouts  12.1 us (10%)
  other arithmetic  3.39 us (3%)
    pallas_call x7, Pallas kernels, expert_apply(): pl.pallas_call(functools.partial(expert_kernel, len(blocks), experts, fea...  37 us
    ppermute x29, starting transfers between devices, go(): return lax.ppermute(block, 'dp', pairs)  30 us
    ppermute x29, waiting for transfers between devices, go(): return lax.ppermute(block, 'dp', pairs)  25.6 us
    unnamed x12, local copies, waits for them, and re-layouts  9.87 us
    pallas_call x2, Pallas kernels, stage(): pl.pallas_call(stage_kernel, in_specs=[pl.BlockSpec(memory_space=pl.ANY)]...  4.47 us
    ppermute x2, starting transfers between devices, shifted(): lax.ppermute(block, axis, [(i, (i + by) % size) for i in range(size)])  3.1 us
  transfers between devices with their start and end apart: 31, of which 12 were waited for; matrix products, arithmetic and copies ran while one was open for 4% of the time, Pallas kernels for 31%

profile of v3, /device:TPU:0, one launch (start us, length us, event | category | flops | bytes accessed | tf_op | source)
XLA Modules:
  0.0 115.9 jit_solution(3788110428378410926)
XLA Ops:
  0.0 0.5 collective-permute-start.10
  0.5 1.0 slice_bitcast_fusion.16
  1.4 1.0 slice_bitcast_fusion.15
  2.5 0.1 copy.6
  2.6 1.1 fusion.1.refs_0_
  3.7 2.5 %collective-permute-start = (bf16[64,2176]{1,0:T(8,128)(2,1)S(1)}, bf16[64,2176]{1,0:T(8,128)(2,1)S(1)}, u32[]{:S(2)}, u32[]{:S(2)}) collective-permute-start(bf16[64,2176]{1,0:T(8,128)(2,1)S(1)} %get-tuple-element.54), channel_id=1, source_target_pairs={{8,0},{10,2},{16,8},{18,10},{24,16},{26,18},{28,24},{30,26},{20,28... | collective-permute-start | bytes 835592 | tf_op jit(solution)/shard_map/ppermute | solution.py:168
  6.3 0.2 collective-permute-start.3
  6.4 1.9 %collective-permute-start.6 = (bf16[64,2176]{1,0:T(8,128)(2,1)S(1)}, bf16[64,2176]{1,0:T(8,128)(2,1)S(1)}, u32[]{:S(2)}, u32[]{:S(2)}) collective-permute-start(bf16[64,2176]{1,0:T(8,128)(2,1)S(1)} %get-tuple-element.53), channel_id=1, source_target_pairs={{8,0},{10,2},{16,8},{18,10},{24,16},{26,18},{28,24},{30,26},{20,28... | collective-permute-start | bytes 835592 | tf_op jit(solution)/shard_map/ppermute | solution.py:168
  8.3 0.2 collective-permute-start.8
  8.5 5.4 %collective-permute-done.refs_2_ = bf16[64,2176]{1,0:T(8,128)(2,1)S(1)} collective-permute-done((bf16[64,2176]{1,0:T(8,128)(2,1)S(1)}, bf16[64,2176]{1,0:T(8,128)(2,1)S(1)}, u32[]{:S(2)}, u32[]{:S(2)}) %collective-permute-start) | collective-permute-done | bytes 278560 | tf_op jit(solution)/shard_map/ppermute | solution.py:168
  13.9 1.9 %collective-permute-start.1 = (bf16[64,2176]{1,0:T(8,128)(2,1)S(1)}, bf16[64,2176]{1,0:T(8,128)(2,1)S(1)}, u32[]{:S(2)}, u32[]{:S(2)}) collective-permute-start(bf16[64,2176]{1,0:T(8,128)(2,1)S(1)} %collective-permute-done.refs_2_), channel_id=1, source_target_pairs={{8,0},{10,2},{16,8},{18,10},{24,16},{26,18},{28,24},{30,26},{20,28... | collective-permute-start | bytes 835592 | tf_op jit(solution)/shard_map/ppermute | solution.py:168
  15.8 0.1 collective-permute-start.4
  15.9 3.7 %copy-done.2 = bf16[1,3,768,2048]{3,2,1,0:T(8,128)(2,1)S(1)} copy-done((bf16[1,3,768,2048]{3,2,1,0:T(8,128)(2,1)S(1)}, bf16[1,3,768,2048]{3,2,1,0:T(8,128)(2,1)}, u32[]{:S(2)}) %copy-start.2) | copy-done | bytes 9437208
  19.6 0.6 shard_map.55.refs_4_.refs_2_.refs_1_
  20.2 3.6 %copy-done = bf16[1,3,768,2048]{3,2,1,0:T(8,128)(2,1)} copy-done((bf16[1,3,768,2048]{3,2,1,0:T(8,128)(2,1)}, bf16[1,3,768,2048]{3,2,1,0:T(8,128)(2,1)S(1)}, u32[]{:S(2)}) %copy-start) | copy-done | bytes 9437208
  23.9 0.1 pad_add_fusion.owners_ref
  24.0 1.9 %collective-permute-start.7 = (bf16[64,2176]{1,0:T(8,128)(2,1)S(1)}, bf16[64,2176]{1,0:T(8,128)(2,1)S(1)}, u32[]{:S(2)}, u32[]{:S(2)}) collective-permute-start(bf16[64,2176]{1,0:T(8,128)(2,1)S(1)} %collective-permute-done.6.refs_0_), channel_id=1, source_target_pairs={{8,0},{10,2},{16,8},{18,10},{24,16},{26,18},{28,24},{30,26},{20,28... | collective-permute-start | bytes 835592 | tf_op jit(solution)/shard_map/ppermute | solution.py:168
  25.9 0.2 collective-permute-start.9
  26.0 1.9 %collective-permute-start.2 = (bf16[64,2176]{1,0:T(8,128)(2,1)S(1)}, bf16[64,2176]{1,0:T(8,128)(2,1)S(1)}, u32[]{:S(2)}, u32[]{:S(2)}) collective-permute-start(bf16[64,2176]{1,0:T(8,128)(2,1)S(1)} %collective-permute-done.1.refs_2_), channel_id=1, source_target_pairs={{8,0},{10,2},{16,8},{18,10},{24,16},{26,18},{28,24},{30,26},{20,28... | collective-permute-start | bytes 835592 | tf_op jit(solution)/shard_map/ppermute | solution.py:168
  27.9 0.2 collective-permute-start.5
  28.0 3.8 %shard_map.56.refs_5_.refs_3_.refs_2_ = bf16[1,3,768,2048]{3,2,1,0:T(8,128)(2,1)S(1)} custom-call(bf16[1,3,768,2048]{3,2,1,0:T(8,128)(2,1)} %collective-permute-done.10.source_ref), custom_call_target="tpu_custom_call" | custom-call | tf_op jit(solution)/shard_map/pallas_call | solution.py:123
  31.9 2.5 %copy-done.1 = bf16[1,3,768,2048]{3,2,1,0:T(8,128)(2,1)S(1)} copy-done((bf16[1,3,768,2048]{3,2,1,0:T(8,128)(2,1)S(1)}, bf16[1,3,768,2048]{3,2,1,0:T(8,128)(2,1)}, u32[]{:S(2)}) %copy-start.1) | copy-done | bytes 9437208
  34.4 5.8 %shard_map.57 = f32[256,2048]{1,0:T(8,128)S(1)} custom-call(s32[3]{0:T(128)S(1)} %pad_add_fusion.owners_ref, bf16[64,2176]{1,0:T(8,128)(2,1)S(1)} %collective-permute-done.6.refs_0_, bf16[64,2176]{1,0:T(8,128)(2,1)S(1)} %collective-permute-done.8.refs_1_, bf16[64,2176]{1,0:T(8,128)(2,1)S(1)} %collective-permute-done.refs_2_, ...), custom_call_target="tpu_custom_call" | custom-call | flops 4831838208 | bytes 23068672 | tf_op jit(solution)/shard_map/pallas_call | solution.py:95
  40.3 1.9 %collective-permute-start.11 = (bf16[64,2176]{1,0:T(8,128)(2,1)S(1)}, bf16[64,2176]{1,0:T(8,128)(2,1)S(1)}, u32[]{:S(2)}, u32[]{:S(2)}) collective-permute-start(bf16[64,2176]{1,0:T(8,128)(2,1)S(1)} %collective-permute-done.7.refs_0_), channel_id=1, source_target_pairs={{8,0},{10,2},{16,8},{18,10},{24,16},{26,18},{28,24},{30,26},{20,28... | collective-permute-start | bytes 835592 | tf_op jit(solution)/shard_map/ppermute | solution.py:168
  42.2 0.3 collective-permute-start.12
  42.5 5.8 %shard_map.58 = f32[256,2048]{1,0:T(8,128)S(1)} custom-call(s32[3]{0:T(128)S(1)} %pad_add_fusion.owners_ref, bf16[64,2176]{1,0:T(8,128)(2,1)S(1)} %collective-permute-done.7.refs_0_, bf16[64,2176]{1,0:T(8,128)(2,1)S(1)} %collective-permute-done.9.refs_1_, bf16[64,2176]{1,0:T(8,128)(2,1)S(1)} %collective-permute-done.1.refs_2_, ...), custom_call_target="tpu_custom_call" | custom-call | flops 4831838208 | bytes 23068672 | tf_op jit(solution)/shard_map/pallas_call | solution.py:95
  48.4 0.7 collective-permute-done.12.refs_1_
  49.0 5.7 %shard_map.59 = f32[128,2048]{1,0:T(8,128)S(1)} custom-call(s32[3]{0:T(128)S(1)} %pad_add_fusion.owners_ref, bf16[64,2176]{1,0:T(8,128)(2,1)S(1)} %collective-permute-done.11.refs_0_, bf16[64,2176]{1,0:T(8,128)(2,1)S(1)} %collective-permute-done.12.refs_1_, bf16[1,3,768,2048]{3,2,1,0:T(8,128)(2,1)S(1)} %copy-done.1, ...), custom_call_target="tpu_custom_call" | custom-call | flops 2415919104 | bytes 20971520 | tf_op jit(solution)/shard_map/pallas_call | solution.py:95
  54.8 1.6 %collective-permute-start.13 = (bf16[64,2176]{1,0:T(8,128)(2,1)S(1)}, bf16[64,2176]{1,0:T(8,128)(2,1)S(1)}, u32[]{:S(2)}, u32[]{:S(2)}) collective-permute-start(bf16[64,2176]{1,0:T(8,128)(2,1)S(1)} %collective-permute-done.2.refs_0_), channel_id=1, source_target_pairs={{8,0},{10,2},{16,8},{18,10},{24,16},{26,18},{28,24},{30,26},{20,28... | collective-permute-start | bytes 835592 | tf_op jit(solution)/shard_map/ppermute | solution.py:168
  56.4 0.4 collective-permute-start.14
  57.0 5.7 %shard_map.60 = f32[128,2048]{1,0:T(8,128)S(1)} custom-call(s32[3]{0:T(128)S(1)} %pad_add_fusion.owners_ref, bf16[64,2176]{1,0:T(8,128)(2,1)S(1)} %collective-permute-done.2.refs_0_, bf16[64,2176]{1,0:T(8,128)(2,1)S(1)} %collective-permute-done.5.refs_1_, bf16[1,3,768,2048]{3,2,1,0:T(8,128)(2,1)S(1)} %copy-done.1, ...), custom_call_target="tpu_custom_call" | custom-call | flops 2415919104 | bytes 20971520 | tf_op jit(solution)/shard_map/pallas_call | solution.py:95
  62.7 0.3 collective-permute-done.14.refs_1_
  63.0 5.7 %shard_map.61 = f32[128,2048]{1,0:T(8,128)S(1)} custom-call(s32[3]{0:T(128)S(1)} %pad_add_fusion.owners_ref, bf16[64,2176]{1,0:T(8,128)(2,1)S(1)} %collective-permute-done.13.refs_0_, bf16[64,2176]{1,0:T(8,128)(2,1)S(1)} %collective-permute-done.14.refs_1_, bf16[1,3,768,2048]{3,2,1,0:T(8,128)(2,1)S(1)} %copy-done.1, ...), custom_call_target="tpu_custom_call" | custom-call | flops 2415919104 | bytes 20971520 | tf_op jit(solution)/shard_map/pallas_call | solution.py:95
  68.8 1.6 %collective-permute-start.20 = (bf16[64,2048]{1,0:T(8,128)(2,1)S(1)}, bf16[64,2048]{1,0:T(8,128)(2,1)S(1)}, u32[]{:S(2)}, u32[]{:S(2)}) collective-permute-start(bf16[64,2048]{1,0:T(8,128)(2,1)S(1)} %get-tuple-element.57), channel_id=1, source_target_pairs={{8,0},{10,2},{16,8},{18,10},{24,16},{26,18},{28,24},{30,26},{20,28... | collective-permute-start | bytes 786440 | tf_op jit(solution)/shard_map/ppermute | solution.py:168
  70.5 0.4 collective-permute-start.27
  71.0 0.9 collective-permute-start.17
  71.9 1.1 collective-permute-start.24
  73.0 5.1 %collective-permute-done.20 = bf16[64,2048]{1,0:T(8,128)(2,1)S(1)} collective-permute-done((bf16[64,2048]{1,0:T(8,128)(2,1)S(1)}, bf16[64,2048]{1,0:T(8,128)(2,1)S(1)}, u32[]{:S(2)}, u32[]{:S(2)}) %collective-permute-start.20) | collective-permute-done | bytes 262176 | tf_op jit(solution)/shard_map/ppermute | solution.py:168
  78.1 1.4 %collective-permute-done.27 = bf16[64,2048]{1,0:T(8,128)(2,1)S(1)} collective-permute-done((bf16[64,2048]{1,0:T(8,128)(2,1)S(1)}, bf16[64,2048]{1,0:T(8,128)(2,1)S(1)}, u32[]{:S(2)}, u32[]{:S(2)}) %collective-permute-start.27) | collective-permute-done | bytes 262176 | tf_op jit(solution)/shard_map/ppermute | solution.py:168
  79.5 0.1 add_convert_fusion.7
  79.7 1.6 %collective-permute-start.21 = (bf16[64,2048]{1,0:T(8,128)(2,1)S(1)}, bf16[64,2048]{1,0:T(8,128)(2,1)S(1)}, u32[]{:S(2)}, u32[]{:S(2)}) collective-permute-start(bf16[64,2048]{1,0:T(8,128)(2,1)S(1)} %get-tuple-element.51), channel_id=1, source_target_pairs={{8,0},{10,2},{16,8},{18,10},{24,16},{26,18},{28,24},{30,26},{20,28... | collective-permute-start | bytes 786440 | tf_op jit(solution)/shard_map/ppermute | solution.py:168
  81.3 0.4 collective-permute-start.28
  81.7 1.5 %collective-permute-start.15 = (bf16[128,2048]{1,0:T(8,128)(2,1)S(1)}, bf16[128,2048]{1,0:T(8,128)(2,1)S(1)}, u32[]{:S(2)}, u32[]{:S(2)}) collective-permute-start(bf16[128,2048]{1,0:T(8,128)(2,1)S(1)} %copy-done.3), channel_id=1, source_target_pairs={{0,1},{1,0},{2,3},{3,2},{4,5},{5,4},{6,7},{7,6},{8,9},{9,8},{10,11... | collective-permute-start | bytes 1572872 | tf_op jit(solution)/shard_map/ppermute | solution.py:17
  83.3 0.2 collective-permute-done.17
  83.5 2.6 %collective-permute-done.21 = bf16[64,2048]{1,0:T(8,128)(2,1)S(1)} collective-permute-done((bf16[64,2048]{1,0:T(8,128)(2,1)S(1)}, bf16[64,2048]{1,0:T(8,128)(2,1)S(1)}, u32[]{:S(2)}, u32[]{:S(2)}) %collective-permute-start.21) | collective-permute-done | bytes 262176 | tf_op jit(solution)/shard_map/ppermute | solution.py:168
  86.1 4.3 %collective-permute-done.28 = bf16[64,2048]{1,0:T(8,128)(2,1)S(1)} collective-permute-done((bf16[64,2048]{1,0:T(8,128)(2,1)S(1)}, bf16[64,2048]{1,0:T(8,128)(2,1)S(1)}, u32[]{:S(2)}, u32[]{:S(2)}) %collective-permute-start.28) | collective-permute-done | bytes 262176 | tf_op jit(solution)/shard_map/ppermute | solution.py:168
  90.4 0.3 add_convert_fusion.9
  90.8 2.0 %collective-permute-start.22 = (bf16[64,2048]{1,0:T(8,128)(2,1)S(1)}, bf16[64,2048]{1,0:T(8,128)(2,1)S(1)}, u32[]{:S(2)}, u32[]{:S(2)}) collective-permute-start(bf16[64,2048]{1,0:T(8,128)(2,1)S(1)} %get-tuple-element.48), channel_id=1, source_target_pairs={{8,0},{10,2},{16,8},{18,10},{24,16},{26,18},{28,24},{30,26},{20,28... | collective-permute-start | bytes 786440 | tf_op jit(solution)/shard_map/ppermute | solution.py:168
  92.8 1.5 %collective-permute-start.25 = (bf16[64,2048]{1,0:T(8,128)(2,1)S(1)}, bf16[64,2048]{1,0:T(8,128)(2,1)S(1)}, u32[]{:S(2)}, u32[]{:S(2)}) collective-permute-start(bf16[64,2048]{1,0:T(8,128)(2,1)S(1)} %get-tuple-element.47), channel_id=1, source_target_pairs={{8,0},{10,2},{16,8},{18,10},{24,16},{26,18},{28,24},{30,26},{20,28... | collective-permute-start | bytes 786440 | tf_op jit(solution)/shard_map/ppermute | solution.py:168
  94.3 0.5 collective-permute-start.29
  94.9 2.4 %shard_map.63 = (f32[128,2048]{1,0:T(8,128)S(1)}, bf16[128,2048]{1,0:T(8,128)(2,1)S(1)}) custom-call(s32[2]{0:T(128)S(1)} %pad_add_fusion.1.owners_ref, bf16[128,2048]{1,0:T(8,128)(2,1)S(1)} %copy-done.3, bf16[128,2048]{1,0:T(8,128)(2,1)S(1)} %collective-permute-done.15.refs_1_, bf16[1,3,384,2048]{3,2,1,0:T(8,128)(2,1)S(1)} %bitcast.37), custom_call_target="tpu_custom_call" | custom-call | flops 1207959552 | bytes 8912896 | tf_op jit(solution)/shard_map/pallas_call | solution.py:95
  97.3 1.6 %collective-permute-start.16 = (bf16[128,2048]{1,0:T(8,128)(2,1)S(1)}, bf16[128,2048]{1,0:T(8,128)(2,1)S(1)}, u32[]{:S(2)}, u32[]{:S(2)}) collective-permute-start(bf16[128,2048]{1,0:T(8,128)(2,1)S(1)} %get-tuple-element.36), channel_id=1, source_target_pairs={{0,1},{1,0},{2,3},{3,2},{4,5},{5,4},{6,7},{7,6},{8,9},{9,8},{10,11... | collective-permute-start | bytes 1572872 | tf_op jit(solution)/shard_map/ppermute | solution.py:17
  98.9 5.7 %shard_map.62 = f32[128,2048]{1,0:T(8,128)S(1)} custom-call(s32[3]{0:T(128)S(1)} %pad_add_fusion.owners_ref, bf16[128,2176]{1,0:T(8,128)(2,1)S(1)} %fusion.1.refs_0_, bf16[1,3,768,2048]{3,2,1,0:T(8,128)(2,1)S(1)} %copy-done.1, bf16[1,3,768,2048]{3,2,1,0:T(8,128)(2,1)S(1)} %shard_map.56.refs_5_.refs_3_.refs_2_), custom_call_target="tpu_custom_call" | custom-call | flops 2415919104 | bytes 20971520 | tf_op jit(solution)/shard_map/pallas_call | solution.py:95
  104.7 0.3 add_convert_fusion.8
  105.0 0.1 collective-permute-start.19
  105.1 2.0 %collective-permute-start.23 = (bf16[64,2048]{1,0:T(8,128)(2,1)S(1)}, bf16[64,2048]{1,0:T(8,128)(2,1)S(1)}, u32[]{:S(2)}, u32[]{:S(2)}) collective-permute-start(bf16[64,2048]{1,0:T(8,128)(2,1)S(1)} %get-tuple-element.44), channel_id=1, source_target_pairs={{8,0},{10,2},{16,8},{18,10},{24,16},{26,18},{28,24},{30,26},{20,28... | collective-permute-start | bytes 786440 | tf_op jit(solution)/shard_map/ppermute | solution.py:168
  107.0 1.5 %collective-permute-start.26 = (bf16[64,2048]{1,0:T(8,128)(2,1)S(1)}, bf16[64,2048]{1,0:T(8,128)(2,1)S(1)}, u32[]{:S(2)}, u32[]{:S(2)}) collective-permute-start(bf16[64,2048]{1,0:T(8,128)(2,1)S(1)} %get-tuple-element.43), channel_id=1, source_target_pairs={{8,0},{10,2},{16,8},{18,10},{24,16},{26,18},{28,24},{30,26},{20,28... | collective-permute-start | bytes 786440 | tf_op jit(solution)/shard_map/ppermute | solution.py:168
  108.5 0.5 collective-permute-start.30
  109.1 0.2 multiply_add_fusion
  109.3 2.1 %collective-permute-done.19 = bf16[64,2048]{1,0:T(8,128)(2,1)S(1)} collective-permute-done((bf16[64,2048]{1,0:T(8,128)(2,1)S(1)}, bf16[64,2048]{1,0:T(8,128)(2,1)S(1)}, u32[]{:S(2)}, u32[]{:S(2)}) %collective-permute-start.19) | collective-permute-done | bytes 262176 | tf_op jit(solution)/shard_map/ppermute | solution.py:168
  111.5 2.8 %collective-permute-done.26 = bf16[64,2048]{1,0:T(8,128)(2,1)S(1)} collective-permute-done((bf16[64,2048]{1,0:T(8,128)(2,1)S(1)}, bf16[64,2048]{1,0:T(8,128)(2,1)S(1)}, u32[]{:S(2)}, u32[]{:S(2)}) %collective-permute-start.26) | collective-permute-done | bytes 262176 | tf_op jit(solution)/shard_map/ppermute | solution.py:168
  114.3 0.6 collective-permute-done.30
  114.9 0.2 fusion.5
  115.1 0.8 pad_maximum_fusion
  (41 shorter events, 0.6 us)
Async XLA Ops:
  0.0 28.0 %collective-permute-start.10 = (bf16[1,3,768,2048]{3,2,1,0:T(8,128)(2,1)}, bf16[1,3,768,2048]{3,2,1,0:T(8,128)(2,1)}, u32[]{:S(2)}, u32[]{:S(2)}) collective-permute-start(bf16[1,3,768,2048]{3,2,1,0:T(8,128)(2,1)} %source_ref.1), channel_id=1, source_target_pairs={{0,2},{2,0},{4,6},{6,4},{8,10},{10,8},{12,14},{14,12},{16,18},{18,... | collective-permute-start | bytes 28311560 | tf_op jit(solution)/shard_map/ppermute | solution.py:168
  3.7 10.1 %collective-permute-start = (bf16[64,2176]{1,0:T(8,128)(2,1)S(1)}, bf16[64,2176]{1,0:T(8,128)(2,1)S(1)}, u32[]{:S(2)}, u32[]{:S(2)}) collective-permute-start(bf16[64,2176]{1,0:T(8,128)(2,1)S(1)} %get-tuple-element.54), channel_id=1, source_target_pairs={{8,0},{10,2},{16,8},{18,10},{24,16},{26,18},{28,24},{30,26},{20,28... | collective-permute-start | bytes 835592 | tf_op jit(solution)/shard_map/ppermute | solution.py:168
  6.3 9.5 %collective-permute-start.3 = (bf16[64,2176]{1,0:T(8,128)(2,1)S(1)}, bf16[64,2176]{1,0:T(8,128)(2,1)S(1)}, u32[]{:S(2)}, u32[]{:S(2)}) collective-permute-start(bf16[64,2176]{1,0:T(8,128)(2,1)S(1)} %get-tuple-element.53), channel_id=1, source_target_pairs={{0,8},{2,10},{8,16},{10,18},{16,24},{18,26},{24,28},{26,30},{28,20... | collective-permute-start | bytes 835592 | tf_op jit(solution)/shard_map/ppermute | solution.py:168
  6.4 17.5 %collective-permute-start.6 = (bf16[64,2176]{1,0:T(8,128)(2,1)S(1)}, bf16[64,2176]{1,0:T(8,128)(2,1)S(1)}, u32[]{:S(2)}, u32[]{:S(2)}) collective-permute-start(bf16[64,2176]{1,0:T(8,128)(2,1)S(1)} %get-tuple-element.53), channel_id=1, source_target_pairs={{8,0},{10,2},{16,8},{18,10},{24,16},{26,18},{28,24},{30,26},{20,28... | collective-permute-start | bytes 835592 | tf_op jit(solution)/shard_map/ppermute | solution.py:168
  8.3 17.6 %collective-permute-start.8 = (bf16[64,2176]{1,0:T(8,128)(2,1)S(1)}, bf16[64,2176]{1,0:T(8,128)(2,1)S(1)}, u32[]{:S(2)}, u32[]{:S(2)}) collective-permute-start(bf16[64,2176]{1,0:T(8,128)(2,1)S(1)} %get-tuple-element.54), channel_id=1, source_target_pairs={{0,8},{2,10},{8,16},{10,18},{16,24},{18,26},{24,28},{26,30},{28,20... | collective-permute-start | bytes 835592 | tf_op jit(solution)/shard_map/ppermute | solution.py:168
  13.9 12.1 %collective-permute-start.1 = (bf16[64,2176]{1,0:T(8,128)(2,1)S(1)}, bf16[64,2176]{1,0:T(8,128)(2,1)S(1)}, u32[]{:S(2)}, u32[]{:S(2)}) collective-permute-start(bf16[64,2176]{1,0:T(8,128)(2,1)S(1)} %collective-permute-done.refs_2_), channel_id=1, source_target_pairs={{8,0},{10,2},{16,8},{18,10},{24,16},{26,18},{28,24},{30,26},{20,28... | collective-permute-start | bytes 835592 | tf_op jit(solution)/shard_map/ppermute | solution.py:168
  15.8 12.1 %collective-permute-start.4 = (bf16[64,2176]{1,0:T(8,128)(2,1)S(1)}, bf16[64,2176]{1,0:T(8,128)(2,1)S(1)}, u32[]{:S(2)}, u32[]{:S(2)}) collective-permute-start(bf16[64,2176]{1,0:T(8,128)(2,1)S(1)} %collective-permute-done.3.refs_3_), channel_id=1, source_target_pairs={{0,8},{2,10},{8,16},{10,18},{16,24},{18,26},{24,28},{26,30},{28,20... | collective-permute-start | bytes 835592 | tf_op jit(solution)/shard_map/ppermute | solution.py:168
  15.9 3.7 %copy-start.2 = (bf16[1,3,768,2048]{3,2,1,0:T(8,128)(2,1)S(1)}, bf16[1,3,768,2048]{3,2,1,0:T(8,128)(2,1)}, u32[]{:S(2)}) copy-start(bf16[1,3,768,2048]{3,2,1,0:T(8,128)(2,1)} %source_ref.1) | copy-start | bytes 28311556
  20.2 3.7 %copy-start = (bf16[1,3,768,2048]{3,2,1,0:T(8,128)(2,1)}, bf16[1,3,768,2048]{3,2,1,0:T(8,128)(2,1)S(1)}, u32[]{:S(2)}) copy-start(bf16[1,3,768,2048]{3,2,1,0:T(8,128)(2,1)S(1)} %shard_map.55.refs_4_.refs_2_.refs_1_) | copy-start | bytes 28311556
  24.0 16.3 %collective-permute-start.7 = (bf16[64,2176]{1,0:T(8,128)(2,1)S(1)}, bf16[64,2176]{1,0:T(8,128)(2,1)S(1)}, u32[]{:S(2)}, u32[]{:S(2)}) collective-permute-start(bf16[64,2176]{1,0:T(8,128)(2,1)S(1)} %collective-permute-done.6.refs_0_), channel_id=1, source_target_pairs={{8,0},{10,2},{16,8},{18,10},{24,16},{26,18},{28,24},{30,26},{20,28... | collective-permute-start | bytes 835592 | tf_op jit(solution)/shard_map/ppermute | solution.py:168
  25.9 14.4 %collective-permute-start.9 = (bf16[64,2176]{1,0:T(8,128)(2,1)S(1)}, bf16[64,2176]{1,0:T(8,128)(2,1)S(1)}, u32[]{:S(2)}, u32[]{:S(2)}) collective-permute-start(bf16[64,2176]{1,0:T(8,128)(2,1)S(1)} %collective-permute-done.8.refs_1_), channel_id=1, source_target_pairs={{0,8},{2,10},{8,16},{10,18},{16,24},{18,26},{24,28},{26,30},{28,20... | collective-permute-start | bytes 835592 | tf_op jit(solution)/shard_map/ppermute | solution.py:168
  26.0 28.8 %collective-permute-start.2 = (bf16[64,2176]{1,0:T(8,128)(2,1)S(1)}, bf16[64,2176]{1,0:T(8,128)(2,1)S(1)}, u32[]{:S(2)}, u32[]{:S(2)}) collective-permute-start(bf16[64,2176]{1,0:T(8,128)(2,1)S(1)} %collective-permute-done.1.refs_2_), channel_id=1, source_target_pairs={{8,0},{10,2},{16,8},{18,10},{24,16},{26,18},{28,24},{30,26},{20,28... | collective-permute-start | bytes 835592 | tf_op jit(solution)/shard_map/ppermute | solution.py:168
  27.9 26.9 %collective-permute-start.5 = (bf16[64,2176]{1,0:T(8,128)(2,1)S(1)}, bf16[64,2176]{1,0:T(8,128)(2,1)S(1)}, u32[]{:S(2)}, u32[]{:S(2)}) collective-permute-start(bf16[64,2176]{1,0:T(8,128)(2,1)S(1)} %collective-permute-done.4.refs_3_), channel_id=1, source_target_pairs={{0,8},{2,10},{8,16},{10,18},{16,24},{18,26},{24,28},{26,30},{28,20... | collective-permute-start | bytes 835592 | tf_op jit(solution)/shard_map/ppermute | solution.py:168
  28.0 6.4 %copy-start.1 = (bf16[1,3,768,2048]{3,2,1,0:T(8,128)(2,1)S(1)}, bf16[1,3,768,2048]{3,2,1,0:T(8,128)(2,1)}, u32[]{:S(2)}) copy-start(bf16[1,3,768,2048]{3,2,1,0:T(8,128)(2,1)} %copy-done) | copy-start | bytes 28311556
  40.3 8.1 %collective-permute-start.11 = (bf16[64,2176]{1,0:T(8,128)(2,1)S(1)}, bf16[64,2176]{1,0:T(8,128)(2,1)S(1)}, u32[]{:S(2)}, u32[]{:S(2)}) collective-permute-start(bf16[64,2176]{1,0:T(8,128)(2,1)S(1)} %collective-permute-done.7.refs_0_), channel_id=1, source_target_pairs={{8,0},{10,2},{16,8},{18,10},{24,16},{26,18},{28,24},{30,26},{20,28... | collective-permute-start | bytes 835592 | tf_op jit(solution)/shard_map/ppermute | solution.py:168
  42.2 6.8 %collective-permute-start.12 = (bf16[64,2176]{1,0:T(8,128)(2,1)S(1)}, bf16[64,2176]{1,0:T(8,128)(2,1)S(1)}, u32[]{:S(2)}, u32[]{:S(2)}) collective-permute-start(bf16[64,2176]{1,0:T(8,128)(2,1)S(1)} %collective-permute-done.9.refs_1_), channel_id=1, source_target_pairs={{0,8},{2,10},{8,16},{10,18},{16,24},{18,26},{24,28},{26,30},{28,20... | collective-permute-start | bytes 835592 | tf_op jit(solution)/shard_map/ppermute | solution.py:168
  54.8 7.9 %collective-permute-start.13 = (bf16[64,2176]{1,0:T(8,128)(2,1)S(1)}, bf16[64,2176]{1,0:T(8,128)(2,1)S(1)}, u32[]{:S(2)}, u32[]{:S(2)}) collective-permute-start(bf16[64,2176]{1,0:T(8,128)(2,1)S(1)} %collective-permute-done.2.refs_0_), channel_id=1, source_target_pairs={{8,0},{10,2},{16,8},{18,10},{24,16},{26,18},{28,24},{30,26},{20,28... | collective-permute-start | bytes 835592 | tf_op jit(solution)/shard_map/ppermute | solution.py:168
  56.4 6.5 %collective-permute-start.14 = (bf16[64,2176]{1,0:T(8,128)(2,1)S(1)}, bf16[64,2176]{1,0:T(8,128)(2,1)S(1)}, u32[]{:S(2)}, u32[]{:S(2)}) collective-permute-start(bf16[64,2176]{1,0:T(8,128)(2,1)S(1)} %collective-permute-done.5.refs_1_), channel_id=1, source_target_pairs={{0,8},{2,10},{8,16},{10,18},{16,24},{18,26},{24,28},{26,30},{28,20... | collective-permute-start | bytes 835592 | tf_op jit(solution)/shard_map/ppermute | solution.py:168
  56.9 37.9 %slice-start = ((s8[4718592]{0:T(1024)(128)(4,1)}), s8[4194304]{0:T(1024)(128)(4,1)S(1)}, s32[]{:S(2)}) async-start(s8[4718592]{0:T(1024)(128)(4,1)} %bitcast.36), calls=%async_computation | async-start | bytes 8388608
  62.7 32.2 %slice-start.1 = ((s8[4718592]{0:T(1024)(128)(4,1)}), s8[524288]{0:T(1024)(128)(4,1)S(1)}, s32[]{:S(2)}) async-start(s8[4718592]{0:T(1024)(128)(4,1)} %bitcast.36), calls=%async_computation.1 | async-start | bytes 1048576
  68.8 13.0 %copy-start.3 = (bf16[128,2048]{1,0:T(8,128)(2,1)S(1)}, bf16[128,2048]{1,0:T(8,128)(2,1)}, u32[]{:S(2)}) copy-start(bf16[128,2048]{1,0:T(8,128)(2,1)} %refs_0_) | copy-start | bytes 1572868
  68.8 9.3 %collective-permute-start.20 = (bf16[64,2048]{1,0:T(8,128)(2,1)S(1)}, bf16[64,2048]{1,0:T(8,128)(2,1)S(1)}, u32[]{:S(2)}, u32[]{:S(2)}) collective-permute-start(bf16[64,2048]{1,0:T(8,128)(2,1)S(1)} %get-tuple-element.57), channel_id=1, source_target_pairs={{8,0},{10,2},{16,8},{18,10},{24,16},{26,18},{28,24},{30,26},{20,28... | collective-permute-start | bytes 786440 | tf_op jit(solution)/shard_map/ppermute | solution.py:168
  70.5 9.1 %collective-permute-start.27 = (bf16[64,2048]{1,0:T(8,128)(2,1)S(1)}, bf16[64,2048]{1,0:T(8,128)(2,1)S(1)}, u32[]{:S(2)}, u32[]{:S(2)}) collective-permute-start(bf16[64,2048]{1,0:T(8,128)(2,1)S(1)} %get-tuple-element.58), channel_id=1, source_target_pairs={{0,8},{2,10},{8,16},{10,18},{16,24},{18,26},{24,28},{26,30},{28,20... | collective-permute-start | bytes 786440 | tf_op jit(solution)/shard_map/ppermute | solution.py:168
  71.0 12.5 %collective-permute-start.17 = (bf16[64,2048]{1,0:T(8,128)(2,1)S(1)}, bf16[64,2048]{1,0:T(8,128)(2,1)S(1)}, u32[]{:S(2)}, u32[]{:S(2)}) collective-permute-start(bf16[64,2048]{1,0:T(8,128)(2,1)S(1)} %get-tuple-element.55), channel_id=1, source_target_pairs={{0,8},{2,10},{8,16},{10,18},{16,24},{18,26},{24,28},{26,30},{28,20... | collective-permute-start | bytes 786440 | tf_op jit(solution)/shard_map/ppermute | solution.py:168
  71.9 11.6 %collective-permute-start.24 = (bf16[64,2048]{1,0:T(8,128)(2,1)S(1)}, bf16[64,2048]{1,0:T(8,128)(2,1)S(1)}, u32[]{:S(2)}, u32[]{:S(2)}) collective-permute-start(bf16[64,2048]{1,0:T(8,128)(2,1)S(1)} %get-tuple-element.56), channel_id=1, source_target_pairs={{8,0},{10,2},{16,8},{18,10},{24,16},{26,18},{28,24},{30,26},{20,28... | collective-permute-start | bytes 786440 | tf_op jit(solution)/shard_map/ppermute | solution.py:168
  79.7 6.5 %collective-permute-start.21 = (bf16[64,2048]{1,0:T(8,128)(2,1)S(1)}, bf16[64,2048]{1,0:T(8,128)(2,1)S(1)}, u32[]{:S(2)}, u32[]{:S(2)}) collective-permute-start(bf16[64,2048]{1,0:T(8,128)(2,1)S(1)} %get-tuple-element.51), channel_id=1, source_target_pairs={{8,0},{10,2},{16,8},{18,10},{24,16},{26,18},{28,24},{30,26},{20,28... | collective-permute-start | bytes 786440 | tf_op jit(solution)/shard_map/ppermute | solution.py:168
  81.3 9.1 %collective-permute-start.28 = (bf16[64,2048]{1,0:T(8,128)(2,1)S(1)}, bf16[64,2048]{1,0:T(8,128)(2,1)S(1)}, u32[]{:S(2)}, u32[]{:S(2)}) collective-permute-start(bf16[64,2048]{1,0:T(8,128)(2,1)S(1)} %get-tuple-element.52), channel_id=1, source_target_pairs={{0,8},{2,10},{8,16},{10,18},{16,24},{18,26},{24,28},{26,30},{28,20... | collective-permute-start | bytes 786440 | tf_op jit(solution)/shard_map/ppermute | solution.py:168
  81.7 13.1 %collective-permute-start.15 = (bf16[128,2048]{1,0:T(8,128)(2,1)S(1)}, bf16[128,2048]{1,0:T(8,128)(2,1)S(1)}, u32[]{:S(2)}, u32[]{:S(2)}) collective-permute-start(bf16[128,2048]{1,0:T(8,128)(2,1)S(1)} %copy-done.3), channel_id=1, source_target_pairs={{0,1},{1,0},{2,3},{3,2},{4,5},{5,4},{6,7},{7,6},{8,9},{9,8},{10,11... | collective-permute-start | bytes 1572872 | tf_op jit(solution)/shard_map/ppermute | solution.py:17
  90.7 13.9 %collective-permute-start.18 = (bf16[64,2048]{1,0:T(8,128)(2,1)S(1)}, bf16[64,2048]{1,0:T(8,128)(2,1)S(1)}, u32[]{:S(2)}, u32[]{:S(2)}) collective-permute-start(bf16[64,2048]{1,0:T(8,128)(2,1)S(1)} %get-tuple-element.45), channel_id=1, source_target_pairs={{0,8},{2,10},{8,16},{10,18},{16,24},{18,26},{24,28},{26,30},{28,20... | collective-permute-start | bytes 786440 | tf_op jit(solution)/shard_map/ppermute | solution.py:168
  90.8 13.8 %collective-permute-start.22 = (bf16[64,2048]{1,0:T(8,128)(2,1)S(1)}, bf16[64,2048]{1,0:T(8,128)(2,1)S(1)}, u32[]{:S(2)}, u32[]{:S(2)}) collective-permute-start(bf16[64,2048]{1,0:T(8,128)(2,1)S(1)} %get-tuple-element.48), channel_id=1, source_target_pairs={{8,0},{10,2},{16,8},{18,10},{24,16},{26,18},{28,24},{30,26},{20,28... | collective-permute-start | bytes 786440 | tf_op jit(solution)/shard_map/ppermute | solution.py:168
  92.8 11.8 %collective-permute-start.25 = (bf16[64,2048]{1,0:T(8,128)(2,1)S(1)}, bf16[64,2048]{1,0:T(8,128)(2,1)S(1)}, u32[]{:S(2)}, u32[]{:S(2)}) collective-permute-start(bf16[64,2048]{1,0:T(8,128)(2,1)S(1)} %get-tuple-element.47), channel_id=1, source_target_pairs={{8,0},{10,2},{16,8},{18,10},{24,16},{26,18},{28,24},{30,26},{20,28... | collective-permute-start | bytes 786440 | tf_op jit(solution)/shard_map/ppermute | solution.py:168
  94.3 10.4 %collective-permute-start.29 = (bf16[64,2048]{1,0:T(8,128)(2,1)S(1)}, bf16[64,2048]{1,0:T(8,128)(2,1)S(1)}, u32[]{:S(2)}, u32[]{:S(2)}) collective-permute-start(bf16[64,2048]{1,0:T(8,128)(2,1)S(1)} %get-tuple-element.46), channel_id=1, source_target_pairs={{0,8},{2,10},{8,16},{10,18},{16,24},{18,26},{24,28},{26,30},{28,20... | collective-permute-start | bytes 786440 | tf_op jit(solution)/shard_map/ppermute | solution.py:168
  97.3 11.8 %collective-permute-start.16 = (bf16[128,2048]{1,0:T(8,128)(2,1)S(1)}, bf16[128,2048]{1,0:T(8,128)(2,1)S(1)}, u32[]{:S(2)}, u32[]{:S(2)}) collective-permute-start(bf16[128,2048]{1,0:T(8,128)(2,1)S(1)} %get-tuple-element.36), channel_id=1, source_target_pairs={{0,1},{1,0},{2,3},{3,2},{4,5},{5,4},{6,7},{7,6},{8,9},{9,8},{10,11... | collective-permute-start | bytes 1572872 | tf_op jit(solution)/shard_map/ppermute | solution.py:17
  105.0 6.4 %collective-permute-start.19 = (bf16[64,2048]{1,0:T(8,128)(2,1)S(1)}, bf16[64,2048]{1,0:T(8,128)(2,1)S(1)}, u32[]{:S(2)}, u32[]{:S(2)}) collective-permute-start(bf16[64,2048]{1,0:T(8,128)(2,1)S(1)} %get-tuple-element.41), channel_id=1, source_target_pairs={{0,8},{2,10},{8,16},{10,18},{16,24},{18,26},{24,28},{26,30},{28,20... | collective-permute-start | bytes 786440 | tf_op jit(solution)/shard_map/ppermute | solution.py:168
  105.1 6.4 %collective-permute-start.23 = (bf16[64,2048]{1,0:T(8,128)(2,1)S(1)}, bf16[64,2048]{1,0:T(8,128)(2,1)S(1)}, u32[]{:S(2)}, u32[]{:S(2)}) collective-permute-start(bf16[64,2048]{1,0:T(8,128)(2,1)S(1)} %get-tuple-element.44), channel_id=1, source_target_pairs={{8,0},{10,2},{16,8},{18,10},{24,16},{26,18},{28,24},{30,26},{20,28... | collective-permute-start | bytes 786440 | tf_op jit(solution)/shard_map/ppermute | solution.py:168
  107.0 7.2 %collective-permute-start.26 = (bf16[64,2048]{1,0:T(8,128)(2,1)S(1)}, bf16[64,2048]{1,0:T(8,128)(2,1)S(1)}, u32[]{:S(2)}, u32[]{:S(2)}) collective-permute-start(bf16[64,2048]{1,0:T(8,128)(2,1)S(1)} %get-tuple-element.43), channel_id=1, source_target_pairs={{8,0},{10,2},{16,8},{18,10},{24,16},{26,18},{28,24},{30,26},{20,28... | collective-permute-start | bytes 786440 | tf_op jit(solution)/shard_map/ppermute | solution.py:168
  108.5 6.4 %collective-permute-start.30 = (bf16[64,2048]{1,0:T(8,128)(2,1)S(1)}, bf16[64,2048]{1,0:T(8,128)(2,1)S(1)}, u32[]{:S(2)}, u32[]{:S(2)}) collective-permute-start(bf16[64,2048]{1,0:T(8,128)(2,1)S(1)} %get-tuple-element.42), channel_id=1, source_target_pairs={{0,8},{2,10},{8,16},{10,18},{16,24},{18,26},{24,28},{26,30},{28,20... | collective-permute-start | bytes 786440 | tf_op jit(solution)/shard_map/ppermute | solution.py:168

commit v4 on v3

--- a/solution.py
+++ b/solution.py
@@ -33,7 +33,8 @@
     return onward, [(target, source) for source, target in onward]
 
 
-def expert_kernel(parts, experts, features, kept_rows, tile, width, owners_ref, *refs):
+def expert_kernel(parts, experts, features, kept_rows, tile, width, marks, owners_ref, *refs):
+    refs = refs[marks:]
     blocks, weights, (keep_ref, *send_ref), (inputs, scales, hidden) = (
         refs[:parts],
         refs[parts : parts + experts],
@@ -83,7 +84,8 @@
             send_ref[0][:, some] = result[kept_rows:].astype(jnp.bfloat16)
 
 
-def expert_apply(blocks, weights, owners, features, kept_rows, tile=256, width=512):
+def expert_apply(blocks, weights, owners, features, kept_rows, tile=256, width=512, after=None):
+    marks = [] if after is None else [after]
     rows = sum(block.shape[0] for block in blocks)
     experts = len(weights)
     units = weights[0].shape[2]
@@ -94,9 +96,11 @@
         out_shape.append(jax.ShapeDtypeStruct((rows - kept_rows, features), jnp.bfloat16))
     return pl.pallas_call(
         functools.partial(
-            expert_kernel, len(blocks), experts, features, kept_rows, tile, width
+            expert_kernel, len(blocks), experts, features, kept_rows, tile, width, len(marks)
         ),
-        in_specs=[pl.BlockSpec(memory_space=pltpu.SMEM)] + [whole] * (len(blocks) + experts),
+        in_specs=[pl.BlockSpec(memory_space=pltpu.SMEM)]
+        + [pl.BlockSpec(memory_space=pl.ANY)] * len(marks)
+        + [whole] * (len(blocks) + experts),
         out_specs=[whole] * len(out_shape),
         out_shape=out_shape,
         scratch_shapes=[
@@ -110,98 +114,111 @@
             bytes_accessed=2 * 3 * units * features * experts + 8 * rows * features,
             transcendentals=rows * units * experts,
         ),
-    )(owners, *blocks, *weights)
-
-
-def stage_kernel(source_ref, target_ref, semaphore):
+    )(owners, *marks, *blocks, *weights)
+
+
+def stage_kernel(source_ref, other_ref, target_ref, mark_ref, semaphore):
     copy = pltpu.make_async_copy(source_ref, target_ref, semaphore)
     copy.start()
+    mark_ref[...] = jnp.zeros(mark_ref.shape, jnp.float32)
     copy.wait()
 
 
-def stage(weights):
+def stage(weights, beside):
     return pl.pallas_call(
         stage_kernel,
-        in_specs=[pl.BlockSpec(memory_space=pl.ANY)],
-        out_specs=pl.BlockSpec(memory_space=pltpu.VMEM),
-        out_shape=jax.ShapeDtypeStruct(weights.shape, weights.dtype),
+        in_specs=[pl.BlockSpec(memory_space=pl.ANY)] * 2,
+        out_specs=[pl.BlockSpec(memory_space=pltpu.VMEM)] * 2,
+        out_shape=[
+            jax.ShapeDtypeStruct(weights.shape, weights.dtype),
+            jax.ShapeDtypeStruct((8, LANES), jnp.float32),
+        ],
         scratch_shapes=[pltpu.SemaphoreType.DMA(())],
         compiler_params=pltpu.CompilerParams(vmem_limit_bytes=VMEM_BYTES),
-    )(weights)
+    )(weights, beside)
+
+
+def payload_kernel(count, tokens_ref, ids_ref, gates_ref, top_ref, bottom_ref, hot_ref):
+    rows, features = tokens_ref.shape
+    half = rows // 2
+    top_ref[:, :features] = tokens_ref[:half, :]
+    bottom_ref[:, :features] = tokens_ref[half:, :]
+    ids, gates = ids_ref[...], gates_ref[...]
+    line = lax.broadcasted_iota(jnp.int32, (top_ref.shape[1] - features, rows), 0)
+    part = (line >= count).astype(jnp.int32) + (line >= 2 * count).astype(jnp.int32)
+    label = line - part * count + 1
+    table = jnp.zeros(line.shape, jnp.float32)
+    for k in range(ids.shape[0]):
+        table = table + jnp.where(ids[k : k + 1, :] == label, gates[k : k + 1, :], 0.0)
+    high = table.astype(jnp.bfloat16).astype(jnp.float32)
+    rest = table - high
+    middle = rest.astype(jnp.bfloat16).astype(jnp.float32)
+    value = jnp.where(part == 0, high, jnp.where(part == 1, middle, rest - middle))
+    value = jnp.where(line < 3 * count, value, 0.0).T.astype(jnp.bfloat16)
+    top_ref[:, features:] = value[:half]
+    bottom_ref[:, features:] = value[half:]
+    hot = jnp.sum(jnp.where(ids == 0, gates, 0.0), axis=0, keepdims=True)
+    hot_ref[...] = jnp.broadcast_to(hot, (LANES, rows)).T[:, :1]
+
+
+def make_payload(tokens, expert_ids, gate_weights, count):
+    rows, features = tokens.shape
+    width = features + 3 * count + -(3 * count) % LANES
+    whole = pl.BlockSpec(memory_space=pltpu.VMEM)
+    block = jax.ShapeDtypeStruct((rows // 2, width), tokens.dtype)
+    return pl.pallas_call(
+        functools.partial(payload_kernel, count),
+        in_specs=[whole] * 3,
+        out_specs=[whole] * 3,
+        out_shape=[block, block, jax.ShapeDtypeStruct((rows, 1), jnp.float32)],
+        compiler_params=pltpu.CompilerParams(vmem_limit_bytes=VMEM_BYTES),
+    )(tokens, expert_ids.T, gate_weights.T)
 
 
 def on_device(tokens, expert_ids, gate_weights, hot_weights, cold_weights):
     rows, features = tokens.shape
     count = lax.axis_size("dp")
     groups = lax.axis_size("expert")
-    experts = 1 + count
     onward, backward = ring_pairs(count)
     across = [(i, i ^ 1) for i in range(count)]
     reach = count // 4
+    last = reach - 1
+    half = rows // 2
     place = lax.axis_index("dp")
     owners = jnp.stack([place, place ^ 1, count]).astype(jnp.int32)
 
-    labels = jnp.arange(experts, dtype=jnp.int32)[None, :]
-    table = jnp.zeros((rows, experts), jnp.float32)
-    for k in range(expert_ids.shape[1]):
-        table = table + jnp.where(
-            expert_ids[:, k : k + 1] == labels, gate_weights[:, k : k + 1], 0.0
-        )
-    cold_table = table[:, 1:]
-    high = lax.reduce_precision(cold_table, 8, 7)
-    rest = cold_table - high
-    middle = lax.reduce_precision(rest, 8, 7)
-    low = rest - middle
-    extra = -(3 * count) % LANES
-    payload = jnp.concatenate(
-        [
-            tokens,
-            jnp.pad(
-                jnp.concatenate([high, middle, low], axis=1).astype(jnp.bfloat16),
-                ((0, 0), (0, extra)),
-            ),
-        ],
-        axis=1,
-    )
-
     def go(block, pairs):
         return lax.ppermute(block, "dp", pairs)
 
+    def move(blocks):
+        return [go(block, way) for block, way in zip(blocks, (backward, onward))]
+
     def hold(*values):
         return lax.optimization_barrier(values)
 
-    half = rows // 2
-    top, bottom = payload[:half], payload[half:]
-    ways = (backward, onward)
-
-    def move(blocks):
-        return [go(block, way) for block, way in zip(blocks, ways)]
-
+    top, bottom, hot_gate = make_payload(tokens, expert_ids, gate_weights, count)
     short = move([top, bottom])
     long = move([bottom, top])
-    mine, other = hold(stage(cold_weights), go(cold_weights, across))
-    pair = [mine, stage(other)]
+    other, staged = stage(go(cold_weights, across), cold_weights)
+    pair = [cold_weights, other]
+    *both, staged = hold(*short, *long, staged)
+    short, long = both[:2], both[2:]
 
     def serve(blocks):
         kept = sum(block.shape[0] for block in blocks)
-        return expert_apply(blocks, pair, owners, features, kept)[0]
+        return expert_apply(blocks, pair, owners, features, kept, after=staged)[0]
 
     sums = {}
-    for k in range(1, reach - 1):
-        here, there = short, long
-        short, long = move(short), move(long)
-        both = serve(here + there)
-        *short, both = hold(*short, both)
+    for k in range(1, reach):
+        here = short + long
+        if k < last:
+            short = move(short)
+        long = move(long)
+        both = serve(here)
+        *long, both = hold(*long, both)
         sums["short", k], sums["long", k] = both[:rows], both[rows:]
-    last = reach - 1
-    both = serve(short)
-    *long, both = hold(*long, both)
-    sums["short", last] = both
-    here, long = long, move(long)
-    both = serve(here)
-    *long, both = hold(*long, both)
-    sums["long", last] = both
-    sums["long", reach] = serve(long)
+    both = serve(long + [top, bottom])
+    sums["long", reach], sums["own"] = both[:rows], both[rows:]
 
     def move_on(values):
         return [go(value.astype(jnp.bfloat16), way) for value, way in zip(values, (onward, backward))]
@@ -216,14 +233,13 @@
             short = grow(short, sums["short", k - 1])
         long = grow(long, sums["long", k])
 
-    worked, own_block, own_tokens = hold(sums["long", reach], payload, tokens)
-    hot_blocks = [own_tokens] + [shifted(own_tokens, "expert", by) for by in range(1, groups)]
+    hot_blocks = [tokens] + [shifted(tokens, "expert", by) for by in range(1, groups)]
     hot, hot_send = expert_apply(
         hot_blocks, [hot_weights], owners[1:], features, rows, tile=384
     )
     for by in range(1, groups):
         hot = hot + shifted(hot_send[(by - 1) * rows : by * rows], "expert", -by)
-    (base,) = hold(serve([own_block]) + table[:, :1] * hot)
+    (base,) = hold(sums["own"] + hot_gate * hot)
     combined = [
         base[:half] + short[0].astype(jnp.float32) + long[1].astype(jnp.float32),
         base[half:] + short[1].astype(jnp.float32) + long[0].astype(jnp.float32),

time: 116 us -> 110 us (0.948)
  Pallas kernels: 41.5 us -> 30.1 us
  waiting for transfers between devices: 25.6 us -> 32 us
  local copies, waits for them, and re-layouts: 12.1 us -> 7.52 us
  other arithmetic: 3.39 us -> 6.11 us
    pallas_call x7 -> x5, Pallas kernels: 37 us -> 26.2 us  [expert_apply(): pl.pallas_call(functools.partial(expert_kernel, len(blocks), experts, fea...]
    ppermute x29, waiting for transfers between devices: 25.6 us -> 32 us  [go(): return lax.ppermute(block, 'dp', pairs)]
    convert_element_type x3, other arithmetic: 0.73 us -> 3.34 us  [move_on(): value.astype(jnp.bfloat16)]
    unnamed x12 -> x18, local copies, waits for them, and re-layouts: 9.87 us -> 7.44 us
    pallas_call x2 -> x1, Pallas kernels: 4.47 us -> 3.84 us  [stage(): pl.pallas_call(stage_kernel, in_specs=[pl.BlockSpec(memory_space=pl.ANY)]...]
  transfers between devices with their start and end apart: 31 -> 31, of which waited for: 12 -> 15; matrix products, arithmetic and copies ran while one was open for 4% -> 5% of each run, Pallas kernels for 31% -> 22%
where the time goes in v4:
time: 110 us
  starting transfers between devices  34 us (31%)
  waiting for transfers between devices  32 us (29%)
  Pallas kernels  30.1 us (27%)
  local copies, waits for them, and re-layouts  7.52 us (7%)
  other arithmetic  6.11 us (6%)
    ppermute x29, waiting for transfers between devices, go(): return lax.ppermute(block, 'dp', pairs)  32 us
    ppermute x29, starting transfers between devices, go(): return lax.ppermute(block, 'dp', pairs)  31 us
    pallas_call x5, Pallas kernels, expert_apply(): pl.pallas_call(functools.partial(expert_kernel, len(blocks), experts, fea...  26.2 us
    unnamed x18, local copies, waits for them, and re-layouts  7.44 us
    pallas_call x1, Pallas kernels, stage(): pl.pallas_call(stage_kernel, in_specs=[pl.BlockSpec(memory_space=pl.ANY)]...  3.84 us
    convert_element_type x3, other arithmetic, move_on(): value.astype(jnp.bfloat16)  3.34 us
    ppermute x2, starting transfers between devices, shifted(): lax.ppermute(block, axis, [(i, (i + by) % size) for i in range(size)])  3.05 us
  transfers between devices with their start and end apart: 31, of which 15 were waited for; matrix products, arithmetic and copies ran while one was open for 5% of the time, Pallas kernels for 22%

profile of v4, /device:TPU:0, one launch (start us, length us, event | category | flops | bytes accessed | tf_op | source)
XLA Modules:
  0.0 110.1 jit_solution(7627872303558975072)
XLA Ops:
  0.0 0.5 collective-permute-start.4
  0.5 1.0 copy-done.3
  1.5 0.7 copy-done.5
  2.2 0.7 copy-done.6
  2.9 0.1 shard_map.55
  3.0 2.5 %collective-permute-start = (bf16[64,2176]{1,0:T(8,128)(2,1)S(1)}, bf16[64,2176]{1,0:T(8,128)(2,1)S(1)}, u32[]{:S(2)}, u32[]{:S(2)}) collective-permute-start(bf16[64,2176]{1,0:T(8,128)(2,1)S(1)} %get-tuple-element.26.refs_3_), channel_id=1, source_target_pairs={{8,0},{10,2},{16,8},{18,10},{24,16},{26,18},{28,24},{30,26},{20,28... | collective-permute-start | bytes 835592 | tf_op jit(solution)/shard_map/ppermute | solution.py:191
  5.5 0.2 collective-permute-start.1
  5.7 1.9 %collective-permute-start.2 = (bf16[64,2176]{1,0:T(8,128)(2,1)S(1)}, bf16[64,2176]{1,0:T(8,128)(2,1)S(1)}, u32[]{:S(2)}, u32[]{:S(2)}) collective-permute-start(bf16[64,2176]{1,0:T(8,128)(2,1)S(1)} %get-tuple-element.27.refs_4_), channel_id=1, source_target_pairs={{8,0},{10,2},{16,8},{18,10},{24,16},{26,18},{28,24},{30,26},{20,28... | collective-permute-start | bytes 835592 | tf_op jit(solution)/shard_map/ppermute | solution.py:191
  7.6 0.2 collective-permute-start.3
  7.8 7.3 %collective-permute-done.4.source_ref = bf16[1,3,768,2048]{3,2,1,0:T(8,128)(2,1)} collective-permute-done((bf16[1,3,768,2048]{3,2,1,0:T(8,128)(2,1)}, bf16[1,3,768,2048]{3,2,1,0:T(8,128)(2,1)}, u32[]{:S(2)}, u32[]{:S(2)}) %collective-permute-start.4) | collective-permute-done | bytes 9437216 | tf_op jit(solution)/shard_map/ppermute | solution.py:191
  15.1 3.7 %copy-done = bf16[1,3,768,2048]{3,2,1,0:T(8,128)(2,1)S(1)} copy-done((bf16[1,3,768,2048]{3,2,1,0:T(8,128)(2,1)S(1)}, bf16[1,3,768,2048]{3,2,1,0:T(8,128)(2,1)}, u32[]{:S(2)}) %copy-start) | copy-done | bytes 9437208
  18.8 3.8 %shard_map.56 = (bf16[1,3,768,2048]{3,2,1,0:T(8,128)(2,1)S(1)}, f32[8,128]{1,0:T(8,128)S(1)}) custom-call(bf16[1,3,768,2048]{3,2,1,0:T(8,128)(2,1)} %collective-permute-done.4.source_ref, bf16[1,3,768,2048]{3,2,1,0:T(8,128)(2,1)S(1)} %copy-done), custom_call_target="tpu_custom_call" | custom-call | tf_op jit(solution)/shard_map/pallas_call | solution.py:128
  22.7 2.9 %collective-permute-start.5 = (bf16[64,2176]{1,0:T(8,128)(2,1)S(1)}, bf16[64,2176]{1,0:T(8,128)(2,1)S(1)}, u32[]{:S(2)}, u32[]{:S(2)}) collective-permute-start(bf16[64,2176]{1,0:T(8,128)(2,1)S(1)} %collective-permute-done.2.refs_3_), channel_id=1, source_target_pairs={{8,0},{10,2},{16,8},{18,10},{24,16},{26,18},{28,24},{30,26},{20,28... | collective-permute-start | bytes 835592 | tf_op jit(solution)/shard_map/ppermute | solution.py:191
  25.6 0.2 collective-permute-start.6
  25.7 2.0 %collective-permute-start.10 = (bf16[64,2176]{1,0:T(8,128)(2,1)S(1)}, bf16[64,2176]{1,0:T(8,128)(2,1)S(1)}, u32[]{:S(2)}, u32[]{:S(2)}) collective-permute-start(bf16[64,2176]{1,0:T(8,128)(2,1)S(1)} %collective-permute-done.1.refs_2_), channel_id=1, source_target_pairs={{0,8},{2,10},{8,16},{10,18},{16,24},{18,26},{24,28},{26,30},{28,20... | collective-permute-start | bytes 835592 | tf_op jit(solution)/shard_map/ppermute | solution.py:191
  27.7 5.7 %shard_map.57 = f32[256,2048]{1,0:T(8,128)S(1)} custom-call(s32[3]{0:T(128)S(1)} %pad_add_fusion.owners_ref, f32[8,128]{1,0:T(8,128)S(1)} %get-tuple-element.29.refs_0_, bf16[64,2176]{1,0:T(8,128)(2,1)S(1)} %collective-permute-done.refs_1_, bf16[64,2176]{1,0:T(8,128)(2,1)S(1)} %collective-permute-done.1.refs_2_, ...), custom_call_target="tpu_custom_call" | custom-call | flops 4831838208 | bytes 23068672 | tf_op jit(solution)/shard_map/pallas_call | solution.py:97
  33.5 1.3 %copy-done.2 = f32[256,2048]{1,0:T(8,128)} copy-done((f32[256,2048]{1,0:T(8,128)}, f32[256,2048]{1,0:T(8,128)S(1)}, u32[]{:S(2)}) %copy-start.2) | copy-done | bytes 2097176
  34.8 0.3 collective-permute-done.6.refs_4_
  35.1 1.6 %collective-permute-start.7 = (bf16[64,2176]{1,0:T(8,128)(2,1)S(1)}, bf16[64,2176]{1,0:T(8,128)(2,1)S(1)}, u32[]{:S(2)}, u32[]{:S(2)}) collective-permute-start(bf16[64,2176]{1,0:T(8,128)(2,1)S(1)} %collective-permute-done.5.refs_3_), channel_id=1, source_target_pairs={{8,0},{10,2},{16,8},{18,10},{24,16},{26,18},{28,24},{30,26},{20,28... | collective-permute-start | bytes 835592 | tf_op jit(solution)/shard_map/ppermute | solution.py:191
  36.7 0.4 collective-permute-start.8
  37.1 1.9 %collective-permute-done.9.refs_1_ = bf16[64,2176]{1,0:T(8,128)(2,1)S(1)} collective-permute-done((bf16[64,2176]{1,0:T(8,128)(2,1)S(1)}, bf16[64,2176]{1,0:T(8,128)(2,1)S(1)}, u32[]{:S(2)}, u32[]{:S(2)}) %collective-permute-start.9) | collective-permute-done | bytes 278560 | tf_op jit(solution)/shard_map/ppermute | solution.py:191
  39.1 2.0 %collective-permute-start.13 = (bf16[64,2176]{1,0:T(8,128)(2,1)S(1)}, bf16[64,2176]{1,0:T(8,128)(2,1)S(1)}, u32[]{:S(2)}, u32[]{:S(2)}) collective-permute-start(bf16[64,2176]{1,0:T(8,128)(2,1)S(1)} %collective-permute-done.9.refs_1_), channel_id=1, source_target_pairs={{8,0},{10,2},{16,8},{18,10},{24,16},{26,18},{28,24},{30,26},{20,28... | collective-permute-start | bytes 835592 | tf_op jit(solution)/shard_map/ppermute | solution.py:191
  41.1 0.1 collective-permute-start.14
  41.2 5.7 %shard_map.58 = f32[256,2048]{1,0:T(8,128)S(1)} custom-call(s32[3]{0:T(128)S(1)} %pad_add_fusion.owners_ref, f32[8,128]{1,0:T(8,128)S(1)} %get-tuple-element.29.refs_0_, bf16[64,2176]{1,0:T(8,128)(2,1)S(1)} %collective-permute-done.9.refs_1_, bf16[64,2176]{1,0:T(8,128)(2,1)S(1)} %collective-permute-done.10.refs_2_, ...), custom_call_target="tpu_custom_call" | custom-call | flops 4831838208 | bytes 23068672 | tf_op jit(solution)/shard_map/pallas_call | solution.py:97
  47.0 1.9 %collective-permute-start.11 = (bf16[64,2176]{1,0:T(8,128)(2,1)S(1)}, bf16[64,2176]{1,0:T(8,128)(2,1)S(1)}, u32[]{:S(2)}, u32[]{:S(2)}) collective-permute-start(bf16[64,2176]{1,0:T(8,128)(2,1)S(1)} %collective-permute-done.7.refs_3_), channel_id=1, source_target_pairs={{8,0},{10,2},{16,8},{18,10},{24,16},{26,18},{28,24},{30,26},{20,28... | collective-permute-start | bytes 835592 | tf_op jit(solution)/shard_map/ppermute | solution.py:191
  48.9 0.3 collective-permute-start.12
  49.3 1.7 %collective-permute-done.13.refs_1_ = bf16[64,2176]{1,0:T(8,128)(2,1)S(1)} collective-permute-done((bf16[64,2176]{1,0:T(8,128)(2,1)S(1)}, bf16[64,2176]{1,0:T(8,128)(2,1)S(1)}, u32[]{:S(2)}, u32[]{:S(2)}) %collective-permute-start.13) | collective-permute-done | bytes 278560 | tf_op jit(solution)/shard_map/ppermute | solution.py:191
  51.0 2.0 %collective-permute-done.14.refs_2_ = bf16[64,2176]{1,0:T(8,128)(2,1)S(1)} collective-permute-done((bf16[64,2176]{1,0:T(8,128)(2,1)S(1)}, bf16[64,2176]{1,0:T(8,128)(2,1)S(1)}, u32[]{:S(2)}, u32[]{:S(2)}) %collective-permute-start.14) | collective-permute-done | bytes 278560 | tf_op jit(solution)/shard_map/ppermute | solution.py:191
  53.0 5.7 %shard_map.59 = f32[256,2048]{1,0:T(8,128)S(1)} custom-call(s32[3]{0:T(128)S(1)} %pad_add_fusion.owners_ref, f32[8,128]{1,0:T(8,128)S(1)} %get-tuple-element.29.refs_0_, bf16[64,2176]{1,0:T(8,128)(2,1)S(1)} %collective-permute-done.13.refs_1_, bf16[64,2176]{1,0:T(8,128)(2,1)S(1)} %collective-permute-done.14.refs_2_, ...), custom_call_target="tpu_custom_call" | custom-call | flops 4831838208 | bytes 23068672 | tf_op jit(solution)/shard_map/pallas_call | solution.py:97
  58.8 5.7 %shard_map.60 = f32[256,2048]{1,0:T(8,128)S(1)} custom-call(s32[3]{0:T(128)S(1)} %pad_add_fusion.owners_ref, f32[8,128]{1,0:T(8,128)S(1)} %get-tuple-element.29.refs_0_, bf16[64,2176]{1,0:T(8,128)(2,1)S(1)} %collective-permute-done.11.refs_1_, bf16[64,2176]{1,0:T(8,128)(2,1)S(1)} %collective-permute-done.12.refs_2_, ...), custom_call_target="tpu_custom_call" | custom-call | flops 4831838208 | bytes 23068672 | tf_op jit(solution)/shard_map/pallas_call | solution.py:97
  64.5 0.1 convert.15
  64.7 1.6 %collective-permute-start.20 = (bf16[64,2048]{1,0:T(8,128)(2,1)S(1)}, bf16[64,2048]{1,0:T(8,128)(2,1)S(1)}, u32[]{:S(2)}, u32[]{:S(2)}) collective-permute-start(bf16[64,2048]{1,0:T(8,128)(2,1)S(1)} %get-tuple-element.61), channel_id=1, source_target_pairs={{8,0},{10,2},{16,8},{18,10},{24,16},{26,18},{28,24},{30,26},{20,28... | collective-permute-start | bytes 786440 | tf_op jit(solution)/shard_map/ppermute | solution.py:191
  66.4 0.5 collective-permute-start.27
  66.8 0.1 convert.14
  67.0 0.2 collective-permute-start.17
  67.2 1.9 %collective-permute-start.24 = (bf16[64,2048]{1,0:T(8,128)(2,1)S(1)}, bf16[64,2048]{1,0:T(8,128)(2,1)S(1)}, u32[]{:S(2)}, u32[]{:S(2)}) collective-permute-start(bf16[64,2048]{1,0:T(8,128)(2,1)S(1)} %get-tuple-element.60), channel_id=1, source_target_pairs={{8,0},{10,2},{16,8},{18,10},{24,16},{26,18},{28,24},{30,26},{20,28... | collective-permute-start | bytes 786440 | tf_op jit(solution)/shard_map/ppermute | solution.py:191
  69.1 4.9 %collective-permute-done.20 = bf16[64,2048]{1,0:T(8,128)(2,1)S(1)} collective-permute-done((bf16[64,2048]{1,0:T(8,128)(2,1)S(1)}, bf16[64,2048]{1,0:T(8,128)(2,1)S(1)}, u32[]{:S(2)}, u32[]{:S(2)}) %collective-permute-start.20) | collective-permute-done | bytes 262176 | tf_op jit(solution)/shard_map/ppermute | solution.py:191
  74.0 1.6 %collective-permute-done.27 = bf16[64,2048]{1,0:T(8,128)(2,1)S(1)} collective-permute-done((bf16[64,2048]{1,0:T(8,128)(2,1)S(1)}, bf16[64,2048]{1,0:T(8,128)(2,1)S(1)}, u32[]{:S(2)}, u32[]{:S(2)}) %collective-permute-start.27) | collective-permute-done | bytes 262176 | tf_op jit(solution)/shard_map/ppermute | solution.py:191
  75.6 0.1 add_convert_fusion.7
  75.7 1.6 %collective-permute-start.21 = (bf16[64,2048]{1,0:T(8,128)(2,1)S(1)}, bf16[64,2048]{1,0:T(8,128)(2,1)S(1)}, u32[]{:S(2)}, u32[]{:S(2)}) collective-permute-start(bf16[64,2048]{1,0:T(8,128)(2,1)S(1)} %get-tuple-element.55), channel_id=1, source_target_pairs={{8,0},{10,2},{16,8},{18,10},{24,16},{26,18},{28,24},{30,26},{20,28... | collective-permute-start | bytes 786440 | tf_op jit(solution)/shard_map/ppermute | solution.py:191
  77.4 0.4 collective-permute-start.28
  77.8 1.5 %collective-permute-start.15 = (bf16[128,2048]{1,0:T(8,128)(2,1)S(1)}, bf16[128,2048]{1,0:T(8,128)(2,1)S(1)}, u32[]{:S(2)}, u32[]{:S(2)}) collective-permute-start(bf16[128,2048]{1,0:T(8,128)(2,1)S(1)} %copy-done.4), channel_id=1, source_target_pairs={{0,1},{1,0},{2,3},{3,2},{4,5},{5,4},{6,7},{7,6},{8,9},{9,8},{10,11... | collective-permute-start | bytes 1572872 | tf_op jit(solution)/shard_map/ppermute | solution.py:17
  79.3 1.4 %collective-permute-done.17 = bf16[64,2048]{1,0:T(8,128)(2,1)S(1)} collective-permute-done((bf16[64,2048]{1,0:T(8,128)(2,1)S(1)}, bf16[64,2048]{1,0:T(8,128)(2,1)S(1)}, u32[]{:S(2)}, u32[]{:S(2)}) %collective-permute-start.17) | collective-permute-done | bytes 262176 | tf_op jit(solution)/shard_map/ppermute | solution.py:191
  80.8 1.5 %collective-permute-done.21 = bf16[64,2048]{1,0:T(8,128)(2,1)S(1)} collective-permute-done((bf16[64,2048]{1,0:T(8,128)(2,1)S(1)}, bf16[64,2048]{1,0:T(8,128)(2,1)S(1)}, u32[]{:S(2)}, u32[]{:S(2)}) %collective-permute-start.21) | collective-permute-done | bytes 262176 | tf_op jit(solution)/shard_map/ppermute | solution.py:191
  82.3 1.5 %collective-permute-done.28 = bf16[64,2048]{1,0:T(8,128)(2,1)S(1)} collective-permute-done((bf16[64,2048]{1,0:T(8,128)(2,1)S(1)}, bf16[64,2048]{1,0:T(8,128)(2,1)S(1)}, u32[]{:S(2)}, u32[]{:S(2)}) %collective-permute-start.28) | collective-permute-done | bytes 262176 | tf_op jit(solution)/shard_map/ppermute | solution.py:191
  83.7 1.2 %add_convert_fusion.9 = (bf16[64,2048]{1,0:T(8,128)(2,1)}, bf16[64,2048]{1,0:T(8,128)(2,1)}, bf16[64,2048]{1,0:T(8,128)(2,1)}, bf16[64,2048]{1,0:T(8,128)(2,1)}) fusion(bf16[64,2048]{1,0:T(8,128)(2,1)S(1)} %collective-permute-done.17, f32[256,2048]{1,0:T(8,128)S(1)} %shard_map.58, bf16[64,2048]{1,0:T(8,128)(2,1)S(1)} %collective-permute-done.28, ...), kind=kLoop, calls=%fused_computation.17 | loop fusion | flops 1572864 | bytes 4194304 | tf_op jit(solution)/shard_map/convert_element_type | solution.py:224
  84.9 0.4 collective-permute-start.18
  85.4 1.6 %collective-permute-start.22 = (bf16[64,2048]{1,0:T(8,128)(2,1)}, bf16[64,2048]{1,0:T(8,128)(2,1)}, u32[]{:S(2)}, u32[]{:S(2)}) collective-permute-start(bf16[64,2048]{1,0:T(8,128)(2,1)} %get-tuple-element.54), channel_id=1, source_target_pairs={{8,0},{10,2},{16,8},{18,10},{24,16},{26,18},{28,24},{30,26},{20,28... | collective-permute-start | bytes 786440 | tf_op jit(solution)/shard_map/ppermute | solution.py:191
  87.0 1.6 %collective-permute-start.25 = (bf16[64,2048]{1,0:T(8,128)(2,1)}, bf16[64,2048]{1,0:T(8,128)(2,1)}, u32[]{:S(2)}, u32[]{:S(2)}) collective-permute-start(bf16[64,2048]{1,0:T(8,128)(2,1)} %get-tuple-element.53), channel_id=1, source_target_pairs={{8,0},{10,2},{16,8},{18,10},{24,16},{26,18},{28,24},{30,26},{20,28... | collective-permute-start | bytes 786440 | tf_op jit(solution)/shard_map/ppermute | solution.py:191
  88.5 0.4 collective-permute-start.29
  89.1 3.2 %shard_map.61 = (f32[128,2048]{1,0:T(8,128)S(1)}, bf16[128,2048]{1,0:T(8,128)(2,1)}) custom-call(s32[2]{0:T(128)S(1)} %pad_add_fusion.1.owners_ref, bf16[128,2048]{1,0:T(8,128)(2,1)S(1)} %copy-done.4, bf16[128,2048]{1,0:T(8,128)(2,1)S(1)} %collective-permute-done.15.refs_1_, bf16[1,3,384,2048]{3,2,1,0:T(8,128)(2,1)S(1)} %bitcast.5), custom_call_target="tpu_custom_call" | custom-call | flops 1207959552 | bytes 8912896 | tf_op jit(solution)/shard_map/pallas_call | solution.py:97
  92.3 1.5 %collective-permute-start.16 = (bf16[128,2048]{1,0:T(8,128)(2,1)}, bf16[128,2048]{1,0:T(8,128)(2,1)}, u32[]{:S(2)}, u32[]{:S(2)}) collective-permute-start(bf16[128,2048]{1,0:T(8,128)(2,1)} %get-tuple-element.43), channel_id=1, source_target_pairs={{0,1},{1,0},{2,3},{3,2},{4,5},{5,4},{6,7},{7,6},{8,9},{9,8},{10,11... | collective-permute-start | bytes 1572872 | tf_op jit(solution)/shard_map/ppermute | solution.py:17
  94.0 2.0 %collective-permute-done.25 = bf16[64,2048]{1,0:T(8,128)(2,1)} collective-permute-done((bf16[64,2048]{1,0:T(8,128)(2,1)}, bf16[64,2048]{1,0:T(8,128)(2,1)}, u32[]{:S(2)}, u32[]{:S(2)}) %collective-permute-start.25) | collective-permute-done | bytes 262176 | tf_op jit(solution)/shard_map/ppermute | solution.py:191
  95.9 2.0 %add_convert_fusion.8 = (bf16[64,2048]{1,0:T(8,128)(2,1)S(1)}, bf16[64,2048]{1,0:T(8,128)(2,1)S(1)}, bf16[64,2048]{1,0:T(8,128)(2,1)S(1)}, bf16[64,2048]{1,0:T(8,128)(2,1)S(1)}) fusion(bf16[64,2048]{1,0:T(8,128)(2,1)S(1)} %collective-permute-done.18, f32[256,2048]{1,0:T(8,128)} %copy-done.2, bf16[64,2048]{1,0:T(8,128)(2,1)} %collective-permute-done.29, ...), kind=kLoop, calls=%fused_computation.16 | loop fusion | flops 1572864 | bytes 4194304 | tf_op jit(solution)/shard_map/convert_element_type | solution.py:224
  98.0 1.3 %collective-permute-start.19 = (bf16[64,2048]{1,0:T(8,128)(2,1)S(1)}, bf16[64,2048]{1,0:T(8,128)(2,1)S(1)}, u32[]{:S(2)}, u32[]{:S(2)}) collective-permute-start(bf16[64,2048]{1,0:T(8,128)(2,1)S(1)} %get-tuple-element.47), channel_id=1, source_target_pairs={{0,8},{2,10},{8,16},{10,18},{16,24},{18,26},{24,28},{26,30},{28,20... | collective-permute-start | bytes 786440 | tf_op jit(solution)/shard_map/ppermute | solution.py:191
  99.3 0.7 collective-permute-start.23
  100.0 1.6 %collective-permute-start.26 = (bf16[64,2048]{1,0:T(8,128)(2,1)S(1)}, bf16[64,2048]{1,0:T(8,128)(2,1)S(1)}, u32[]{:S(2)}, u32[]{:S(2)}) collective-permute-start(bf16[64,2048]{1,0:T(8,128)(2,1)S(1)} %get-tuple-element.49), channel_id=1, source_target_pairs={{8,0},{10,2},{16,8},{18,10},{24,16},{26,18},{28,24},{30,26},{20,28... | collective-permute-start | bytes 786440 | tf_op jit(solution)/shard_map/ppermute | solution.py:191
  101.6 0.5 collective-permute-start.30
  102.1 1.2 %slice_add_fusion = f32[128,2048]{1,0:T(8,128)S(1)} fusion(f32[256,2048]{1,0:T(8,128)S(1)} %shard_map.60, f32[128,2048]{1,0:T(8,128)S(1)} %get-tuple-element.42, bf16[128,2048]{1,0:T(8,128)(2,1)} %collective-permute-done.16, f32[128]{0:T(128)S(1)} %reduce), kind=kLoop, calls=%fused_computation | loop fusion | flops 1048576 | bytes 3670528 | tf_op jit(solution)/shard_map/add | solution.py:242
  103.3 1.3 %collective-permute-done.19 = bf16[64,2048]{1,0:T(8,128)(2,1)S(1)} collective-permute-done((bf16[64,2048]{1,0:T(8,128)(2,1)S(1)}, bf16[64,2048]{1,0:T(8,128)(2,1)S(1)}, u32[]{:S(2)}, u32[]{:S(2)}) %collective-permute-start.19) | collective-permute-done | bytes 262176 | tf_op jit(solution)/shard_map/ppermute | solution.py:191
  104.6 1.6 %collective-permute-done.23 = bf16[64,2048]{1,0:T(8,128)(2,1)S(1)} collective-permute-done((bf16[64,2048]{1,0:T(8,128)(2,1)S(1)}, bf16[64,2048]{1,0:T(8,128)(2,1)S(1)}, u32[]{:S(2)}, u32[]{:S(2)}) %collective-permute-start.23) | collective-permute-done | bytes 262176 | tf_op jit(solution)/shard_map/ppermute | solution.py:191
  106.2 2.8 %collective-permute-done.26 = bf16[64,2048]{1,0:T(8,128)(2,1)S(1)} collective-permute-done((bf16[64,2048]{1,0:T(8,128)(2,1)S(1)}, bf16[64,2048]{1,0:T(8,128)(2,1)S(1)}, u32[]{:S(2)}, u32[]{:S(2)}) %collective-permute-start.26) | collective-permute-done | bytes 262176 | tf_op jit(solution)/shard_map/ppermute | solution.py:191
  109.0 0.2 fusion.3
  109.2 0.8 pad_maximum_fusion
  (37 shorter events, 0.6 us)
Async XLA Ops:
  0.0 15.1 %collective-permute-start.4 = (bf16[1,3,768,2048]{3,2,1,0:T(8,128)(2,1)}, bf16[1,3,768,2048]{3,2,1,0:T(8,128)(2,1)}, u32[]{:S(2)}, u32[]{:S(2)}) collective-permute-start(bf16[1,3,768,2048]{3,2,1,0:T(8,128)(2,1)} %refs_5_.7), channel_id=1, source_target_pairs={{0,2},{2,0},{4,6},{6,4},{8,10},{10,8},{12,14},{14,12},{16,18},{18,... | collective-permute-start | bytes 28311560 | tf_op jit(solution)/shard_map/ppermute | solution.py:191
  0.5 1.0 copy-start.3
  1.5 0.7 copy-start.5
  2.2 0.7 copy-start.6
  3.0 19.6 %collective-permute-start = (bf16[64,2176]{1,0:T(8,128)(2,1)S(1)}, bf16[64,2176]{1,0:T(8,128)(2,1)S(1)}, u32[]{:S(2)}, u32[]{:S(2)}) collective-permute-start(bf16[64,2176]{1,0:T(8,128)(2,1)S(1)} %get-tuple-element.26.refs_3_), channel_id=1, source_target_pairs={{8,0},{10,2},{16,8},{18,10},{24,16},{26,18},{28,24},{30,26},{20,28... | collective-permute-start | bytes 835592 | tf_op jit(solution)/shard_map/ppermute | solution.py:191
  5.5 17.1 %collective-permute-start.1 = (bf16[64,2176]{1,0:T(8,128)(2,1)S(1)}, bf16[64,2176]{1,0:T(8,128)(2,1)S(1)}, u32[]{:S(2)}, u32[]{:S(2)}) collective-permute-start(bf16[64,2176]{1,0:T(8,128)(2,1)S(1)} %get-tuple-element.27.refs_4_), channel_id=1, source_target_pairs={{0,8},{2,10},{8,16},{10,18},{16,24},{18,26},{24,28},{26,30},{28,20... | collective-permute-start | bytes 835592 | tf_op jit(solution)/shard_map/ppermute | solution.py:191
  5.7 16.9 %collective-permute-start.2 = (bf16[64,2176]{1,0:T(8,128)(2,1)S(1)}, bf16[64,2176]{1,0:T(8,128)(2,1)S(1)}, u32[]{:S(2)}, u32[]{:S(2)}) collective-permute-start(bf16[64,2176]{1,0:T(8,128)(2,1)S(1)} %get-tuple-element.27.refs_4_), channel_id=1, source_target_pairs={{8,0},{10,2},{16,8},{18,10},{24,16},{26,18},{28,24},{30,26},{20,28... | collective-permute-start | bytes 835592 | tf_op jit(solution)/shard_map/ppermute | solution.py:191
  7.6 15.1 %collective-permute-start.3 = (bf16[64,2176]{1,0:T(8,128)(2,1)S(1)}, bf16[64,2176]{1,0:T(8,128)(2,1)S(1)}, u32[]{:S(2)}, u32[]{:S(2)}) collective-permute-start(bf16[64,2176]{1,0:T(8,128)(2,1)S(1)} %get-tuple-element.26.refs_3_), channel_id=1, source_target_pairs={{0,8},{2,10},{8,16},{10,18},{16,24},{18,26},{24,28},{26,30},{28,20... | collective-permute-start | bytes 835592 | tf_op jit(solution)/shard_map/ppermute | solution.py:191
  15.1 3.7 %copy-start = (bf16[1,3,768,2048]{3,2,1,0:T(8,128)(2,1)S(1)}, bf16[1,3,768,2048]{3,2,1,0:T(8,128)(2,1)}, u32[]{:S(2)}) copy-start(bf16[1,3,768,2048]{3,2,1,0:T(8,128)(2,1)} %refs_5_.7) | copy-start | bytes 28311556
  18.8 9.0 %copy-start.1 = (bf16[1,3,768,2048]{3,2,1,0:T(8,128)(2,1)S(1)}, bf16[1,3,768,2048]{3,2,1,0:T(8,128)(2,1)}, u32[]{:S(2)}) copy-start(bf16[1,3,768,2048]{3,2,1,0:T(8,128)(2,1)} %refs_5_.7) | copy-start | bytes 28311556
  22.7 12.2 %collective-permute-start.5 = (bf16[64,2176]{1,0:T(8,128)(2,1)S(1)}, bf16[64,2176]{1,0:T(8,128)(2,1)S(1)}, u32[]{:S(2)}, u32[]{:S(2)}) collective-permute-start(bf16[64,2176]{1,0:T(8,128)(2,1)S(1)} %collective-permute-done.2.refs_3_), channel_id=1, source_target_pairs={{8,0},{10,2},{16,8},{18,10},{24,16},{26,18},{28,24},{30,26},{20,28... | collective-permute-start | bytes 835592 | tf_op jit(solution)/shard_map/ppermute | solution.py:191
  25.6 9.5 %collective-permute-start.6 = (bf16[64,2176]{1,0:T(8,128)(2,1)S(1)}, bf16[64,2176]{1,0:T(8,128)(2,1)S(1)}, u32[]{:S(2)}, u32[]{:S(2)}) collective-permute-start(bf16[64,2176]{1,0:T(8,128)(2,1)S(1)} %collective-permute-done.3.refs_4_), channel_id=1, source_target_pairs={{0,8},{2,10},{8,16},{10,18},{16,24},{18,26},{24,28},{26,30},{28,20... | collective-permute-start | bytes 835592 | tf_op jit(solution)/shard_map/ppermute | solution.py:191
  25.7 15.4 %collective-permute-start.10 = (bf16[64,2176]{1,0:T(8,128)(2,1)S(1)}, bf16[64,2176]{1,0:T(8,128)(2,1)S(1)}, u32[]{:S(2)}, u32[]{:S(2)}) collective-permute-start(bf16[64,2176]{1,0:T(8,128)(2,1)S(1)} %collective-permute-done.1.refs_2_), channel_id=1, source_target_pairs={{0,8},{2,10},{8,16},{10,18},{16,24},{18,26},{24,28},{26,30},{28,20... | collective-permute-start | bytes 835592 | tf_op jit(solution)/shard_map/ppermute | solution.py:191
  27.7 11.4 %collective-permute-start.9 = (bf16[64,2176]{1,0:T(8,128)(2,1)S(1)}, bf16[64,2176]{1,0:T(8,128)(2,1)S(1)}, u32[]{:S(2)}, u32[]{:S(2)}) collective-permute-start(bf16[64,2176]{1,0:T(8,128)(2,1)S(1)} %collective-permute-done.refs_1_), channel_id=1, source_target_pairs={{8,0},{10,2},{16,8},{18,10},{24,16},{26,18},{28,24},{30,26},{20,28... | collective-permute-start | bytes 835592 | tf_op jit(solution)/shard_map/ppermute | solution.py:191
  33.5 1.3 %copy-start.2 = (f32[256,2048]{1,0:T(8,128)}, f32[256,2048]{1,0:T(8,128)S(1)}, u32[]{:S(2)}) copy-start(f32[256,2048]{1,0:T(8,128)S(1)} %shard_map.57) | copy-start | bytes 6291460
  35.1 11.8 %collective-permute-start.7 = (bf16[64,2176]{1,0:T(8,128)(2,1)S(1)}, bf16[64,2176]{1,0:T(8,128)(2,1)S(1)}, u32[]{:S(2)}, u32[]{:S(2)}) collective-permute-start(bf16[64,2176]{1,0:T(8,128)(2,1)S(1)} %collective-permute-done.5.refs_3_), channel_id=1, source_target_pairs={{8,0},{10,2},{16,8},{18,10},{24,16},{26,18},{28,24},{30,26},{20,28... | collective-permute-start | bytes 835592 | tf_op jit(solution)/shard_map/ppermute | solution.py:191
  36.7 10.3 %collective-permute-start.8 = (bf16[64,2176]{1,0:T(8,128)(2,1)S(1)}, bf16[64,2176]{1,0:T(8,128)(2,1)S(1)}, u32[]{:S(2)}, u32[]{:S(2)}) collective-permute-start(bf16[64,2176]{1,0:T(8,128)(2,1)S(1)} %collective-permute-done.6.refs_4_), channel_id=1, source_target_pairs={{0,8},{2,10},{8,16},{10,18},{16,24},{18,26},{24,28},{26,30},{28,20... | collective-permute-start | bytes 835592 | tf_op jit(solution)/shard_map/ppermute | solution.py:191
  39.1 11.9 %collective-permute-start.13 = (bf16[64,2176]{1,0:T(8,128)(2,1)S(1)}, bf16[64,2176]{1,0:T(8,128)(2,1)S(1)}, u32[]{:S(2)}, u32[]{:S(2)}) collective-permute-start(bf16[64,2176]{1,0:T(8,128)(2,1)S(1)} %collective-permute-done.9.refs_1_), channel_id=1, source_target_pairs={{8,0},{10,2},{16,8},{18,10},{24,16},{26,18},{28,24},{30,26},{20,28... | collective-permute-start | bytes 835592 | tf_op jit(solution)/shard_map/ppermute | solution.py:191
  41.1 11.9 %collective-permute-start.14 = (bf16[64,2176]{1,0:T(8,128)(2,1)S(1)}, bf16[64,2176]{1,0:T(8,128)(2,1)S(1)}, u32[]{:S(2)}, u32[]{:S(2)}) collective-permute-start(bf16[64,2176]{1,0:T(8,128)(2,1)S(1)} %collective-permute-done.10.refs_2_), channel_id=1, source_target_pairs={{0,8},{2,10},{8,16},{10,18},{16,24},{18,26},{24,28},{26,30},{28,20... | collective-permute-start | bytes 835592 | tf_op jit(solution)/shard_map/ppermute | solution.py:191
  47.0 11.7 %collective-permute-start.11 = (bf16[64,2176]{1,0:T(8,128)(2,1)S(1)}, bf16[64,2176]{1,0:T(8,128)(2,1)S(1)}, u32[]{:S(2)}, u32[]{:S(2)}) collective-permute-start(bf16[64,2176]{1,0:T(8,128)(2,1)S(1)} %collective-permute-done.7.refs_3_), channel_id=1, source_target_pairs={{8,0},{10,2},{16,8},{18,10},{24,16},{26,18},{28,24},{30,26},{20,28... | collective-permute-start | bytes 835592 | tf_op jit(solution)/shard_map/ppermute | solution.py:191
  48.9 9.9 %collective-permute-start.12 = (bf16[64,2176]{1,0:T(8,128)(2,1)S(1)}, bf16[64,2176]{1,0:T(8,128)(2,1)S(1)}, u32[]{:S(2)}, u32[]{:S(2)}) collective-permute-start(bf16[64,2176]{1,0:T(8,128)(2,1)S(1)} %collective-permute-done.8.refs_4_), channel_id=1, source_target_pairs={{0,8},{2,10},{8,16},{10,18},{16,24},{18,26},{24,28},{26,30},{28,20... | collective-permute-start | bytes 835592 | tf_op jit(solution)/shard_map/ppermute | solution.py:191
  53.0 36.1 %slice-start = ((s8[4718592]{0:T(1024)(128)(4,1)}), s8[4194304]{0:T(1024)(128)(4,1)S(1)}, s32[]{:S(2)}) async-start(s8[4718592]{0:T(1024)(128)(4,1)} %bitcast.4), calls=%async_computation | async-start | bytes 8388608
  58.8 30.3 %slice-start.1 = ((s8[4718592]{0:T(1024)(128)(4,1)}), s8[524288]{0:T(1024)(128)(4,1)S(1)}, s32[]{:S(2)}) async-start(s8[4718592]{0:T(1024)(128)(4,1)} %bitcast.4), calls=%async_computation.1 | async-start | bytes 1048576
  64.7 9.3 %collective-permute-start.20 = (bf16[64,2048]{1,0:T(8,128)(2,1)S(1)}, bf16[64,2048]{1,0:T(8,128)(2,1)S(1)}, u32[]{:S(2)}, u32[]{:S(2)}) collective-permute-start(bf16[64,2048]{1,0:T(8,128)(2,1)S(1)} %get-tuple-element.61), channel_id=1, source_target_pairs={{8,0},{10,2},{16,8},{18,10},{24,16},{26,18},{28,24},{30,26},{20,28... | collective-permute-start | bytes 786440 | tf_op jit(solution)/shard_map/ppermute | solution.py:191
  66.4 9.2 %collective-permute-start.27 = (bf16[64,2048]{1,0:T(8,128)(2,1)S(1)}, bf16[64,2048]{1,0:T(8,128)(2,1)S(1)}, u32[]{:S(2)}, u32[]{:S(2)}) collective-permute-start(bf16[64,2048]{1,0:T(8,128)(2,1)S(1)} %get-tuple-element.62), channel_id=1, source_target_pairs={{0,8},{2,10},{8,16},{10,18},{16,24},{18,26},{24,28},{26,30},{28,20... | collective-permute-start | bytes 786440 | tf_op jit(solution)/shard_map/ppermute | solution.py:191
  67.0 10.9 %copy-start.4 = (bf16[128,2048]{1,0:T(8,128)(2,1)S(1)}, bf16[128,2048]{1,0:T(8,128)(2,1)}, u32[]{:S(2)}) copy-start(bf16[128,2048]{1,0:T(8,128)(2,1)} %refs_0_.1) | copy-start | bytes 1572868
  67.0 13.7 %collective-permute-start.17 = (bf16[64,2048]{1,0:T(8,128)(2,1)S(1)}, bf16[64,2048]{1,0:T(8,128)(2,1)S(1)}, u32[]{:S(2)}, u32[]{:S(2)}) collective-permute-start(bf16[64,2048]{1,0:T(8,128)(2,1)S(1)} %get-tuple-element.59), channel_id=1, source_target_pairs={{0,8},{2,10},{8,16},{10,18},{16,24},{18,26},{24,28},{26,30},{28,20... | collective-permute-start | bytes 786440 | tf_op jit(solution)/shard_map/ppermute | solution.py:191
  67.2 13.5 %collective-permute-start.24 = (bf16[64,2048]{1,0:T(8,128)(2,1)S(1)}, bf16[64,2048]{1,0:T(8,128)(2,1)S(1)}, u32[]{:S(2)}, u32[]{:S(2)}) collective-permute-start(bf16[64,2048]{1,0:T(8,128)(2,1)S(1)} %get-tuple-element.60), channel_id=1, source_target_pairs={{8,0},{10,2},{16,8},{18,10},{24,16},{26,18},{28,24},{30,26},{20,28... | collective-permute-start | bytes 786440 | tf_op jit(solution)/shard_map/ppermute | solution.py:191
  75.7 6.5 %collective-permute-start.21 = (bf16[64,2048]{1,0:T(8,128)(2,1)S(1)}, bf16[64,2048]{1,0:T(8,128)(2,1)S(1)}, u32[]{:S(2)}, u32[]{:S(2)}) collective-permute-start(bf16[64,2048]{1,0:T(8,128)(2,1)S(1)} %get-tuple-element.55), channel_id=1, source_target_pairs={{8,0},{10,2},{16,8},{18,10},{24,16},{26,18},{28,24},{30,26},{20,28... | collective-permute-start | bytes 786440 | tf_op jit(solution)/shard_map/ppermute | solution.py:191
  77.4 6.4 %collective-permute-start.28 = (bf16[64,2048]{1,0:T(8,128)(2,1)S(1)}, bf16[64,2048]{1,0:T(8,128)(2,1)S(1)}, u32[]{:S(2)}, u32[]{:S(2)}) collective-permute-start(bf16[64,2048]{1,0:T(8,128)(2,1)S(1)} %get-tuple-element.56), channel_id=1, source_target_pairs={{0,8},{2,10},{8,16},{10,18},{16,24},{18,26},{24,28},{26,30},{28,20... | collective-permute-start | bytes 786440 | tf_op jit(solution)/shard_map/ppermute | solution.py:191
  77.8 11.2 %collective-permute-start.15 = (bf16[128,2048]{1,0:T(8,128)(2,1)S(1)}, bf16[128,2048]{1,0:T(8,128)(2,1)S(1)}, u32[]{:S(2)}, u32[]{:S(2)}) collective-permute-start(bf16[128,2048]{1,0:T(8,128)(2,1)S(1)} %copy-done.4), channel_id=1, source_target_pairs={{0,1},{1,0},{2,3},{3,2},{4,5},{5,4},{6,7},{7,6},{8,9},{9,8},{10,11... | collective-permute-start | bytes 1572872 | tf_op jit(solution)/shard_map/ppermute | solution.py:17
  84.9 9.0 %collective-permute-start.18 = (bf16[64,2048]{1,0:T(8,128)(2,1)}, bf16[64,2048]{1,0:T(8,128)(2,1)S(1)}, u32[]{:S(2)}, u32[]{:S(2)}) collective-permute-start(bf16[64,2048]{1,0:T(8,128)(2,1)} %get-tuple-element.51), channel_id=1, source_target_pairs={{0,8},{2,10},{8,16},{10,18},{16,24},{18,26},{24,28},{26,30},{28,20... | collective-permute-start | bytes 786440 | tf_op jit(solution)/shard_map/ppermute | solution.py:191
  85.4 8.6 %collective-permute-start.22 = (bf16[64,2048]{1,0:T(8,128)(2,1)}, bf16[64,2048]{1,0:T(8,128)(2,1)}, u32[]{:S(2)}, u32[]{:S(2)}) collective-permute-start(bf16[64,2048]{1,0:T(8,128)(2,1)} %get-tuple-element.54), channel_id=1, source_target_pairs={{8,0},{10,2},{16,8},{18,10},{24,16},{26,18},{28,24},{30,26},{20,28... | collective-permute-start | bytes 786440 | tf_op jit(solution)/shard_map/ppermute | solution.py:191
  87.0 9.0 %collective-permute-start.25 = (bf16[64,2048]{1,0:T(8,128)(2,1)}, bf16[64,2048]{1,0:T(8,128)(2,1)}, u32[]{:S(2)}, u32[]{:S(2)}) collective-permute-start(bf16[64,2048]{1,0:T(8,128)(2,1)} %get-tuple-element.53), channel_id=1, source_target_pairs={{8,0},{10,2},{16,8},{18,10},{24,16},{26,18},{28,24},{30,26},{20,28... | collective-permute-start | bytes 786440 | tf_op jit(solution)/shard_map/ppermute | solution.py:191
  88.5 7.4 %collective-permute-start.29 = (bf16[64,2048]{1,0:T(8,128)(2,1)}, bf16[64,2048]{1,0:T(8,128)(2,1)}, u32[]{:S(2)}, u32[]{:S(2)}) collective-permute-start(bf16[64,2048]{1,0:T(8,128)(2,1)} %get-tuple-element.52), channel_id=1, source_target_pairs={{0,8},{2,10},{8,16},{10,18},{16,24},{18,26},{24,28},{26,30},{28,20... | collective-permute-start | bytes 786440 | tf_op jit(solution)/shard_map/ppermute | solution.py:191
  92.3 9.8 %collective-permute-start.16 = (bf16[128,2048]{1,0:T(8,128)(2,1)}, bf16[128,2048]{1,0:T(8,128)(2,1)}, u32[]{:S(2)}, u32[]{:S(2)}) collective-permute-start(bf16[128,2048]{1,0:T(8,128)(2,1)} %get-tuple-element.43), channel_id=1, source_target_pairs={{0,1},{1,0},{2,3},{3,2},{4,5},{5,4},{6,7},{7,6},{8,9},{9,8},{10,11... | collective-permute-start | bytes 1572872 | tf_op jit(solution)/shard_map/ppermute | solution.py:17
  98.0 6.7 %collective-permute-start.19 = (bf16[64,2048]{1,0:T(8,128)(2,1)S(1)}, bf16[64,2048]{1,0:T(8,128)(2,1)S(1)}, u32[]{:S(2)}, u32[]{:S(2)}) collective-permute-start(bf16[64,2048]{1,0:T(8,128)(2,1)S(1)} %get-tuple-element.47), channel_id=1, source_target_pairs={{0,8},{2,10},{8,16},{10,18},{16,24},{18,26},{24,28},{26,30},{28,20... | collective-permute-start | bytes 786440 | tf_op jit(solution)/shard_map/ppermute | solution.py:191
  99.3 6.9 %collective-permute-start.23 = (bf16[64,2048]{1,0:T(8,128)(2,1)S(1)}, bf16[64,2048]{1,0:T(8,128)(2,1)S(1)}, u32[]{:S(2)}, u32[]{:S(2)}) collective-permute-start(bf16[64,2048]{1,0:T(8,128)(2,1)S(1)} %get-tuple-element.50), channel_id=1, source_target_pairs={{8,0},{10,2},{16,8},{18,10},{24,16},{26,18},{28,24},{30,26},{20,28... | collective-permute-start | bytes 786440 | tf_op jit(solution)/shard_map/ppermute | solution.py:191
  100.0 9.0 %collective-permute-start.26 = (bf16[64,2048]{1,0:T(8,128)(2,1)S(1)}, bf16[64,2048]{1,0:T(8,128)(2,1)S(1)}, u32[]{:S(2)}, u32[]{:S(2)}) collective-permute-start(bf16[64,2048]{1,0:T(8,128)(2,1)S(1)} %get-tuple-element.49), channel_id=1, source_target_pairs={{8,0},{10,2},{16,8},{18,10},{24,16},{26,18},{28,24},{30,26},{20,28... | collective-permute-start | bytes 786440 | tf_op jit(solution)/shard_map/ppermute | solution.py:191
  101.6 7.4 %collective-permute-start.30 = (bf16[64,2048]{1,0:T(8,128)(2,1)S(1)}, bf16[64,2048]{1,0:T(8,128)(2,1)S(1)}, u32[]{:S(2)}, u32[]{:S(2)}) collective-permute-start(bf16[64,2048]{1,0:T(8,128)(2,1)S(1)} %get-tuple-element.48), channel_id=1, source_target_pairs={{0,8},{2,10},{8,16},{10,18},{16,24},{18,26},{24,28},{26,30},{28,20... | collective-permute-start | bytes 786440 | tf_op jit(solution)/shard_map/ppermute | solution.py:191

commit v5 on v4

--- a/solution.py
+++ b/solution.py
@@ -33,9 +33,9 @@
     return onward, [(target, source) for source, target in onward]
 
 
-def expert_kernel(parts, experts, features, kept_rows, tile, width, marks, owners_ref, *refs):
+def expert_kernel(parts, experts, features, tile, width, marks, owners_ref, *refs):
     refs = refs[marks:]
-    blocks, weights, (keep_ref, *send_ref), (inputs, scales, hidden) = (
+    blocks, weights, outs, (inputs, scales, hidden) = (
         refs[:parts],
         refs[parts : parts + experts],
         refs[parts + experts : -3],
@@ -79,9 +79,11 @@
                 hidden[expert], weights[expert][0, 2, :, some], preferred_element_type=jnp.float32
             )
             result = result + output * scales[expert]
-        keep_ref[:, some] = result[:kept_rows]
-        if send_ref:
-            send_ref[0][:, some] = result[kept_rows:].astype(jnp.bfloat16)
+        row = 0
+        for out in outs:
+            rows = out.shape[0]
+            out[:, some] = result[row : row + rows].astype(out.dtype)
+            row += rows
 
 
 def expert_apply(blocks, weights, owners, features, kept_rows, tile=256, width=512, after=None):
@@ -91,12 +93,14 @@
     units = weights[0].shape[2]
     tile = tile if units % tile == 0 else units
     whole = pl.BlockSpec(memory_space=pltpu.VMEM)
-    out_shape = [jax.ShapeDtypeStruct((kept_rows, features), jnp.float32)]
-    if rows > kept_rows:
-        out_shape.append(jax.ShapeDtypeStruct((rows - kept_rows, features), jnp.bfloat16))
+    out_shape, row = [], 0
+    for block in blocks:
+        out_type = jnp.float32 if row < kept_rows else jnp.bfloat16
+        out_shape.append(jax.ShapeDtypeStruct((block.shape[0], features), out_type))
+        row += block.shape[0]
     return pl.pallas_call(
         functools.partial(
-            expert_kernel, len(blocks), experts, features, kept_rows, tile, width, len(marks)
+            expert_kernel, len(blocks), experts, features, tile, width, len(marks)
         ),
         in_specs=[pl.BlockSpec(memory_space=pltpu.SMEM)]
         + [pl.BlockSpec(memory_space=pl.ANY)] * len(marks)
@@ -201,12 +205,12 @@
     long = move([bottom, top])
     other, staged = stage(go(cold_weights, across), cold_weights)
     pair = [cold_weights, other]
-    *both, staged = hold(*short, *long, staged)
+    *both, staged, own_tokens = hold(*short, *long, staged, tokens)
     short, long = both[:2], both[2:]
 
     def serve(blocks):
         kept = sum(block.shape[0] for block in blocks)
-        return expert_apply(blocks, pair, owners, features, kept, after=staged)[0]
+        return expert_apply(blocks, pair, owners, features, kept, after=staged)
 
     sums = {}
     for k in range(1, reach):
@@ -214,35 +218,35 @@
         if k < last:
             short = move(short)
         long = move(long)
-        both = serve(here)
-        *long, both = hold(*long, both)
-        sums["short", k], sums["long", k] = both[:rows], both[rows:]
-    both = serve(long + [top, bottom])
-    sums["long", reach], sums["own"] = both[:rows], both[rows:]
+        *long, first, second, third, fourth = hold(*long, *serve(here))
+        sums["short", k], sums["long", k] = [first, second], [third, fourth]
+    *sums["long", reach], own_top, own_bottom = serve(long + [top, bottom])
 
     def move_on(values):
         return [go(value.astype(jnp.bfloat16), way) for value, way in zip(values, (onward, backward))]
 
     def grow(moving, mine):
-        return move_on([mine[:half] + moving[0], mine[half:] + moving[1]])
-
-    short = move_on([sums["short", last][:half], sums["short", last][half:]])
-    long = move_on([sums["long", reach][:half], sums["long", reach][half:]])
+        return move_on([mine[0] + moving[0], mine[1] + moving[1]])
+
+    short = move_on(sums["short", last])
+    *short, first, second = hold(*short, *sums["long", reach])
+    long = move_on([first, second])
     for k in range(last, 0, -1):
         if k > 1:
             short = grow(short, sums["short", k - 1])
         long = grow(long, sums["long", k])
 
-    hot_blocks = [tokens] + [shifted(tokens, "expert", by) for by in range(1, groups)]
-    hot, hot_send = expert_apply(
+    hot_blocks = [own_tokens] + [shifted(own_tokens, "expert", by) for by in range(1, groups)]
+    hot, *hot_send = expert_apply(
         hot_blocks, [hot_weights], owners[1:], features, rows, tile=384
     )
     for by in range(1, groups):
-        hot = hot + shifted(hot_send[(by - 1) * rows : by * rows], "expert", -by)
-    (base,) = hold(sums["own"] + hot_gate * hot)
+        hot = hot + shifted(hot_send[by - 1], "expert", -by)
+    hot = hot_gate * hot
+    own_top, own_bottom = hold(own_top + hot[:half], own_bottom + hot[half:])
     combined = [
-        base[:half] + short[0].astype(jnp.float32) + long[1].astype(jnp.float32),
-        base[half:] + short[1].astype(jnp.float32) + long[0].astype(jnp.float32),
+        own_top + short[0].astype(jnp.float32) + long[1].astype(jnp.float32),
+        own_bottom + short[1].astype(jnp.float32) + long[0].astype(jnp.float32),
     ]
     return jnp.concatenate(combined, axis=0).astype(jnp.bfloat16)
 

time: 110 us -> 107 us (0.973)
  other arithmetic: 6.11 us -> 2.26 us
  local copies, waits for them, and re-layouts: 7.52 us -> 6.11 us
  starting transfers between devices: 34 us -> 35.2 us
  waiting for transfers between devices: 32 us -> 33.1 us
    convert_element_type x3 -> x14, other arithmetic: 3.34 us -> 0.62 us  [move_on(): value.astype(jnp.bfloat16)]
    unnamed x18 -> x16, local copies, waits for them, and re-layouts: 7.44 us -> 6.11 us
    ppermute x29, waiting for transfers between devices: 32 us -> 33.1 us  [go(): return lax.ppermute(block, 'dp', pairs)]
  transfers between devices with their start and end apart: 31 -> 31, of which waited for: 15 -> 10; matrix products, arithmetic and copies ran while one was open for 5% -> 1% of each run, Pallas kernels for 22% -> 28%
where the time goes in v5:
time: 107 us
  starting transfers between devices  35.2 us (33%)
  waiting for transfers between devices  33.1 us (31%)
  Pallas kernels  29.7 us (28%)
  local copies, waits for them, and re-layouts  6.11 us (6%)
  other arithmetic  2.26 us (2%)
    ppermute x29, waiting for transfers between devices, go(): return lax.ppermute(block, 'dp', pairs)  33.1 us
    ppermute x29, starting transfers between devices, go(): return lax.ppermute(block, 'dp', pairs)  31.3 us
    pallas_call x5, Pallas kernels, expert_apply(): pl.pallas_call(functools.partial(expert_kernel, len(blocks), experts, fea...  25.8 us
    unnamed x16, local copies, waits for them, and re-layouts  6.11 us
    ppermute x2, starting transfers between devices, shifted(): lax.ppermute(block, axis, [(i, (i + by) % size) for i in range(size)])  3.92 us
    pallas_call x1, Pallas kernels, stage(): pl.pallas_call(stage_kernel, in_specs=[pl.BlockSpec(memory_space=pl.ANY)]...  3.84 us
  transfers between devices with their start and end apart: 31, of which 10 were waited for; matrix products, arithmetic and copies ran while one was open for 1% of the time, Pallas kernels for 28%

profile of v5, /device:TPU:0, one launch (start us, length us, event | category | flops | bytes accessed | tf_op | source)
XLA Modules:
  0.0 106.7 jit_solution(9054735982790881672)
XLA Ops:
  0.0 0.5 collective-permute-start.4
  0.5 1.0 copy-done.2
  1.5 0.7 copy-done.4
  2.2 0.7 copy-done.5
  2.9 0.1 shard_map.55
  3.0 2.6 %collective-permute-start.3 = (bf16[64,2176]{1,0:T(8,128)(2,1)S(1)}, bf16[64,2176]{1,0:T(8,128)(2,1)S(1)}, u32[]{:S(2)}, u32[]{:S(2)}) collective-permute-start(bf16[64,2176]{1,0:T(8,128)(2,1)S(1)} %get-tuple-element.58.refs_3_), channel_id=1, source_target_pairs={{0,8},{2,10},{8,16},{10,18},{16,24},{18,26},{24,28},{26,30},{28,20... | collective-permute-start | bytes 835592 | tf_op jit(solution)/shard_map/ppermute | solution.py:195
  5.6 1.9 %collective-permute-start.2 = (bf16[64,2176]{1,0:T(8,128)(2,1)S(1)}, bf16[64,2176]{1,0:T(8,128)(2,1)S(1)}, u32[]{:S(2)}, u32[]{:S(2)}) collective-permute-start(bf16[64,2176]{1,0:T(8,128)(2,1)S(1)} %get-tuple-element.59.refs_4_), channel_id=1, source_target_pairs={{8,0},{10,2},{16,8},{18,10},{24,16},{26,18},{28,24},{30,26},{20,28... | collective-permute-start | bytes 835592 | tf_op jit(solution)/shard_map/ppermute | solution.py:195
  7.6 0.1 collective-permute-start.1
  7.7 0.1 reduce
  7.8 0.1 pad_add_fusion.1.owners_ref
  7.9 0.1 pad_add_fusion.owners_ref
  7.9 7.1 %collective-permute-done.4.source_ref = bf16[1,3,768,2048]{3,2,1,0:T(8,128)(2,1)} collective-permute-done((bf16[1,3,768,2048]{3,2,1,0:T(8,128)(2,1)}, bf16[1,3,768,2048]{3,2,1,0:T(8,128)(2,1)}, u32[]{:S(2)}, u32[]{:S(2)}) %collective-permute-start.4) | collective-permute-done | bytes 9437216 | tf_op jit(solution)/shard_map/ppermute | solution.py:195
  15.1 3.7 %copy-done = bf16[1,3,768,2048]{3,2,1,0:T(8,128)(2,1)S(1)} copy-done((bf16[1,3,768,2048]{3,2,1,0:T(8,128)(2,1)S(1)}, bf16[1,3,768,2048]{3,2,1,0:T(8,128)(2,1)}, u32[]{:S(2)}) %copy-start) | copy-done | bytes 9437208
  18.8 3.8 %shard_map.56 = (bf16[1,3,768,2048]{3,2,1,0:T(8,128)(2,1)S(1)}, f32[8,128]{1,0:T(8,128)S(1)}) custom-call(bf16[1,3,768,2048]{3,2,1,0:T(8,128)(2,1)} %collective-permute-done.4.source_ref, bf16[1,3,768,2048]{3,2,1,0:T(8,128)(2,1)S(1)} %copy-done), custom_call_target="tpu_custom_call" | custom-call | tf_op jit(solution)/shard_map/pallas_call | solution.py:132
  22.7 2.9 %collective-permute-start.5 = (bf16[64,2176]{1,0:T(8,128)(2,1)S(1)}, bf16[64,2176]{1,0:T(8,128)(2,1)S(1)}, u32[]{:S(2)}, u32[]{:S(2)}) collective-permute-start(bf16[64,2176]{1,0:T(8,128)(2,1)S(1)} %collective-permute-done.2.refs_3_), channel_id=1, source_target_pairs={{8,0},{10,2},{16,8},{18,10},{24,16},{26,18},{28,24},{30,26},{20,28... | collective-permute-start | bytes 835592 | tf_op jit(solution)/shard_map/ppermute | solution.py:195
  25.6 0.2 collective-permute-start.6
  25.7 1.9 %collective-permute-start.9 = (bf16[64,2176]{1,0:T(8,128)(2,1)S(1)}, bf16[64,2176]{1,0:T(8,128)(2,1)S(1)}, u32[]{:S(2)}, u32[]{:S(2)}) collective-permute-start(bf16[64,2176]{1,0:T(8,128)(2,1)S(1)} %collective-permute-done.refs_1_), channel_id=1, source_target_pairs={{8,0},{10,2},{16,8},{18,10},{24,16},{26,18},{28,24},{30,26},{20,28... | collective-permute-start | bytes 835592 | tf_op jit(solution)/shard_map/ppermute | solution.py:195
  27.6 0.2 collective-permute-start.10
  27.7 1.9 %collective-permute-start.15 = (bf16[128,2048]{1,0:T(8,128)(2,1)S(1)}, bf16[128,2048]{1,0:T(8,128)(2,1)S(1)}, u32[]{:S(2)}, u32[]{:S(2)}) collective-permute-start(bf16[128,2048]{1,0:T(8,128)(2,1)S(1)} %copy-done.3), channel_id=1, source_target_pairs={{0,1},{1,0},{2,3},{3,2},{4,5},{5,4},{6,7},{7,6},{8,9},{9,8},{10,11... | collective-permute-start | bytes 1572872 | tf_op jit(solution)/shard_map/ppermute | solution.py:17
  29.7 5.8 %shard_map.57 = (f32[64,2048]{1,0:T(8,128)S(1)}, f32[64,2048]{1,0:T(8,128)S(1)}, f32[64,2048]{1,0:T(8,128)S(1)}, f32[64,2048]{1,0:T(8,128)S(1)}) custom-call(s32[3]{0:T(128)S(1)} %pad_add_fusion.owners_ref, f32[8,128]{1,0:T(8,128)S(1)} %get-tuple-element.61.refs_0_, bf16[64,2176]{1,0:T(8,128)(2,1)S(1)} %collective-permute-done.refs_1_, ...), custom_call_target="tpu_custom_call" | custom-call | flops 4831838208 | bytes 23068672 | tf_op jit(solution)/shard_map/pallas_call | solution.py:101
  35.5 0.0 slice-start
  35.5 1.5 %collective-permute-start.7 = (bf16[64,2176]{1,0:T(8,128)(2,1)S(1)}, bf16[64,2176]{1,0:T(8,128)(2,1)S(1)}, u32[]{:S(2)}, u32[]{:S(2)}) collective-permute-start(bf16[64,2176]{1,0:T(8,128)(2,1)S(1)} %collective-permute-done.5.refs_3_), channel_id=1, source_target_pairs={{8,0},{10,2},{16,8},{18,10},{24,16},{26,18},{28,24},{30,26},{20,28... | collective-permute-start | bytes 835592 | tf_op jit(solution)/shard_map/ppermute | solution.py:195
  37.1 0.5 collective-permute-start.8
  37.6 1.4 %collective-permute-done.9.refs_1_ = bf16[64,2176]{1,0:T(8,128)(2,1)S(1)} collective-permute-done((bf16[64,2176]{1,0:T(8,128)(2,1)S(1)}, bf16[64,2176]{1,0:T(8,128)(2,1)S(1)}, u32[]{:S(2)}, u32[]{:S(2)}) %collective-permute-start.9) | collective-permute-done | bytes 278560 | tf_op jit(solution)/shard_map/ppermute | solution.py:195
  39.1 2.0 %collective-permute-start.13 = (bf16[64,2176]{1,0:T(8,128)(2,1)S(1)}, bf16[64,2176]{1,0:T(8,128)(2,1)S(1)}, u32[]{:S(2)}, u32[]{:S(2)}) collective-permute-start(bf16[64,2176]{1,0:T(8,128)(2,1)S(1)} %collective-permute-done.9.refs_1_), channel_id=1, source_target_pairs={{8,0},{10,2},{16,8},{18,10},{24,16},{26,18},{28,24},{30,26},{20,28... | collective-permute-start | bytes 835592 | tf_op jit(solution)/shard_map/ppermute | solution.py:195
  41.0 0.0 collective-permute-done.10.refs_2_
  41.1 0.1 collective-permute-start.14
  41.2 5.8 %shard_map.58 = (f32[64,2048]{1,0:T(8,128)S(1)}, f32[64,2048]{1,0:T(8,128)S(1)}, f32[64,2048]{1,0:T(8,128)S(1)}, f32[64,2048]{1,0:T(8,128)S(1)}) custom-call(s32[3]{0:T(128)S(1)} %pad_add_fusion.owners_ref, f32[8,128]{1,0:T(8,128)S(1)} %get-tuple-element.61.refs_0_, bf16[64,2176]{1,0:T(8,128)(2,1)S(1)} %collective-permute-done.9.refs_1_, ...), custom_call_target="tpu_custom_call" | custom-call | flops 4831838208 | bytes 23068672 | tf_op jit(solution)/shard_map/pallas_call | solution.py:101
  47.1 2.4 %shard_map.61 = (f32[128,2048]{1,0:T(8,128)S(1)}, bf16[128,2048]{1,0:T(8,128)(2,1)S(1)}) custom-call(s32[2]{0:T(128)S(1)} %pad_add_fusion.1.owners_ref, bf16[128,2048]{1,0:T(8,128)(2,1)S(1)} %copy-done.3, bf16[128,2048]{1,0:T(8,128)(2,1)S(1)} %collective-permute-done.15.refs_1_, bf16[1,3,384,2048]{3,2,1,0:T(8,128)(2,1)S(1)} %bitcast.5), custom_call_target="tpu_custom_call" | custom-call | flops 1207959552 | bytes 8912896 | tf_op jit(solution)/shard_map/pallas_call | solution.py:101
  49.5 2.0 %collective-permute-start.16 = (bf16[128,2048]{1,0:T(8,128)(2,1)S(1)}, bf16[128,2048]{1,0:T(8,128)(2,1)S(1)}, u32[]{:S(2)}, u32[]{:S(2)}) collective-permute-start(bf16[128,2048]{1,0:T(8,128)(2,1)S(1)} %get-tuple-element.89), channel_id=1, source_target_pairs={{0,1},{1,0},{2,3},{3,2},{4,5},{5,4},{6,7},{7,6},{8,9},{9,8},{10,11... | collective-permute-start | bytes 1572872 | tf_op jit(solution)/shard_map/ppermute | solution.py:17
  51.5 1.5 %collective-permute-start.11 = (bf16[64,2176]{1,0:T(8,128)(2,1)S(1)}, bf16[64,2176]{1,0:T(8,128)(2,1)S(1)}, u32[]{:S(2)}, u32[]{:S(2)}) collective-permute-start(bf16[64,2176]{1,0:T(8,128)(2,1)S(1)} %collective-permute-done.7.refs_3_), channel_id=1, source_target_pairs={{8,0},{10,2},{16,8},{18,10},{24,16},{26,18},{28,24},{30,26},{20,28... | collective-permute-start | bytes 835592 | tf_op jit(solution)/shard_map/ppermute | solution.py:195
  53.0 0.5 collective-permute-start.12
  53.6 5.8 %shard_map.59 = (f32[64,2048]{1,0:T(8,128)S(1)}, f32[64,2048]{1,0:T(8,128)S(1)}, f32[64,2048]{1,0:T(8,128)S(1)}, f32[64,2048]{1,0:T(8,128)S(1)}) custom-call(s32[3]{0:T(128)S(1)} %pad_add_fusion.owners_ref, f32[8,128]{1,0:T(8,128)S(1)} %get-tuple-element.61.refs_0_, bf16[64,2176]{1,0:T(8,128)(2,1)S(1)} %collective-permute-done.13.refs_1_, ...), custom_call_target="tpu_custom_call" | custom-call | flops 4831838208 | bytes 23068672 | tf_op jit(solution)/shard_map/pallas_call | solution.py:101
  59.4 0.1 collective-permute-done.12.refs_2_
  59.6 1.6 %collective-permute-start.18 = (bf16[64,2048]{1,0:T(8,128)(2,1)S(1)}, bf16[64,2048]{1,0:T(8,128)(2,1)S(1)}, u32[]{:S(2)}, u32[]{:S(2)}) collective-permute-start(bf16[64,2048]{1,0:T(8,128)(2,1)S(1)} %convert_element_type.90), channel_id=1, source_target_pairs={{8,0},{10,2},{16,8},{18,10},{24,16},{26,18},{28,24},{30,26},{20,28... | collective-permute-start | bytes 786440 | tf_op jit(solution)/shard_map/ppermute | solution.py:195
  61.3 0.5 collective-permute-start.17
  61.7 5.8 %shard_map.60 = (f32[64,2048]{1,0:T(8,128)S(1)}, f32[64,2048]{1,0:T(8,128)S(1)}, f32[64,2048]{1,0:T(8,128)S(1)}, f32[64,2048]{1,0:T(8,128)S(1)}) custom-call(s32[3]{0:T(128)S(1)} %pad_add_fusion.owners_ref, f32[8,128]{1,0:T(8,128)S(1)} %get-tuple-element.61.refs_0_, bf16[64,2176]{1,0:T(8,128)(2,1)S(1)} %collective-permute-done.11.refs_1_, ...), custom_call_target="tpu_custom_call" | custom-call | flops 4831838208 | bytes 23068672 | tf_op jit(solution)/shard_map/pallas_call | solution.py:101
  67.6 0.2 add_multiply_fusion
  67.8 0.1 slice_add_fusion
  67.9 0.0 collective-permute-done.17
  68.0 1.5 %collective-permute-start.27 = (bf16[64,2048]{1,0:T(8,128)(2,1)S(1)}, bf16[64,2048]{1,0:T(8,128)(2,1)S(1)}, u32[]{:S(2)}, u32[]{:S(2)}) collective-permute-start(bf16[64,2048]{1,0:T(8,128)(2,1)S(1)} %convert_element_type.109), channel_id=1, source_target_pairs={{0,8},{2,10},{8,16},{10,18},{16,24},{18,26},{24,28},{26,30},{28,20... | collective-permute-start | bytes 786440 | tf_op jit(solution)/shard_map/ppermute | solution.py:195
  69.5 0.6 collective-permute-start.21
  70.1 0.1 add_convert_fusion.11
  70.2 1.5 %collective-permute-start.19 = (bf16[64,2048]{1,0:T(8,128)(2,1)S(1)}, bf16[64,2048]{1,0:T(8,128)(2,1)S(1)}, u32[]{:S(2)}, u32[]{:S(2)}) collective-permute-start(bf16[64,2048]{1,0:T(8,128)(2,1)S(1)} %add_convert_fusion.11), channel_id=1, source_target_pairs={{0,8},{2,10},{8,16},{10,18},{16,24},{18,26},{24,28},{26,30},{28,20... | collective-permute-start | bytes 786440 | tf_op jit(solution)/shard_map/ppermute | solution.py:195
  71.7 0.6 collective-permute-start.25
  72.4 5.0 %collective-permute-done.27 = bf16[64,2048]{1,0:T(8,128)(2,1)S(1)} collective-permute-done((bf16[64,2048]{1,0:T(8,128)(2,1)S(1)}, bf16[64,2048]{1,0:T(8,128)(2,1)S(1)}, u32[]{:S(2)}, u32[]{:S(2)}) %collective-permute-start.27) | collective-permute-done | bytes 262176 | tf_op jit(solution)/shard_map/ppermute | solution.py:195
  77.4 1.5 %collective-permute-start.28 = (bf16[64,2048]{1,0:T(8,128)(2,1)S(1)}, bf16[64,2048]{1,0:T(8,128)(2,1)S(1)}, u32[]{:S(2)}, u32[]{:S(2)}) collective-permute-start(bf16[64,2048]{1,0:T(8,128)(2,1)S(1)} %add_convert_fusion.3), channel_id=1, source_target_pairs={{0,8},{2,10},{8,16},{10,18},{16,24},{18,26},{24,28},{26,30},{28,20... | collective-permute-start | bytes 786440 | tf_op jit(solution)/shard_map/ppermute | solution.py:195
  78.9 0.1 add_convert_fusion.9
  78.9 0.6 collective-permute-start.22
  79.6 3.4 %collective-permute-done.19 = bf16[64,2048]{1,0:T(8,128)(2,1)S(1)} collective-permute-done((bf16[64,2048]{1,0:T(8,128)(2,1)S(1)}, bf16[64,2048]{1,0:T(8,128)(2,1)S(1)}, u32[]{:S(2)}, u32[]{:S(2)}) %collective-permute-start.19) | collective-permute-done | bytes 262176 | tf_op jit(solution)/shard_map/ppermute | solution.py:195
  83.0 1.5 %collective-permute-start.20 = (bf16[64,2048]{1,0:T(8,128)(2,1)S(1)}, bf16[64,2048]{1,0:T(8,128)(2,1)S(1)}, u32[]{:S(2)}, u32[]{:S(2)}) collective-permute-start(bf16[64,2048]{1,0:T(8,128)(2,1)S(1)} %add_convert_fusion.10), channel_id=1, source_target_pairs={{0,8},{2,10},{8,16},{10,18},{16,24},{18,26},{24,28},{26,30},{28,20... | collective-permute-start | bytes 786440 | tf_op jit(solution)/shard_map/ppermute | solution.py:195
  84.5 0.6 collective-permute-start.26
  85.2 4.8 %collective-permute-done.22 = bf16[64,2048]{1,0:T(8,128)(2,1)S(1)} collective-permute-done((bf16[64,2048]{1,0:T(8,128)(2,1)S(1)}, bf16[64,2048]{1,0:T(8,128)(2,1)S(1)}, u32[]{:S(2)}, u32[]{:S(2)}) %collective-permute-start.22) | collective-permute-done | bytes 262176 | tf_op jit(solution)/shard_map/ppermute | solution.py:195
  90.1 0.6 collective-permute-start.23
  90.7 1.5 %collective-permute-start.29 = (bf16[64,2048]{1,0:T(8,128)(2,1)S(1)}, bf16[64,2048]{1,0:T(8,128)(2,1)S(1)}, u32[]{:S(2)}, u32[]{:S(2)}) collective-permute-start(bf16[64,2048]{1,0:T(8,128)(2,1)S(1)} %add_convert_fusion.2), channel_id=1, source_target_pairs={{0,8},{2,10},{8,16},{10,18},{16,24},{18,26},{24,28},{26,30},{28,20... | collective-permute-start | bytes 786440 | tf_op jit(solution)/shard_map/ppermute | solution.py:195
  92.2 6.3 %collective-permute-done.23 = bf16[64,2048]{1,0:T(8,128)(2,1)S(1)} collective-permute-done((bf16[64,2048]{1,0:T(8,128)(2,1)S(1)}, bf16[64,2048]{1,0:T(8,128)(2,1)S(1)}, u32[]{:S(2)}, u32[]{:S(2)}) %collective-permute-start.23) | collective-permute-done | bytes 262176 | tf_op jit(solution)/shard_map/ppermute | solution.py:195
  98.6 0.5 collective-permute-start.24
  99.0 0.3 collective-permute-done.29
  99.4 1.7 %collective-permute-start.30 = (bf16[64,2048]{1,0:T(8,128)(2,1)S(1)}, bf16[64,2048]{1,0:T(8,128)(2,1)S(1)}, u32[]{:S(2)}, u32[]{:S(2)}) collective-permute-start(bf16[64,2048]{1,0:T(8,128)(2,1)S(1)} %add_convert_fusion.1), channel_id=1, source_target_pairs={{0,8},{2,10},{8,16},{10,18},{16,24},{18,26},{24,28},{26,30},{28,20... | collective-permute-start | bytes 786440 | tf_op jit(solution)/shard_map/ppermute | solution.py:195
  101.1 3.9 %collective-permute-done.24 = bf16[64,2048]{1,0:T(8,128)(2,1)S(1)} collective-permute-done((bf16[64,2048]{1,0:T(8,128)(2,1)S(1)}, bf16[64,2048]{1,0:T(8,128)(2,1)S(1)}, u32[]{:S(2)}, u32[]{:S(2)}) %collective-permute-start.24) | collective-permute-done | bytes 262176 | tf_op jit(solution)/shard_map/ppermute | solution.py:195
  105.0 0.1 add_convert_fusion.6
  105.1 0.7 collective-permute-done.30
  105.8 0.1 add_convert_fusion
  105.9 0.8 pad_maximum_fusion
  (44 shorter events, 0.6 us)
Async XLA Ops:
  0.0 15.1 %collective-permute-start.4 = (bf16[1,3,768,2048]{3,2,1,0:T(8,128)(2,1)}, bf16[1,3,768,2048]{3,2,1,0:T(8,128)(2,1)}, u32[]{:S(2)}, u32[]{:S(2)}) collective-permute-start(bf16[1,3,768,2048]{3,2,1,0:T(8,128)(2,1)} %refs_5_.7), channel_id=1, source_target_pairs={{0,2},{2,0},{4,6},{6,4},{8,10},{10,8},{12,14},{14,12},{16,18},{18,... | collective-permute-start | bytes 28311560 | tf_op jit(solution)/shard_map/ppermute | solution.py:195
  0.5 1.0 copy-start.2
  1.5 0.7 copy-start.4
  2.2 0.7 copy-start.5
  3.0 19.6 %collective-permute-start.3 = (bf16[64,2176]{1,0:T(8,128)(2,1)S(1)}, bf16[64,2176]{1,0:T(8,128)(2,1)S(1)}, u32[]{:S(2)}, u32[]{:S(2)}) collective-permute-start(bf16[64,2176]{1,0:T(8,128)(2,1)S(1)} %get-tuple-element.58.refs_3_), channel_id=1, source_target_pairs={{0,8},{2,10},{8,16},{10,18},{16,24},{18,26},{24,28},{26,30},{28,20... | collective-permute-start | bytes 835592 | tf_op jit(solution)/shard_map/ppermute | solution.py:195
  5.6 17.0 %collective-permute-start = (bf16[64,2176]{1,0:T(8,128)(2,1)S(1)}, bf16[64,2176]{1,0:T(8,128)(2,1)S(1)}, u32[]{:S(2)}, u32[]{:S(2)}) collective-permute-start(bf16[64,2176]{1,0:T(8,128)(2,1)S(1)} %get-tuple-element.58.refs_3_), channel_id=1, source_target_pairs={{8,0},{10,2},{16,8},{18,10},{24,16},{26,18},{28,24},{30,26},{20,28... | collective-permute-start | bytes 835592 | tf_op jit(solution)/shard_map/ppermute | solution.py:195
  5.6 17.0 %collective-permute-start.2 = (bf16[64,2176]{1,0:T(8,128)(2,1)S(1)}, bf16[64,2176]{1,0:T(8,128)(2,1)S(1)}, u32[]{:S(2)}, u32[]{:S(2)}) collective-permute-start(bf16[64,2176]{1,0:T(8,128)(2,1)S(1)} %get-tuple-element.59.refs_4_), channel_id=1, source_target_pairs={{8,0},{10,2},{16,8},{18,10},{24,16},{26,18},{28,24},{30,26},{20,28... | collective-permute-start | bytes 835592 | tf_op jit(solution)/shard_map/ppermute | solution.py:195
  7.6 15.1 %collective-permute-start.1 = (bf16[64,2176]{1,0:T(8,128)(2,1)S(1)}, bf16[64,2176]{1,0:T(8,128)(2,1)S(1)}, u32[]{:S(2)}, u32[]{:S(2)}) collective-permute-start(bf16[64,2176]{1,0:T(8,128)(2,1)S(1)} %get-tuple-element.59.refs_4_), channel_id=1, source_target_pairs={{0,8},{2,10},{8,16},{10,18},{16,24},{18,26},{24,28},{26,30},{28,20... | collective-permute-start | bytes 835592 | tf_op jit(solution)/shard_map/ppermute | solution.py:195
  15.1 3.7 %copy-start = (bf16[1,3,768,2048]{3,2,1,0:T(8,128)(2,1)S(1)}, bf16[1,3,768,2048]{3,2,1,0:T(8,128)(2,1)}, u32[]{:S(2)}) copy-start(bf16[1,3,768,2048]{3,2,1,0:T(8,128)(2,1)} %refs_5_.7) | copy-start | bytes 28311556
  18.8 9.0 %copy-start.3 = (bf16[128,2048]{1,0:T(8,128)(2,1)S(1)}, bf16[128,2048]{1,0:T(8,128)(2,1)}, u32[]{:S(2)}) copy-start(bf16[128,2048]{1,0:T(8,128)(2,1)} %refs_0_) | copy-start | bytes 1572868
  18.8 10.9 %copy-start.1 = (bf16[1,3,768,2048]{3,2,1,0:T(8,128)(2,1)S(1)}, bf16[1,3,768,2048]{3,2,1,0:T(8,128)(2,1)}, u32[]{:S(2)}) copy-start(bf16[1,3,768,2048]{3,2,1,0:T(8,128)(2,1)} %refs_5_.7) | copy-start | bytes 28311556
  22.7 12.8 %collective-permute-start.5 = (bf16[64,2176]{1,0:T(8,128)(2,1)S(1)}, bf16[64,2176]{1,0:T(8,128)(2,1)S(1)}, u32[]{:S(2)}, u32[]{:S(2)}) collective-permute-start(bf16[64,2176]{1,0:T(8,128)(2,1)S(1)} %collective-permute-done.2.refs_3_), channel_id=1, source_target_pairs={{8,0},{10,2},{16,8},{18,10},{24,16},{26,18},{28,24},{30,26},{20,28... | collective-permute-start | bytes 835592 | tf_op jit(solution)/shard_map/ppermute | solution.py:195
  25.6 9.9 %collective-permute-start.6 = (bf16[64,2176]{1,0:T(8,128)(2,1)S(1)}, bf16[64,2176]{1,0:T(8,128)(2,1)S(1)}, u32[]{:S(2)}, u32[]{:S(2)}) collective-permute-start(bf16[64,2176]{1,0:T(8,128)(2,1)S(1)} %collective-permute-done.3.refs_4_), channel_id=1, source_target_pairs={{0,8},{2,10},{8,16},{10,18},{16,24},{18,26},{24,28},{26,30},{28,20... | collective-permute-start | bytes 835592 | tf_op jit(solution)/shard_map/ppermute | solution.py:195
  25.7 13.3 %collective-permute-start.9 = (bf16[64,2176]{1,0:T(8,128)(2,1)S(1)}, bf16[64,2176]{1,0:T(8,128)(2,1)S(1)}, u32[]{:S(2)}, u32[]{:S(2)}) collective-permute-start(bf16[64,2176]{1,0:T(8,128)(2,1)S(1)} %collective-permute-done.refs_1_), channel_id=1, source_target_pairs={{8,0},{10,2},{16,8},{18,10},{24,16},{26,18},{28,24},{30,26},{20,28... | collective-permute-start | bytes 835592 | tf_op jit(solution)/shard_map/ppermute | solution.py:195
  27.6 13.5 %collective-permute-start.10 = (bf16[64,2176]{1,0:T(8,128)(2,1)S(1)}, bf16[64,2176]{1,0:T(8,128)(2,1)S(1)}, u32[]{:S(2)}, u32[]{:S(2)}) collective-permute-start(bf16[64,2176]{1,0:T(8,128)(2,1)S(1)} %collective-permute-done.1.refs_2_), channel_id=1, source_target_pairs={{0,8},{2,10},{8,16},{10,18},{16,24},{18,26},{24,28},{26,30},{28,20... | collective-permute-start | bytes 835592 | tf_op jit(solution)/shard_map/ppermute | solution.py:195
  27.7 19.3 %collective-permute-start.15 = (bf16[128,2048]{1,0:T(8,128)(2,1)S(1)}, bf16[128,2048]{1,0:T(8,128)(2,1)S(1)}, u32[]{:S(2)}, u32[]{:S(2)}) collective-permute-start(bf16[128,2048]{1,0:T(8,128)(2,1)S(1)} %copy-done.3), channel_id=1, source_target_pairs={{0,1},{1,0},{2,3},{3,2},{4,5},{5,4},{6,7},{7,6},{8,9},{9,8},{10,11... | collective-permute-start | bytes 1572872 | tf_op jit(solution)/shard_map/ppermute | solution.py:17
  35.5 11.5 %slice-start = ((s8[4718592]{0:T(1024)(128)(4,1)}), s8[4194304]{0:T(1024)(128)(4,1)S(1)}, s32[]{:S(2)}) async-start(s8[4718592]{0:T(1024)(128)(4,1)} %bitcast.4), calls=%async_computation | async-start | bytes 8388608
  35.5 11.5 %slice-start.1 = ((s8[4718592]{0:T(1024)(128)(4,1)}), s8[524288]{0:T(1024)(128)(4,1)S(1)}, s32[]{:S(2)}) async-start(s8[4718592]{0:T(1024)(128)(4,1)} %bitcast.4), calls=%async_computation.1 | async-start | bytes 1048576
  35.5 16.0 %collective-permute-start.7 = (bf16[64,2176]{1,0:T(8,128)(2,1)S(1)}, bf16[64,2176]{1,0:T(8,128)(2,1)S(1)}, u32[]{:S(2)}, u32[]{:S(2)}) collective-permute-start(bf16[64,2176]{1,0:T(8,128)(2,1)S(1)} %collective-permute-done.5.refs_3_), channel_id=1, source_target_pairs={{8,0},{10,2},{16,8},{18,10},{24,16},{26,18},{28,24},{30,26},{20,28... | collective-permute-start | bytes 835592 | tf_op jit(solution)/shard_map/ppermute | solution.py:195
  37.1 14.5 %collective-permute-start.8 = (bf16[64,2176]{1,0:T(8,128)(2,1)S(1)}, bf16[64,2176]{1,0:T(8,128)(2,1)S(1)}, u32[]{:S(2)}, u32[]{:S(2)}) collective-permute-start(bf16[64,2176]{1,0:T(8,128)(2,1)S(1)} %collective-permute-done.6.refs_4_), channel_id=1, source_target_pairs={{0,8},{2,10},{8,16},{10,18},{16,24},{18,26},{24,28},{26,30},{28,20... | collective-permute-start | bytes 835592 | tf_op jit(solution)/shard_map/ppermute | solution.py:195
  39.1 14.5 %collective-permute-start.13 = (bf16[64,2176]{1,0:T(8,128)(2,1)S(1)}, bf16[64,2176]{1,0:T(8,128)(2,1)S(1)}, u32[]{:S(2)}, u32[]{:S(2)}) collective-permute-start(bf16[64,2176]{1,0:T(8,128)(2,1)S(1)} %collective-permute-done.9.refs_1_), channel_id=1, source_target_pairs={{8,0},{10,2},{16,8},{18,10},{24,16},{26,18},{28,24},{30,26},{20,28... | collective-permute-start | bytes 835592 | tf_op jit(solution)/shard_map/ppermute | solution.py:195
  41.1 12.5 %collective-permute-start.14 = (bf16[64,2176]{1,0:T(8,128)(2,1)S(1)}, bf16[64,2176]{1,0:T(8,128)(2,1)S(1)}, u32[]{:S(2)}, u32[]{:S(2)}) collective-permute-start(bf16[64,2176]{1,0:T(8,128)(2,1)S(1)} %collective-permute-done.10.refs_2_), channel_id=1, source_target_pairs={{0,8},{2,10},{8,16},{10,18},{16,24},{18,26},{24,28},{26,30},{28,20... | collective-permute-start | bytes 835592 | tf_op jit(solution)/shard_map/ppermute | solution.py:195
  49.5 18.1 %collective-permute-start.16 = (bf16[128,2048]{1,0:T(8,128)(2,1)S(1)}, bf16[128,2048]{1,0:T(8,128)(2,1)S(1)}, u32[]{:S(2)}, u32[]{:S(2)}) collective-permute-start(bf16[128,2048]{1,0:T(8,128)(2,1)S(1)} %get-tuple-element.89), channel_id=1, source_target_pairs={{0,1},{1,0},{2,3},{3,2},{4,5},{5,4},{6,7},{7,6},{8,9},{9,8},{10,11... | collective-permute-start | bytes 1572872 | tf_op jit(solution)/shard_map/ppermute | solution.py:17
  51.5 7.9 %collective-permute-start.11 = (bf16[64,2176]{1,0:T(8,128)(2,1)S(1)}, bf16[64,2176]{1,0:T(8,128)(2,1)S(1)}, u32[]{:S(2)}, u32[]{:S(2)}) collective-permute-start(bf16[64,2176]{1,0:T(8,128)(2,1)S(1)} %collective-permute-done.7.refs_3_), channel_id=1, source_target_pairs={{8,0},{10,2},{16,8},{18,10},{24,16},{26,18},{28,24},{30,26},{20,28... | collective-permute-start | bytes 835592 | tf_op jit(solution)/shard_map/ppermute | solution.py:195
  53.0 6.5 %collective-permute-start.12 = (bf16[64,2176]{1,0:T(8,128)(2,1)S(1)}, bf16[64,2176]{1,0:T(8,128)(2,1)S(1)}, u32[]{:S(2)}, u32[]{:S(2)}) collective-permute-start(bf16[64,2176]{1,0:T(8,128)(2,1)S(1)} %collective-permute-done.8.refs_4_), channel_id=1, source_target_pairs={{0,8},{2,10},{8,16},{10,18},{16,24},{18,26},{24,28},{26,30},{28,20... | collective-permute-start | bytes 835592 | tf_op jit(solution)/shard_map/ppermute | solution.py:195
  59.6 8.3 %collective-permute-start.18 = (bf16[64,2048]{1,0:T(8,128)(2,1)S(1)}, bf16[64,2048]{1,0:T(8,128)(2,1)S(1)}, u32[]{:S(2)}, u32[]{:S(2)}) collective-permute-start(bf16[64,2048]{1,0:T(8,128)(2,1)S(1)} %convert_element_type.90), channel_id=1, source_target_pairs={{8,0},{10,2},{16,8},{18,10},{24,16},{26,18},{28,24},{30,26},{20,28... | collective-permute-start | bytes 786440 | tf_op jit(solution)/shard_map/ppermute | solution.py:195
  61.3 6.7 %collective-permute-start.17 = (bf16[64,2048]{1,0:T(8,128)(2,1)S(1)}, bf16[64,2048]{1,0:T(8,128)(2,1)S(1)}, u32[]{:S(2)}, u32[]{:S(2)}) collective-permute-start(bf16[64,2048]{1,0:T(8,128)(2,1)S(1)} %convert_element_type.89), channel_id=1, source_target_pairs={{0,8},{2,10},{8,16},{10,18},{16,24},{18,26},{24,28},{26,30},{28,20... | collective-permute-start | bytes 786440 | tf_op jit(solution)/shard_map/ppermute | solution.py:195
  68.0 9.3 %collective-permute-start.27 = (bf16[64,2048]{1,0:T(8,128)(2,1)S(1)}, bf16[64,2048]{1,0:T(8,128)(2,1)S(1)}, u32[]{:S(2)}, u32[]{:S(2)}) collective-permute-start(bf16[64,2048]{1,0:T(8,128)(2,1)S(1)} %convert_element_type.109), channel_id=1, source_target_pairs={{0,8},{2,10},{8,16},{10,18},{16,24},{18,26},{24,28},{26,30},{28,20... | collective-permute-start | bytes 786440 | tf_op jit(solution)/shard_map/ppermute | solution.py:195
  69.5 9.4 %collective-permute-start.21 = (bf16[64,2048]{1,0:T(8,128)(2,1)S(1)}, bf16[64,2048]{1,0:T(8,128)(2,1)S(1)}, u32[]{:S(2)}, u32[]{:S(2)}) collective-permute-start(bf16[64,2048]{1,0:T(8,128)(2,1)S(1)} %convert_element_type.96), channel_id=1, source_target_pairs={{8,0},{10,2},{16,8},{18,10},{24,16},{26,18},{28,24},{30,26},{20,28... | collective-permute-start | bytes 786440 | tf_op jit(solution)/shard_map/ppermute | solution.py:195
  70.2 12.8 %collective-permute-start.19 = (bf16[64,2048]{1,0:T(8,128)(2,1)S(1)}, bf16[64,2048]{1,0:T(8,128)(2,1)S(1)}, u32[]{:S(2)}, u32[]{:S(2)}) collective-permute-start(bf16[64,2048]{1,0:T(8,128)(2,1)S(1)} %add_convert_fusion.11), channel_id=1, source_target_pairs={{0,8},{2,10},{8,16},{10,18},{16,24},{18,26},{24,28},{26,30},{28,20... | collective-permute-start | bytes 786440 | tf_op jit(solution)/shard_map/ppermute | solution.py:195
  71.7 12.8 %collective-permute-start.25 = (bf16[64,2048]{1,0:T(8,128)(2,1)S(1)}, bf16[64,2048]{1,0:T(8,128)(2,1)S(1)}, u32[]{:S(2)}, u32[]{:S(2)}) collective-permute-start(bf16[64,2048]{1,0:T(8,128)(2,1)S(1)} %add_convert_fusion.5), channel_id=1, source_target_pairs={{8,0},{10,2},{16,8},{18,10},{24,16},{26,18},{28,24},{30,26},{20,28... | collective-permute-start | bytes 786440 | tf_op jit(solution)/shard_map/ppermute | solution.py:195
  77.4 13.3 %collective-permute-start.28 = (bf16[64,2048]{1,0:T(8,128)(2,1)S(1)}, bf16[64,2048]{1,0:T(8,128)(2,1)S(1)}, u32[]{:S(2)}, u32[]{:S(2)}) collective-permute-start(bf16[64,2048]{1,0:T(8,128)(2,1)S(1)} %add_convert_fusion.3), channel_id=1, source_target_pairs={{0,8},{2,10},{8,16},{10,18},{16,24},{18,26},{24,28},{26,30},{28,20... | collective-permute-start | bytes 786440 | tf_op jit(solution)/shard_map/ppermute | solution.py:195
  78.9 11.1 %collective-permute-start.22 = (bf16[64,2048]{1,0:T(8,128)(2,1)S(1)}, bf16[64,2048]{1,0:T(8,128)(2,1)S(1)}, u32[]{:S(2)}, u32[]{:S(2)}) collective-permute-start(bf16[64,2048]{1,0:T(8,128)(2,1)S(1)} %add_convert_fusion.9), channel_id=1, source_target_pairs={{8,0},{10,2},{16,8},{18,10},{24,16},{26,18},{28,24},{30,26},{20,28... | collective-permute-start | bytes 786440 | tf_op jit(solution)/shard_map/ppermute | solution.py:195
  83.0 18.1 %collective-permute-start.20 = (bf16[64,2048]{1,0:T(8,128)(2,1)S(1)}, bf16[64,2048]{1,0:T(8,128)(2,1)S(1)}, u32[]{:S(2)}, u32[]{:S(2)}) collective-permute-start(bf16[64,2048]{1,0:T(8,128)(2,1)S(1)} %add_convert_fusion.10), channel_id=1, source_target_pairs={{0,8},{2,10},{8,16},{10,18},{16,24},{18,26},{24,28},{26,30},{28,20... | collective-permute-start | bytes 786440 | tf_op jit(solution)/shard_map/ppermute | solution.py:195
  84.5 20.6 %collective-permute-start.26 = (bf16[64,2048]{1,0:T(8,128)(2,1)S(1)}, bf16[64,2048]{1,0:T(8,128)(2,1)S(1)}, u32[]{:S(2)}, u32[]{:S(2)}) collective-permute-start(bf16[64,2048]{1,0:T(8,128)(2,1)S(1)} %add_convert_fusion.4), channel_id=1, source_target_pairs={{8,0},{10,2},{16,8},{18,10},{24,16},{26,18},{28,24},{30,26},{20,28... | collective-permute-start | bytes 786440 | tf_op jit(solution)/shard_map/ppermute | solution.py:195
  90.1 8.5 %collective-permute-start.23 = (bf16[64,2048]{1,0:T(8,128)(2,1)S(1)}, bf16[64,2048]{1,0:T(8,128)(2,1)S(1)}, u32[]{:S(2)}, u32[]{:S(2)}) collective-permute-start(bf16[64,2048]{1,0:T(8,128)(2,1)S(1)} %add_convert_fusion.8), channel_id=1, source_target_pairs={{8,0},{10,2},{16,8},{18,10},{24,16},{26,18},{28,24},{30,26},{20,28... | collective-permute-start | bytes 786440 | tf_op jit(solution)/shard_map/ppermute | solution.py:195
  90.7 8.6 %collective-permute-start.29 = (bf16[64,2048]{1,0:T(8,128)(2,1)S(1)}, bf16[64,2048]{1,0:T(8,128)(2,1)S(1)}, u32[]{:S(2)}, u32[]{:S(2)}) collective-permute-start(bf16[64,2048]{1,0:T(8,128)(2,1)S(1)} %add_convert_fusion.2), channel_id=1, source_target_pairs={{0,8},{2,10},{8,16},{10,18},{16,24},{18,26},{24,28},{26,30},{28,20... | collective-permute-start | bytes 786440 | tf_op jit(solution)/shard_map/ppermute | solution.py:195
  98.6 6.4 %collective-permute-start.24 = (bf16[64,2048]{1,0:T(8,128)(2,1)S(1)}, bf16[64,2048]{1,0:T(8,128)(2,1)S(1)}, u32[]{:S(2)}, u32[]{:S(2)}) collective-permute-start(bf16[64,2048]{1,0:T(8,128)(2,1)S(1)} %add_convert_fusion.7), channel_id=1, source_target_pairs={{8,0},{10,2},{16,8},{18,10},{24,16},{26,18},{28,24},{30,26},{20,28... | collective-permute-start | bytes 786440 | tf_op jit(solution)/shard_map/ppermute | solution.py:195
  99.4 6.4 %collective-permute-start.30 = (bf16[64,2048]{1,0:T(8,128)(2,1)S(1)}, bf16[64,2048]{1,0:T(8,128)(2,1)S(1)}, u32[]{:S(2)}, u32[]{:S(2)}) collective-permute-start(bf16[64,2048]{1,0:T(8,128)(2,1)S(1)} %add_convert_fusion.1), channel_id=1, source_target_pairs={{0,8},{2,10},{8,16},{10,18},{16,24},{18,26},{24,28},{26,30},{28,20... | collective-permute-start | bytes 786440 | tf_op jit(solution)/shard_map/ppermute | solution.py:195

commit v6 on v5

--- a/solution.py
+++ b/solution.py
@@ -205,7 +205,7 @@
     long = move([bottom, top])
     other, staged = stage(go(cold_weights, across), cold_weights)
     pair = [cold_weights, other]
-    *both, staged, own_tokens = hold(*short, *long, staged, tokens)
+    *both, staged = hold(*short, *long, staged)
     short, long = both[:2], both[2:]
 
     def serve(blocks):
@@ -229,7 +229,7 @@
         return move_on([mine[0] + moving[0], mine[1] + moving[1]])
 
     short = move_on(sums["short", last])
-    *short, first, second = hold(*short, *sums["long", reach])
+    *short, first, second, own_tokens = hold(*short, *sums["long", reach], tokens)
     long = move_on([first, second])
     for k in range(last, 0, -1):
         if k > 1:

time: 107 us -> 104 us (0.972)
  waiting for transfers between devices: 33.1 us -> 30.7 us
    ppermute x29, waiting for transfers between devices: 33.1 us -> 27.1 us  [go(): return lax.ppermute(block, 'dp', pairs)]
    ppermute x2, waiting for transfers between devices: 0.01 us -> 3.58 us  [shifted(): lax.ppermute(block, axis, [(i, (i + by) % size) for i in range(size)])]
  transfers between devices with their start and end apart: 31 -> 31, of which waited for: 10 -> 13; matrix products, arithmetic and copies ran while one was open for 1% -> 1% of each run, Pallas kernels for 28% -> 29%
where the time goes in v6:
time: 104 us
  starting transfers between devices  34.8 us (33%)
  waiting for transfers between devices  30.7 us (30%)
  Pallas kernels  29.8 us (29%)
  local copies, waits for them, and re-layouts  6.12 us (6%)
  other arithmetic  2.27 us (2%)
    ppermute x29, starting transfers between devices, go(): return lax.ppermute(block, 'dp', pairs)  31.7 us
    ppermute x29, waiting for transfers between devices, go(): return lax.ppermute(block, 'dp', pairs)  27.1 us
    pallas_call x5, Pallas kernels, expert_apply(): pl.pallas_call(functools.partial(expert_kernel, len(blocks), experts, fea...  25.8 us
    unnamed x16, local copies, waits for them, and re-layouts  6.12 us
    pallas_call x1, Pallas kernels, stage(): pl.pallas_call(stage_kernel, in_specs=[pl.BlockSpec(memory_space=pl.ANY)]...  3.84 us
    ppermute x2, waiting for transfers between devices, shifted(): lax.ppermute(block, axis, [(i, (i + by) % size) for i in range(size)])  3.58 us
    ppermute x2, starting transfers between devices, shifted(): lax.ppermute(block, axis, [(i, (i + by) % size) for i in range(size)])  3.12 us
  transfers between devices with their start and end apart: 31, of which 13 were waited for; matrix products, arithmetic and copies ran while one was open for 1% of the time, Pallas kernels for 29%

profile of v6, /device:TPU:0, one launch (start us, length us, event | category | flops | bytes accessed | tf_op | source)
XLA Modules:
  0.0 103.9 jit_solution(2092692325458434930)
XLA Ops:
  0.0 0.5 collective-permute-start.4
  0.5 1.0 %copy-done.2 = bf16[128,2048]{1,0:T(8,128)(2,1)S(1)} copy-done((bf16[128,2048]{1,0:T(8,128)(2,1)S(1)}, bf16[128,2048]{1,0:T(8,128)(2,1)}, u32[]{:S(2)}) %copy-start.2) | copy-done | bytes 524312
  1.5 0.7 copy-done.4
  2.2 0.7 copy-done.5
  2.9 0.1 shard_map.55
  3.0 2.6 %collective-permute-start.3 = (bf16[64,2176]{1,0:T(8,128)(2,1)S(1)}, bf16[64,2176]{1,0:T(8,128)(2,1)S(1)}, u32[]{:S(2)}, u32[]{:S(2)}) collective-permute-start(bf16[64,2176]{1,0:T(8,128)(2,1)S(1)} %get-tuple-element.58.refs_3_), channel_id=1, source_target_pairs={{0,8},{2,10},{8,16},{10,18},{16,24},{18,26},{24,28},{26,30},{28,20... | collective-permute-start | bytes 835592 | tf_op jit(solution)/shard_map/ppermute | solution.py:195
  5.6 1.9 %collective-permute-start.2 = (bf16[64,2176]{1,0:T(8,128)(2,1)S(1)}, bf16[64,2176]{1,0:T(8,128)(2,1)S(1)}, u32[]{:S(2)}, u32[]{:S(2)}) collective-permute-start(bf16[64,2176]{1,0:T(8,128)(2,1)S(1)} %get-tuple-element.59.refs_4_), channel_id=1, source_target_pairs={{8,0},{10,2},{16,8},{18,10},{24,16},{26,18},{28,24},{30,26},{20,28... | collective-permute-start | bytes 835592 | tf_op jit(solution)/shard_map/ppermute | solution.py:195
  7.6 0.1 collective-permute-start.1
  7.7 0.1 reduce
  7.8 0.1 pad_add_fusion.1.owners_ref
  7.9 0.1 pad_add_fusion.owners_ref
  7.9 7.1 %collective-permute-done.4.source_ref = bf16[1,3,768,2048]{3,2,1,0:T(8,128)(2,1)} collective-permute-done((bf16[1,3,768,2048]{3,2,1,0:T(8,128)(2,1)}, bf16[1,3,768,2048]{3,2,1,0:T(8,128)(2,1)}, u32[]{:S(2)}, u32[]{:S(2)}) %collective-permute-start.4) | collective-permute-done | bytes 9437216 | tf_op jit(solution)/shard_map/ppermute | solution.py:195
  15.1 3.7 %copy-done = bf16[1,3,768,2048]{3,2,1,0:T(8,128)(2,1)S(1)} copy-done((bf16[1,3,768,2048]{3,2,1,0:T(8,128)(2,1)S(1)}, bf16[1,3,768,2048]{3,2,1,0:T(8,128)(2,1)}, u32[]{:S(2)}) %copy-start) | copy-done | bytes 9437208
  18.8 3.8 %shard_map.56 = (bf16[1,3,768,2048]{3,2,1,0:T(8,128)(2,1)S(1)}, f32[8,128]{1,0:T(8,128)S(1)}) custom-call(bf16[1,3,768,2048]{3,2,1,0:T(8,128)(2,1)} %collective-permute-done.4.source_ref, bf16[1,3,768,2048]{3,2,1,0:T(8,128)(2,1)S(1)} %copy-done), custom_call_target="tpu_custom_call" | custom-call | tf_op jit(solution)/shard_map/pallas_call | solution.py:132
  22.7 2.9 %collective-permute-start.5 = (bf16[64,2176]{1,0:T(8,128)(2,1)S(1)}, bf16[64,2176]{1,0:T(8,128)(2,1)S(1)}, u32[]{:S(2)}, u32[]{:S(2)}) collective-permute-start(bf16[64,2176]{1,0:T(8,128)(2,1)S(1)} %collective-permute-done.2.refs_3_), channel_id=1, source_target_pairs={{8,0},{10,2},{16,8},{18,10},{24,16},{26,18},{28,24},{30,26},{20,28... | collective-permute-start | bytes 835592 | tf_op jit(solution)/shard_map/ppermute | solution.py:195
  25.6 0.2 collective-permute-start.6
  25.7 1.9 %collective-permute-start.9 = (bf16[64,2176]{1,0:T(8,128)(2,1)S(1)}, bf16[64,2176]{1,0:T(8,128)(2,1)S(1)}, u32[]{:S(2)}, u32[]{:S(2)}) collective-permute-start(bf16[64,2176]{1,0:T(8,128)(2,1)S(1)} %collective-permute-done.refs_1_), channel_id=1, source_target_pairs={{8,0},{10,2},{16,8},{18,10},{24,16},{26,18},{28,24},{30,26},{20,28... | collective-permute-start | bytes 835592 | tf_op jit(solution)/shard_map/ppermute | solution.py:195
  27.6 0.2 collective-permute-start.10
  27.7 5.8 %shard_map.57 = (f32[64,2048]{1,0:T(8,128)S(1)}, f32[64,2048]{1,0:T(8,128)S(1)}, f32[64,2048]{1,0:T(8,128)S(1)}, f32[64,2048]{1,0:T(8,128)S(1)}) custom-call(s32[3]{0:T(128)S(1)} %pad_add_fusion.owners_ref, f32[8,128]{1,0:T(8,128)S(1)} %get-tuple-element.61.refs_0_, bf16[64,2176]{1,0:T(8,128)(2,1)S(1)} %collective-permute-done.refs_1_, ...), custom_call_target="tpu_custom_call" | custom-call | flops 4831838208 | bytes 23068672 | tf_op jit(solution)/shard_map/pallas_call | solution.py:101
  33.6 1.5 %collective-permute-done.6.refs_4_ = bf16[64,2176]{1,0:T(8,128)(2,1)S(1)} collective-permute-done((bf16[64,2176]{1,0:T(8,128)(2,1)S(1)}, bf16[64,2176]{1,0:T(8,128)(2,1)S(1)}, u32[]{:S(2)}, u32[]{:S(2)}) %collective-permute-start.6) | collective-permute-done | bytes 278560 | tf_op jit(solution)/shard_map/ppermute | solution.py:195
  35.1 1.6 %collective-permute-start.7 = (bf16[64,2176]{1,0:T(8,128)(2,1)S(1)}, bf16[64,2176]{1,0:T(8,128)(2,1)S(1)}, u32[]{:S(2)}, u32[]{:S(2)}) collective-permute-start(bf16[64,2176]{1,0:T(8,128)(2,1)S(1)} %collective-permute-done.5.refs_3_), channel_id=1, source_target_pairs={{8,0},{10,2},{16,8},{18,10},{24,16},{26,18},{28,24},{30,26},{20,28... | collective-permute-start | bytes 835592 | tf_op jit(solution)/shard_map/ppermute | solution.py:195
  36.7 0.4 collective-permute-start.8
  37.1 1.9 %collective-permute-done.9.refs_1_ = bf16[64,2176]{1,0:T(8,128)(2,1)S(1)} collective-permute-done((bf16[64,2176]{1,0:T(8,128)(2,1)S(1)}, bf16[64,2176]{1,0:T(8,128)(2,1)S(1)}, u32[]{:S(2)}, u32[]{:S(2)}) %collective-permute-start.9) | collective-permute-done | bytes 278560 | tf_op jit(solution)/shard_map/ppermute | solution.py:195
  39.1 2.0 %collective-permute-start.13 = (bf16[64,2176]{1,0:T(8,128)(2,1)S(1)}, bf16[64,2176]{1,0:T(8,128)(2,1)S(1)}, u32[]{:S(2)}, u32[]{:S(2)}) collective-permute-start(bf16[64,2176]{1,0:T(8,128)(2,1)S(1)} %collective-permute-done.9.refs_1_), channel_id=1, source_target_pairs={{8,0},{10,2},{16,8},{18,10},{24,16},{26,18},{28,24},{30,26},{20,28... | collective-permute-start | bytes 835592 | tf_op jit(solution)/shard_map/ppermute | solution.py:195
  41.1 0.1 collective-permute-start.14
  41.2 5.8 %shard_map.58 = (f32[64,2048]{1,0:T(8,128)S(1)}, f32[64,2048]{1,0:T(8,128)S(1)}, f32[64,2048]{1,0:T(8,128)S(1)}, f32[64,2048]{1,0:T(8,128)S(1)}) custom-call(s32[3]{0:T(128)S(1)} %pad_add_fusion.owners_ref, f32[8,128]{1,0:T(8,128)S(1)} %get-tuple-element.61.refs_0_, bf16[64,2176]{1,0:T(8,128)(2,1)S(1)} %collective-permute-done.9.refs_1_, ...), custom_call_target="tpu_custom_call" | custom-call | flops 4831838208 | bytes 23068672 | tf_op jit(solution)/shard_map/pallas_call | solution.py:101
  47.1 2.0 %collective-permute-start.11 = (bf16[64,2176]{1,0:T(8,128)(2,1)S(1)}, bf16[64,2176]{1,0:T(8,128)(2,1)S(1)}, u32[]{:S(2)}, u32[]{:S(2)}) collective-permute-start(bf16[64,2176]{1,0:T(8,128)(2,1)S(1)} %collective-permute-done.7.refs_3_), channel_id=1, source_target_pairs={{8,0},{10,2},{16,8},{18,10},{24,16},{26,18},{28,24},{30,26},{20,28... | collective-permute-start | bytes 835592 | tf_op jit(solution)/shard_map/ppermute | solution.py:195
  49.0 0.3 collective-permute-start.12
  49.4 1.6 %collective-permute-done.13.refs_1_ = bf16[64,2176]{1,0:T(8,128)(2,1)S(1)} collective-permute-done((bf16[64,2176]{1,0:T(8,128)(2,1)S(1)}, bf16[64,2176]{1,0:T(8,128)(2,1)S(1)}, u32[]{:S(2)}, u32[]{:S(2)}) %collective-permute-start.13) | collective-permute-done | bytes 278560 | tf_op jit(solution)/shard_map/ppermute | solution.py:195
  51.0 2.0 %collective-permute-done.14.refs_2_ = bf16[64,2176]{1,0:T(8,128)(2,1)S(1)} collective-permute-done((bf16[64,2176]{1,0:T(8,128)(2,1)S(1)}, bf16[64,2176]{1,0:T(8,128)(2,1)S(1)}, u32[]{:S(2)}, u32[]{:S(2)}) %collective-permute-start.14) | collective-permute-done | bytes 278560 | tf_op jit(solution)/shard_map/ppermute | solution.py:195
  53.0 5.8 %shard_map.59 = (f32[64,2048]{1,0:T(8,128)S(1)}, f32[64,2048]{1,0:T(8,128)S(1)}, f32[64,2048]{1,0:T(8,128)S(1)}, f32[64,2048]{1,0:T(8,128)S(1)}) custom-call(s32[3]{0:T(128)S(1)} %pad_add_fusion.owners_ref, f32[8,128]{1,0:T(8,128)S(1)} %get-tuple-element.61.refs_0_, bf16[64,2176]{1,0:T(8,128)(2,1)S(1)} %collective-permute-done.13.refs_1_, ...), custom_call_target="tpu_custom_call" | custom-call | flops 4831838208 | bytes 23068672 | tf_op jit(solution)/shard_map/pallas_call | solution.py:101
  59.0 1.6 %collective-permute-start.16 = (bf16[64,2048]{1,0:T(8,128)(2,1)S(1)}, bf16[64,2048]{1,0:T(8,128)(2,1)S(1)}, u32[]{:S(2)}, u32[]{:S(2)}) collective-permute-start(bf16[64,2048]{1,0:T(8,128)(2,1)S(1)} %convert_element_type.89), channel_id=1, source_target_pairs={{8,0},{10,2},{16,8},{18,10},{24,16},{26,18},{28,24},{30,26},{20,28... | collective-permute-start | bytes 786440 | tf_op jit(solution)/shard_map/ppermute | solution.py:195
  60.6 0.5 collective-permute-start.15
  61.1 5.8 %shard_map.60 = (f32[64,2048]{1,0:T(8,128)S(1)}, f32[64,2048]{1,0:T(8,128)S(1)}, f32[64,2048]{1,0:T(8,128)S(1)}, f32[64,2048]{1,0:T(8,128)S(1)}) custom-call(s32[3]{0:T(128)S(1)} %pad_add_fusion.owners_ref, f32[8,128]{1,0:T(8,128)S(1)} %get-tuple-element.61.refs_0_, bf16[64,2176]{1,0:T(8,128)(2,1)S(1)} %collective-permute-done.11.refs_1_, ...), custom_call_target="tpu_custom_call" | custom-call | flops 4831838208 | bytes 23068672 | tf_op jit(solution)/shard_map/pallas_call | solution.py:101
  67.1 0.5 collective-permute-start.27
  67.6 1.6 %collective-permute-start.21 = (bf16[64,2048]{1,0:T(8,128)(2,1)S(1)}, bf16[64,2048]{1,0:T(8,128)(2,1)S(1)}, u32[]{:S(2)}, u32[]{:S(2)}) collective-permute-start(bf16[64,2048]{1,0:T(8,128)(2,1)S(1)} %convert_element_type.96), channel_id=1, source_target_pairs={{8,0},{10,2},{16,8},{18,10},{24,16},{26,18},{28,24},{30,26},{20,28... | collective-permute-start | bytes 786440 | tf_op jit(solution)/shard_map/ppermute | solution.py:195
  69.1 0.1 add_convert_fusion.11
  69.2 0.5 collective-permute-start.19
  69.8 1.6 %collective-permute-start.25 = (bf16[64,2048]{1,0:T(8,128)(2,1)S(1)}, bf16[64,2048]{1,0:T(8,128)(2,1)S(1)}, u32[]{:S(2)}, u32[]{:S(2)}) collective-permute-start(bf16[64,2048]{1,0:T(8,128)(2,1)S(1)} %add_convert_fusion.5), channel_id=1, source_target_pairs={{8,0},{10,2},{16,8},{18,10},{24,16},{26,18},{28,24},{30,26},{20,28... | collective-permute-start | bytes 786440 | tf_op jit(solution)/shard_map/ppermute | solution.py:195
  71.4 1.5 %collective-permute-start.17 = (bf16[128,2048]{1,0:T(8,128)(2,1)S(1)}, bf16[128,2048]{1,0:T(8,128)(2,1)S(1)}, u32[]{:S(2)}, u32[]{:S(2)}) collective-permute-start(bf16[128,2048]{1,0:T(8,128)(2,1)S(1)} %copy-done.3), channel_id=1, source_target_pairs={{0,1},{1,0},{2,3},{3,2},{4,5},{5,4},{6,7},{7,6},{8,9},{9,8},{10,11... | collective-permute-start | bytes 1572872 | tf_op jit(solution)/shard_map/ppermute | solution.py:17
  72.9 3.4 %collective-permute-done.27 = bf16[64,2048]{1,0:T(8,128)(2,1)S(1)} collective-permute-done((bf16[64,2048]{1,0:T(8,128)(2,1)S(1)}, bf16[64,2048]{1,0:T(8,128)(2,1)S(1)}, u32[]{:S(2)}, u32[]{:S(2)}) %collective-permute-start.27) | collective-permute-done | bytes 262176 | tf_op jit(solution)/shard_map/ppermute | solution.py:195
  76.4 0.5 collective-permute-start.28
  77.0 1.6 %collective-permute-start.22 = (bf16[64,2048]{1,0:T(8,128)(2,1)S(1)}, bf16[64,2048]{1,0:T(8,128)(2,1)S(1)}, u32[]{:S(2)}, u32[]{:S(2)}) collective-permute-start(bf16[64,2048]{1,0:T(8,128)(2,1)S(1)} %add_convert_fusion.9), channel_id=1, source_target_pairs={{8,0},{10,2},{16,8},{18,10},{24,16},{26,18},{28,24},{30,26},{20,28... | collective-permute-start | bytes 786440 | tf_op jit(solution)/shard_map/ppermute | solution.py:195
  78.6 3.4 %collective-permute-done.19 = bf16[64,2048]{1,0:T(8,128)(2,1)S(1)} collective-permute-done((bf16[64,2048]{1,0:T(8,128)(2,1)S(1)}, bf16[64,2048]{1,0:T(8,128)(2,1)S(1)}, u32[]{:S(2)}, u32[]{:S(2)}) %collective-permute-start.19) | collective-permute-done | bytes 262176 | tf_op jit(solution)/shard_map/ppermute | solution.py:195
  82.0 0.1 add_convert_fusion.10
  82.0 0.5 collective-permute-start.20
  82.6 0.1 add_convert_fusion.4
  82.6 1.6 %collective-permute-start.26 = (bf16[64,2048]{1,0:T(8,128)(2,1)S(1)}, bf16[64,2048]{1,0:T(8,128)(2,1)S(1)}, u32[]{:S(2)}, u32[]{:S(2)}) collective-permute-start(bf16[64,2048]{1,0:T(8,128)(2,1)S(1)} %add_convert_fusion.4), channel_id=1, source_target_pairs={{8,0},{10,2},{16,8},{18,10},{24,16},{26,18},{28,24},{30,26},{20,28... | collective-permute-start | bytes 786440 | tf_op jit(solution)/shard_map/ppermute | solution.py:195
  84.2 3.4 %collective-permute-done.28 = bf16[64,2048]{1,0:T(8,128)(2,1)S(1)} collective-permute-done((bf16[64,2048]{1,0:T(8,128)(2,1)S(1)}, bf16[64,2048]{1,0:T(8,128)(2,1)S(1)}, u32[]{:S(2)}, u32[]{:S(2)}) %collective-permute-start.28) | collective-permute-done | bytes 262176 | tf_op jit(solution)/shard_map/ppermute | solution.py:195
  87.6 0.5 collective-permute-start.29
  88.2 1.8 %collective-permute-start.23 = (bf16[64,2048]{1,0:T(8,128)(2,1)S(1)}, bf16[64,2048]{1,0:T(8,128)(2,1)S(1)}, u32[]{:S(2)}, u32[]{:S(2)}) collective-permute-start(bf16[64,2048]{1,0:T(8,128)(2,1)S(1)} %add_convert_fusion.8), channel_id=1, source_target_pairs={{8,0},{10,2},{16,8},{18,10},{24,16},{26,18},{28,24},{30,26},{20,28... | collective-permute-start | bytes 786440 | tf_op jit(solution)/shard_map/ppermute | solution.py:195
  90.1 2.4 %shard_map.61 = (f32[128,2048]{1,0:T(8,128)S(1)}, bf16[128,2048]{1,0:T(8,128)(2,1)S(1)}) custom-call(s32[2]{0:T(128)S(1)} %pad_add_fusion.1.owners_ref, bf16[128,2048]{1,0:T(8,128)(2,1)S(1)} %copy-done.3, bf16[128,2048]{1,0:T(8,128)(2,1)S(1)} %collective-permute-done.17.refs_1_, bf16[1,3,384,2048]{3,2,1,0:T(8,128)(2,1)S(1)} %bitcast.5), custom_call_target="tpu_custom_call" | custom-call | flops 1207959552 | bytes 8912896 | tf_op jit(solution)/shard_map/pallas_call | solution.py:101
  92.5 1.6 %collective-permute-start.18 = (bf16[128,2048]{1,0:T(8,128)(2,1)S(1)}, bf16[128,2048]{1,0:T(8,128)(2,1)S(1)}, u32[]{:S(2)}, u32[]{:S(2)}) collective-permute-start(bf16[128,2048]{1,0:T(8,128)(2,1)S(1)} %get-tuple-element.93), channel_id=1, source_target_pairs={{0,1},{1,0},{2,3},{3,2},{4,5},{5,4},{6,7},{7,6},{8,9},{9,8},{10,11... | collective-permute-start | bytes 1572872 | tf_op jit(solution)/shard_map/ppermute | solution.py:17
  94.1 1.8 %collective-permute-done.29 = bf16[64,2048]{1,0:T(8,128)(2,1)S(1)} collective-permute-done((bf16[64,2048]{1,0:T(8,128)(2,1)S(1)}, bf16[64,2048]{1,0:T(8,128)(2,1)S(1)}, u32[]{:S(2)}, u32[]{:S(2)}) %collective-permute-start.29) | collective-permute-done | bytes 262176 | tf_op jit(solution)/shard_map/ppermute | solution.py:195
  96.0 0.5 collective-permute-start.30
  96.6 1.6 %collective-permute-start.24 = (bf16[64,2048]{1,0:T(8,128)(2,1)S(1)}, bf16[64,2048]{1,0:T(8,128)(2,1)S(1)}, u32[]{:S(2)}, u32[]{:S(2)}) collective-permute-start(bf16[64,2048]{1,0:T(8,128)(2,1)S(1)} %add_convert_fusion.7), channel_id=1, source_target_pairs={{8,0},{10,2},{16,8},{18,10},{24,16},{26,18},{28,24},{30,26},{20,28... | collective-permute-start | bytes 786440 | tf_op jit(solution)/shard_map/ppermute | solution.py:195
  98.2 3.6 %collective-permute-done.18 = bf16[128,2048]{1,0:T(8,128)(2,1)S(1)} collective-permute-done((bf16[128,2048]{1,0:T(8,128)(2,1)S(1)}, bf16[128,2048]{1,0:T(8,128)(2,1)S(1)}, u32[]{:S(2)}, u32[]{:S(2)}) %collective-permute-start.18) | collective-permute-done | bytes 524320 | tf_op jit(solution)/shard_map/ppermute | solution.py:17
  101.8 0.2 add_multiply_fusion
  102.0 0.1 slice_add_fusion
  102.1 0.3 collective-permute-done.30
  102.4 0.1 add_convert_fusion
  102.5 0.4 collective-permute-done.24
  103.0 0.1 add_convert_fusion.6
  103.1 0.8 pad_maximum_fusion
  (44 shorter events, 0.6 us)
Async XLA Ops:
  0.0 15.1 %collective-permute-start.4 = (bf16[1,3,768,2048]{3,2,1,0:T(8,128)(2,1)}, bf16[1,3,768,2048]{3,2,1,0:T(8,128)(2,1)}, u32[]{:S(2)}, u32[]{:S(2)}) collective-permute-start(bf16[1,3,768,2048]{3,2,1,0:T(8,128)(2,1)} %refs_5_.7), channel_id=1, source_target_pairs={{0,2},{2,0},{4,6},{6,4},{8,10},{10,8},{12,14},{14,12},{16,18},{18,... | collective-permute-start | bytes 28311560 | tf_op jit(solution)/shard_map/ppermute | solution.py:195
  0.5 1.0 %copy-start.2 = (bf16[128,2048]{1,0:T(8,128)(2,1)S(1)}, bf16[128,2048]{1,0:T(8,128)(2,1)}, u32[]{:S(2)}) copy-start(bf16[128,2048]{1,0:T(8,128)(2,1)} %refs_0_) | copy-start | bytes 1572868
  1.5 0.7 copy-start.4
  2.2 0.7 copy-start.5
  3.0 19.6 %collective-permute-start.3 = (bf16[64,2176]{1,0:T(8,128)(2,1)S(1)}, bf16[64,2176]{1,0:T(8,128)(2,1)S(1)}, u32[]{:S(2)}, u32[]{:S(2)}) collective-permute-start(bf16[64,2176]{1,0:T(8,128)(2,1)S(1)} %get-tuple-element.58.refs_3_), channel_id=1, source_target_pairs={{0,8},{2,10},{8,16},{10,18},{16,24},{18,26},{24,28},{26,30},{28,20... | collective-permute-start | bytes 835592 | tf_op jit(solution)/shard_map/ppermute | solution.py:195
  5.6 17.0 %collective-permute-start = (bf16[64,2176]{1,0:T(8,128)(2,1)S(1)}, bf16[64,2176]{1,0:T(8,128)(2,1)S(1)}, u32[]{:S(2)}, u32[]{:S(2)}) collective-permute-start(bf16[64,2176]{1,0:T(8,128)(2,1)S(1)} %get-tuple-element.58.refs_3_), channel_id=1, source_target_pairs={{8,0},{10,2},{16,8},{18,10},{24,16},{26,18},{28,24},{30,26},{20,28... | collective-permute-start | bytes 835592 | tf_op jit(solution)/shard_map/ppermute | solution.py:195
  5.6 17.0 %collective-permute-start.2 = (bf16[64,2176]{1,0:T(8,128)(2,1)S(1)}, bf16[64,2176]{1,0:T(8,128)(2,1)S(1)}, u32[]{:S(2)}, u32[]{:S(2)}) collective-permute-start(bf16[64,2176]{1,0:T(8,128)(2,1)S(1)} %get-tuple-element.59.refs_4_), channel_id=1, source_target_pairs={{8,0},{10,2},{16,8},{18,10},{24,16},{26,18},{28,24},{30,26},{20,28... | collective-permute-start | bytes 835592 | tf_op jit(solution)/shard_map/ppermute | solution.py:195
  7.6 15.1 %collective-permute-start.1 = (bf16[64,2176]{1,0:T(8,128)(2,1)S(1)}, bf16[64,2176]{1,0:T(8,128)(2,1)S(1)}, u32[]{:S(2)}, u32[]{:S(2)}) collective-permute-start(bf16[64,2176]{1,0:T(8,128)(2,1)S(1)} %get-tuple-element.59.refs_4_), channel_id=1, source_target_pairs={{0,8},{2,10},{8,16},{10,18},{16,24},{18,26},{24,28},{26,30},{28,20... | collective-permute-start | bytes 835592 | tf_op jit(solution)/shard_map/ppermute | solution.py:195
  15.1 3.7 %copy-start = (bf16[1,3,768,2048]{3,2,1,0:T(8,128)(2,1)S(1)}, bf16[1,3,768,2048]{3,2,1,0:T(8,128)(2,1)}, u32[]{:S(2)}) copy-start(bf16[1,3,768,2048]{3,2,1,0:T(8,128)(2,1)} %refs_5_.7) | copy-start | bytes 28311556
  18.8 9.0 %copy-start.1 = (bf16[1,3,768,2048]{3,2,1,0:T(8,128)(2,1)S(1)}, bf16[1,3,768,2048]{3,2,1,0:T(8,128)(2,1)}, u32[]{:S(2)}) copy-start(bf16[1,3,768,2048]{3,2,1,0:T(8,128)(2,1)} %refs_5_.7) | copy-start | bytes 28311556
  22.7 10.9 %collective-permute-start.5 = (bf16[64,2176]{1,0:T(8,128)(2,1)S(1)}, bf16[64,2176]{1,0:T(8,128)(2,1)S(1)}, u32[]{:S(2)}, u32[]{:S(2)}) collective-permute-start(bf16[64,2176]{1,0:T(8,128)(2,1)S(1)} %collective-permute-done.2.refs_3_), channel_id=1, source_target_pairs={{8,0},{10,2},{16,8},{18,10},{24,16},{26,18},{28,24},{30,26},{20,28... | collective-permute-start | bytes 835592 | tf_op jit(solution)/shard_map/ppermute | solution.py:195
  25.6 9.5 %collective-permute-start.6 = (bf16[64,2176]{1,0:T(8,128)(2,1)S(1)}, bf16[64,2176]{1,0:T(8,128)(2,1)S(1)}, u32[]{:S(2)}, u32[]{:S(2)}) collective-permute-start(bf16[64,2176]{1,0:T(8,128)(2,1)S(1)} %collective-permute-done.3.refs_4_), channel_id=1, source_target_pairs={{0,8},{2,10},{8,16},{10,18},{16,24},{18,26},{24,28},{26,30},{28,20... | collective-permute-start | bytes 835592 | tf_op jit(solution)/shard_map/ppermute | solution.py:195
  25.7 13.3 %collective-permute-start.9 = (bf16[64,2176]{1,0:T(8,128)(2,1)S(1)}, bf16[64,2176]{1,0:T(8,128)(2,1)S(1)}, u32[]{:S(2)}, u32[]{:S(2)}) collective-permute-start(bf16[64,2176]{1,0:T(8,128)(2,1)S(1)} %collective-permute-done.refs_1_), channel_id=1, source_target_pairs={{8,0},{10,2},{16,8},{18,10},{24,16},{26,18},{28,24},{30,26},{20,28... | collective-permute-start | bytes 835592 | tf_op jit(solution)/shard_map/ppermute | solution.py:195
  27.6 13.5 %collective-permute-start.10 = (bf16[64,2176]{1,0:T(8,128)(2,1)S(1)}, bf16[64,2176]{1,0:T(8,128)(2,1)S(1)}, u32[]{:S(2)}, u32[]{:S(2)}) collective-permute-start(bf16[64,2176]{1,0:T(8,128)(2,1)S(1)} %collective-permute-done.1.refs_2_), channel_id=1, source_target_pairs={{0,8},{2,10},{8,16},{10,18},{16,24},{18,26},{24,28},{26,30},{28,20... | collective-permute-start | bytes 835592 | tf_op jit(solution)/shard_map/ppermute | solution.py:195
  35.1 11.9 %collective-permute-start.7 = (bf16[64,2176]{1,0:T(8,128)(2,1)S(1)}, bf16[64,2176]{1,0:T(8,128)(2,1)S(1)}, u32[]{:S(2)}, u32[]{:S(2)}) collective-permute-start(bf16[64,2176]{1,0:T(8,128)(2,1)S(1)} %collective-permute-done.5.refs_3_), channel_id=1, source_target_pairs={{8,0},{10,2},{16,8},{18,10},{24,16},{26,18},{28,24},{30,26},{20,28... | collective-permute-start | bytes 835592 | tf_op jit(solution)/shard_map/ppermute | solution.py:195
  36.7 10.4 %collective-permute-start.8 = (bf16[64,2176]{1,0:T(8,128)(2,1)S(1)}, bf16[64,2176]{1,0:T(8,128)(2,1)S(1)}, u32[]{:S(2)}, u32[]{:S(2)}) collective-permute-start(bf16[64,2176]{1,0:T(8,128)(2,1)S(1)} %collective-permute-done.6.refs_4_), channel_id=1, source_target_pairs={{0,8},{2,10},{8,16},{10,18},{16,24},{18,26},{24,28},{26,30},{28,20... | collective-permute-start | bytes 835592 | tf_op jit(solution)/shard_map/ppermute | solution.py:195
  39.1 11.9 %collective-permute-start.13 = (bf16[64,2176]{1,0:T(8,128)(2,1)S(1)}, bf16[64,2176]{1,0:T(8,128)(2,1)S(1)}, u32[]{:S(2)}, u32[]{:S(2)}) collective-permute-start(bf16[64,2176]{1,0:T(8,128)(2,1)S(1)} %collective-permute-done.9.refs_1_), channel_id=1, source_target_pairs={{8,0},{10,2},{16,8},{18,10},{24,16},{26,18},{28,24},{30,26},{20,28... | collective-permute-start | bytes 835592 | tf_op jit(solution)/shard_map/ppermute | solution.py:195
  41.1 11.9 %collective-permute-start.14 = (bf16[64,2176]{1,0:T(8,128)(2,1)S(1)}, bf16[64,2176]{1,0:T(8,128)(2,1)S(1)}, u32[]{:S(2)}, u32[]{:S(2)}) collective-permute-start(bf16[64,2176]{1,0:T(8,128)(2,1)S(1)} %collective-permute-done.10.refs_2_), channel_id=1, source_target_pairs={{0,8},{2,10},{8,16},{10,18},{16,24},{18,26},{24,28},{26,30},{28,20... | collective-permute-start | bytes 835592 | tf_op jit(solution)/shard_map/ppermute | solution.py:195
  47.1 11.8 %collective-permute-start.11 = (bf16[64,2176]{1,0:T(8,128)(2,1)S(1)}, bf16[64,2176]{1,0:T(8,128)(2,1)S(1)}, u32[]{:S(2)}, u32[]{:S(2)}) collective-permute-start(bf16[64,2176]{1,0:T(8,128)(2,1)S(1)} %collective-permute-done.7.refs_3_), channel_id=1, source_target_pairs={{8,0},{10,2},{16,8},{18,10},{24,16},{26,18},{28,24},{30,26},{20,28... | collective-permute-start | bytes 835592 | tf_op jit(solution)/shard_map/ppermute | solution.py:195
  49.0 9.9 %collective-permute-start.12 = (bf16[64,2176]{1,0:T(8,128)(2,1)S(1)}, bf16[64,2176]{1,0:T(8,128)(2,1)S(1)}, u32[]{:S(2)}, u32[]{:S(2)}) collective-permute-start(bf16[64,2176]{1,0:T(8,128)(2,1)S(1)} %collective-permute-done.8.refs_4_), channel_id=1, source_target_pairs={{0,8},{2,10},{8,16},{10,18},{16,24},{18,26},{24,28},{26,30},{28,20... | collective-permute-start | bytes 835592 | tf_op jit(solution)/shard_map/ppermute | solution.py:195
  58.9 31.1 %slice-start = ((s8[4718592]{0:T(1024)(128)(4,1)}), s8[4194304]{0:T(1024)(128)(4,1)S(1)}, s32[]{:S(2)}) async-start(s8[4718592]{0:T(1024)(128)(4,1)} %bitcast.4), calls=%async_computation | async-start | bytes 8388608
  59.0 12.4 %copy-start.3 = (bf16[128,2048]{1,0:T(8,128)(2,1)S(1)}, bf16[128,2048]{1,0:T(8,128)(2,1)}, u32[]{:S(2)}) copy-start(bf16[128,2048]{1,0:T(8,128)(2,1)} %refs_0_) | copy-start | bytes 1572868
  59.0 31.1 %slice-start.1 = ((s8[4718592]{0:T(1024)(128)(4,1)}), s8[524288]{0:T(1024)(128)(4,1)S(1)}, s32[]{:S(2)}) async-start(s8[4718592]{0:T(1024)(128)(4,1)} %bitcast.4), calls=%async_computation.1 | async-start | bytes 1048576
  59.0 7.9 %collective-permute-start.16 = (bf16[64,2048]{1,0:T(8,128)(2,1)S(1)}, bf16[64,2048]{1,0:T(8,128)(2,1)S(1)}, u32[]{:S(2)}, u32[]{:S(2)}) collective-permute-start(bf16[64,2048]{1,0:T(8,128)(2,1)S(1)} %convert_element_type.89), channel_id=1, source_target_pairs={{8,0},{10,2},{16,8},{18,10},{24,16},{26,18},{28,24},{30,26},{20,28... | collective-permute-start | bytes 786440 | tf_op jit(solution)/shard_map/ppermute | solution.py:195
  60.6 6.4 %collective-permute-start.15 = (bf16[64,2048]{1,0:T(8,128)(2,1)S(1)}, bf16[64,2048]{1,0:T(8,128)(2,1)S(1)}, u32[]{:S(2)}, u32[]{:S(2)}) collective-permute-start(bf16[64,2048]{1,0:T(8,128)(2,1)S(1)} %convert_element_type.88), channel_id=1, source_target_pairs={{0,8},{2,10},{8,16},{10,18},{16,24},{18,26},{24,28},{26,30},{28,20... | collective-permute-start | bytes 786440 | tf_op jit(solution)/shard_map/ppermute | solution.py:195
  67.1 9.3 %collective-permute-start.27 = (bf16[64,2048]{1,0:T(8,128)(2,1)S(1)}, bf16[64,2048]{1,0:T(8,128)(2,1)S(1)}, u32[]{:S(2)}, u32[]{:S(2)}) collective-permute-start(bf16[64,2048]{1,0:T(8,128)(2,1)S(1)} %convert_element_type.109), channel_id=1, source_target_pairs={{0,8},{2,10},{8,16},{10,18},{16,24},{18,26},{24,28},{26,30},{28,20... | collective-permute-start | bytes 786440 | tf_op jit(solution)/shard_map/ppermute | solution.py:195
  67.6 9.3 %collective-permute-start.21 = (bf16[64,2048]{1,0:T(8,128)(2,1)S(1)}, bf16[64,2048]{1,0:T(8,128)(2,1)S(1)}, u32[]{:S(2)}, u32[]{:S(2)}) collective-permute-start(bf16[64,2048]{1,0:T(8,128)(2,1)S(1)} %convert_element_type.96), channel_id=1, source_target_pairs={{8,0},{10,2},{16,8},{18,10},{24,16},{26,18},{28,24},{30,26},{20,28... | collective-permute-start | bytes 786440 | tf_op jit(solution)/shard_map/ppermute | solution.py:195
  69.2 12.8 %collective-permute-start.19 = (bf16[64,2048]{1,0:T(8,128)(2,1)S(1)}, bf16[64,2048]{1,0:T(8,128)(2,1)S(1)}, u32[]{:S(2)}, u32[]{:S(2)}) collective-permute-start(bf16[64,2048]{1,0:T(8,128)(2,1)S(1)} %add_convert_fusion.11), channel_id=1, source_target_pairs={{0,8},{2,10},{8,16},{10,18},{16,24},{18,26},{24,28},{26,30},{28,20... | collective-permute-start | bytes 786440 | tf_op jit(solution)/shard_map/ppermute | solution.py:195
  69.8 12.8 %collective-permute-start.25 = (bf16[64,2048]{1,0:T(8,128)(2,1)S(1)}, bf16[64,2048]{1,0:T(8,128)(2,1)S(1)}, u32[]{:S(2)}, u32[]{:S(2)}) collective-permute-start(bf16[64,2048]{1,0:T(8,128)(2,1)S(1)} %add_convert_fusion.5), channel_id=1, source_target_pairs={{8,0},{10,2},{16,8},{18,10},{24,16},{26,18},{28,24},{30,26},{20,28... | collective-permute-start | bytes 786440 | tf_op jit(solution)/shard_map/ppermute | solution.py:195
  71.4 18.7 %collective-permute-start.17 = (bf16[128,2048]{1,0:T(8,128)(2,1)S(1)}, bf16[128,2048]{1,0:T(8,128)(2,1)S(1)}, u32[]{:S(2)}, u32[]{:S(2)}) collective-permute-start(bf16[128,2048]{1,0:T(8,128)(2,1)S(1)} %copy-done.3), channel_id=1, source_target_pairs={{0,1},{1,0},{2,3},{3,2},{4,5},{5,4},{6,7},{7,6},{8,9},{9,8},{10,11... | collective-permute-start | bytes 1572872 | tf_op jit(solution)/shard_map/ppermute | solution.py:17
  76.4 11.2 %collective-permute-start.28 = (bf16[64,2048]{1,0:T(8,128)(2,1)S(1)}, bf16[64,2048]{1,0:T(8,128)(2,1)S(1)}, u32[]{:S(2)}, u32[]{:S(2)}) collective-permute-start(bf16[64,2048]{1,0:T(8,128)(2,1)S(1)} %add_convert_fusion.3), channel_id=1, source_target_pairs={{0,8},{2,10},{8,16},{10,18},{16,24},{18,26},{24,28},{26,30},{28,20... | collective-permute-start | bytes 786440 | tf_op jit(solution)/shard_map/ppermute | solution.py:195
  77.0 11.2 %collective-permute-start.22 = (bf16[64,2048]{1,0:T(8,128)(2,1)S(1)}, bf16[64,2048]{1,0:T(8,128)(2,1)S(1)}, u32[]{:S(2)}, u32[]{:S(2)}) collective-permute-start(bf16[64,2048]{1,0:T(8,128)(2,1)S(1)} %add_convert_fusion.9), channel_id=1, source_target_pairs={{8,0},{10,2},{16,8},{18,10},{24,16},{26,18},{28,24},{30,26},{20,28... | collective-permute-start | bytes 786440 | tf_op jit(solution)/shard_map/ppermute | solution.py:195
  82.0 20.5 %collective-permute-start.20 = (bf16[64,2048]{1,0:T(8,128)(2,1)S(1)}, bf16[64,2048]{1,0:T(8,128)(2,1)S(1)}, u32[]{:S(2)}, u32[]{:S(2)}) collective-permute-start(bf16[64,2048]{1,0:T(8,128)(2,1)S(1)} %add_convert_fusion.10), channel_id=1, source_target_pairs={{0,8},{2,10},{8,16},{10,18},{16,24},{18,26},{24,28},{26,30},{28,20... | collective-permute-start | bytes 786440 | tf_op jit(solution)/shard_map/ppermute | solution.py:195
  82.6 19.5 %collective-permute-start.26 = (bf16[64,2048]{1,0:T(8,128)(2,1)S(1)}, bf16[64,2048]{1,0:T(8,128)(2,1)S(1)}, u32[]{:S(2)}, u32[]{:S(2)}) collective-permute-start(bf16[64,2048]{1,0:T(8,128)(2,1)S(1)} %add_convert_fusion.4), channel_id=1, source_target_pairs={{8,0},{10,2},{16,8},{18,10},{24,16},{26,18},{28,24},{30,26},{20,28... | collective-permute-start | bytes 786440 | tf_op jit(solution)/shard_map/ppermute | solution.py:195
  87.6 8.3 %collective-permute-start.29 = (bf16[64,2048]{1,0:T(8,128)(2,1)S(1)}, bf16[64,2048]{1,0:T(8,128)(2,1)S(1)}, u32[]{:S(2)}, u32[]{:S(2)}) collective-permute-start(bf16[64,2048]{1,0:T(8,128)(2,1)S(1)} %add_convert_fusion.2), channel_id=1, source_target_pairs={{0,8},{2,10},{8,16},{10,18},{16,24},{18,26},{24,28},{26,30},{28,20... | collective-permute-start | bytes 786440 | tf_op jit(solution)/shard_map/ppermute | solution.py:195
  88.2 8.3 %collective-permute-start.23 = (bf16[64,2048]{1,0:T(8,128)(2,1)S(1)}, bf16[64,2048]{1,0:T(8,128)(2,1)S(1)}, u32[]{:S(2)}, u32[]{:S(2)}) collective-permute-start(bf16[64,2048]{1,0:T(8,128)(2,1)S(1)} %add_convert_fusion.8), channel_id=1, source_target_pairs={{8,0},{10,2},{16,8},{18,10},{24,16},{26,18},{28,24},{30,26},{20,28... | collective-permute-start | bytes 786440 | tf_op jit(solution)/shard_map/ppermute | solution.py:195
  92.5 9.2 %collective-permute-start.18 = (bf16[128,2048]{1,0:T(8,128)(2,1)S(1)}, bf16[128,2048]{1,0:T(8,128)(2,1)S(1)}, u32[]{:S(2)}, u32[]{:S(2)}) collective-permute-start(bf16[128,2048]{1,0:T(8,128)(2,1)S(1)} %get-tuple-element.93), channel_id=1, source_target_pairs={{0,1},{1,0},{2,3},{3,2},{4,5},{5,4},{6,7},{7,6},{8,9},{9,8},{10,11... | collective-permute-start | bytes 1572872 | tf_op jit(solution)/shard_map/ppermute | solution.py:17
  96.0 6.4 %collective-permute-start.30 = (bf16[64,2048]{1,0:T(8,128)(2,1)S(1)}, bf16[64,2048]{1,0:T(8,128)(2,1)S(1)}, u32[]{:S(2)}, u32[]{:S(2)}) collective-permute-start(bf16[64,2048]{1,0:T(8,128)(2,1)S(1)} %add_convert_fusion.1), channel_id=1, source_target_pairs={{0,8},{2,10},{8,16},{10,18},{16,24},{18,26},{24,28},{26,30},{28,20... | collective-permute-start | bytes 786440 | tf_op jit(solution)/shard_map/ppermute | solution.py:195
  96.6 6.4 %collective-permute-start.24 = (bf16[64,2048]{1,0:T(8,128)(2,1)S(1)}, bf16[64,2048]{1,0:T(8,128)(2,1)S(1)}, u32[]{:S(2)}, u32[]{:S(2)}) collective-permute-start(bf16[64,2048]{1,0:T(8,128)(2,1)S(1)} %add_convert_fusion.7), channel_id=1, source_target_pairs={{8,0},{10,2},{16,8},{18,10},{24,16},{26,18},{28,24},{30,26},{20,28... | collective-permute-start | bytes 786440 | tf_op jit(solution)/shard_map/ppermute | solution.py:195
